TPU v7x, 128 devices: a whole 4x4x4 slice. The times are simulated.
128 devices in a mesh: dp: 4 (over z_hi, core), context: 8 (over x, z_lo), experts: 4 (over y).
Axes of the slice: x: 4, y: 4, z: 4 (z_hi: 2, z_lo: 2; z = z_hi * 2 + z_lo), core: 2. Of those that a mesh axis runs over, the one named last changes fastest.
Arguments:
- hidden_in: bfloat16 [12, 1024, 2048], P('dp', 'context'), may hold values from -6 to 6
- segments: int32 [12, 1024], P('dp'), may hold values from 0 to 2, as said below
- attn_gain: bfloat16 [2048], replicated, may hold values from 0.5 to 1.5
- query_gain: bfloat16 [128], replicated, may hold values from 0.5 to 1.5
- key_gain: bfloat16 [128], replicated, may hold values from 0.5 to 1.5
- w_query: bfloat16 [2048, 4096], P(None, 'experts'), may hold values from -0.125 to 0.125
- key_weight_matrix: bfloat16 [2048, 512], P(None, 'experts'), may hold values from -0.125 to 0.125
- value_weight_matrix: bfloat16 [2048, 512], P(None, 'experts'), may hold values from -0.125 to 0.125
- w_out: bfloat16 [2048, 4096], P(None, 'experts'), may hold values from -1.5 to 1.5
- moe_gain: bfloat16 [2048], replicated, may hold values from 0.5 to 1.5
- expert_ids: int32 [12, 1024, 8], P('dp', ('context', 'experts')), may hold values from 0 to 15, as said below
- gate_values: float32 [12, 1024, 8], P('dp', ('context', 'experts')), may hold values from 0.06 to 0.2
- capacity: int32 [16], replicated, may hold values from 24 to 48, as said below
- w_gate: bfloat16 [16, 2048, 768], P(('dp', 'experts')), may hold values from -0.125 to 0.125
- w_up: bfloat16 [16, 2048, 768], P(('dp', 'experts')), may hold values from -0.125 to 0.125
- w_down: bfloat16 [16, 2048, 768], P(('dp', 'experts')), may hold values from -0.875 to 0.875
- cotangent: bfloat16 [12, 1024, 2048], P('dp', ('context', 'experts')), may hold values from -6 to 6
Outputs:
- layer_out: float32 [12, 1024, 2048], P('dp', ('context', 'experts'))
- input_grad: float32 [12, 1024, 2048], P('dp', ('context', 'experts'))
- attn_gain_grad: float32 [2048], replicated
- query_gain_grad: float32 [128], replicated
- key_gain_grad: float32 [128], replicated
- w_query_grad: float32 [2048, 4096], P(('dp', 'context'), 'experts')
- w_key_grad: float32 [2048, 512], P(('dp', 'context'), 'experts')
- w_value_grad: float32 [2048, 512], P(('dp', 'context'), 'experts')
- w_out_grad: float32 [2048, 4096], P(('dp', 'context'), 'experts')
- moe_gain_grad: float32 [2048], replicated
- gate_grad: float32 [12, 1024, 8], P('dp', ('context', 'experts'))
- w_gate_grad: float32 [16, 2048, 768], P(('dp', 'experts'), 'context')
- w_up_grad: float32 [16, 2048, 768], P(('dp', 'experts'), 'context')
- w_down_grad: float32 [16, 2048, 768], P(('dp', 'experts'), 'context')
- head_clip_scale: float32 [32], P('experts')
Inputs may be any that keep to these rules, and one draw needn't show every extreme that they name: `segments`: in each sequence the document numbers never fall and take the values 0, 1, 2; document 1 starts within the first 128 positions and ends within the last 128 positions. `expert_ids`: each token names 8 different experts in increasing order; one expert is named by every token. The expert that every token names has capacity 48; some other expert has capacity 48 // 2.
All inputs are finite; a program needn't handle non-finite values.
Results may differ from a plain program's by a relative error of at most 0.028.
Values may be sent and summed in bfloat16 or wider, within the bound.
A program may use at most 192 MiB of HBM per device.

v0:
```python
import jax
import jax.numpy as jnp
from jax import lax
from jax.sharding import PartitionSpec as P

HEAD_SIZE = 128


epsilon = 1e-06
rope_base = 1000000.0
clip_limit = 1.0
masked_value = -1e30


def rms_scale(values, factor):
    return values * lax.rsqrt(jnp.mean(values * values, axis=-1, keepdims=True) + epsilon) * factor


def rms_back(gradient, values, factor):
    inverse = lax.rsqrt(jnp.mean(values * values, axis=-1, keepdims=True) + epsilon)
    normal = values * inverse
    scaled = gradient * factor
    result = inverse * (scaled - normal * jnp.mean(scaled * normal, axis=-1, keepdims=True))
    return (result, jnp.sum(gradient * normal, axis=tuple(range(values.ndim - 1))))


def turn(values):
    middle = values.shape[-1] // 2
    return jnp.concatenate([-values[..., middle:], values[..., :middle]], axis=-1)


def turn_back(values):
    middle = values.shape[-1] // 2
    return jnp.concatenate([values[..., middle:], -values[..., :middle]], axis=-1)


def rotary(offset, amount):
    inverse = 1.0 / rope_base ** (jnp.arange(0, HEAD_SIZE, 2, dtype=jnp.float32) / HEAD_SIZE)
    position = (offset + jnp.arange(amount, dtype=jnp.int32)).astype(jnp.float32)
    angle = position[:, None] * inverse[None, :]
    angle = jnp.concatenate([angle, angle], axis=-1)
    return (jnp.cos(angle), jnp.sin(angle))


def contract_last(left, right):
    return lax.dot_general(
        left, right, (((1,), (1,)), ((), ())), preferred_element_type=jnp.float32
    )


def contract_first(left, right):
    return lax.dot_general(
        left, right, (((0,), (0,)), ((), ())), preferred_element_type=jnp.float32
    )


def shards(
    hidden_in,
    segments,
    attn_gain,
    query_gain,
    key_gain,
    w_query,
    key_weight_matrix,
    value_weight_matrix,
    w_out,
    moe_gain,
    expert_ids,
    gate_values,
    capacity,
    w_gate,
    w_up,
    w_down,
    cotangent,
):
    seqs_local, rows_ctx, model_width = hidden_in.shape
    seq_length = segments.shape[1]
    expert_span = lax.axis_size("experts")
    ctx_index = lax.axis_index("context")
    own_index = lax.axis_index("experts")
    own_rows = rows_ctx // expert_span
    head_count = w_query.shape[1] // HEAD_SIZE
    kv_count = key_weight_matrix.shape[1] // HEAD_SIZE
    per_group = head_count // kv_count
    score_scale = HEAD_SIZE ** (-0.5)
    token_count = seqs_local * rows_ctx
    inputs = hidden_in.astype(jnp.float32)
    gain_attn = attn_gain.astype(jnp.float32)
    gain_query = query_gain.astype(jnp.float32)
    gain_key = key_gain.astype(jnp.float32)
    gain_moe = moe_gain.astype(jnp.float32)
    normalized_input = rms_scale(inputs, gain_attn).astype(jnp.bfloat16)
    normed_flat = normalized_input.reshape(token_count, model_width)
    query_raw = jnp.dot(normed_flat, w_query, preferred_element_type=jnp.float32).reshape(
        seqs_local, rows_ctx, head_count, HEAD_SIZE
    )
    unclipped_key = jnp.dot(
        normed_flat, key_weight_matrix, preferred_element_type=jnp.float32
    ).reshape(seqs_local, rows_ctx, kv_count, HEAD_SIZE)
    value_reduced = (
        jnp.dot(normed_flat, value_weight_matrix, preferred_element_type=jnp.float32)
        .astype(jnp.bfloat16)
        .reshape(seqs_local, rows_ctx, kv_count, HEAD_SIZE)
    )
    cosine_table, sine_table = rotary(ctx_index * rows_ctx, rows_ctx)
    cosine_table = cosine_table[None, :, None, :]
    sine_table = sine_table[None, :, None, :]
    query_normed = rms_scale(query_raw, gain_query)
    query_rot = (query_normed * cosine_table + turn(query_normed) * sine_table).astype(jnp.bfloat16)
    key_normed = rms_scale(unclipped_key, gain_key)
    key_rot = (key_normed * cosine_table + turn(key_normed) * sine_table).astype(jnp.bfloat16)
    keys_all, values_all = (
        lax.all_gather(key_rot, "context", axis=1, tiled=True),
        lax.all_gather(value_reduced, "context", axis=1, tiled=True),
    )
    query_group = query_rot.reshape(seqs_local, rows_ctx, kv_count, per_group, HEAD_SIZE)
    seg_query = lax.dynamic_slice_in_dim(segments, ctx_index * rows_ctx, rows_ctx, 1)
    query_spot = ctx_index * rows_ctx + jnp.arange(rows_ctx, dtype=jnp.int32)
    key_spot = jnp.arange(seq_length, dtype=jnp.int32)
    allowed = (seg_query[:, :, None] == segments[:, None, :]) & (
        key_spot[None, None, :] <= query_spot[None, :, None]
    )
    allowed = allowed[:, None, :, None, :]

    def masked_scores():
        raw_score = (
            jnp.einsum(
                "sqhgd,skhd->shqgk", query_group, keys_all, preferred_element_type=jnp.float32
            )
            * score_scale
        )
        return jnp.where(allowed, raw_score, masked_value)

    masked = masked_scores()
    row_peak = jnp.max(masked, axis=-1, keepdims=True)
    log_total = row_peak + jnp.log(jnp.sum(jnp.exp(masked - row_peak), axis=-1, keepdims=True))
    head_peak = jnp.max(masked, axis=(0, 2, 4)).reshape(head_count)
    prob_low = jnp.exp(masked - log_total).astype(jnp.bfloat16)
    mixed_heads = jnp.einsum(
        "shqgk,skhd->sqhgd", prob_low, values_all, preferred_element_type=jnp.float32
    )
    mixed_low = mixed_heads.astype(jnp.bfloat16).reshape(token_count, head_count * HEAD_SIZE)
    branch_part = contract_last(mixed_low, w_out)
    branch = lax.psum_scatter(
        branch_part.reshape(seqs_local, rows_ctx, model_width).astype(jnp.bfloat16),
        "experts",
        scatter_dimension=1,
        tiled=True,
    ).astype(jnp.float32)
    own_inputs = lax.dynamic_slice_in_dim(inputs, own_index * own_rows, own_rows, 1)
    after_attn = own_inputs + branch
    peak_all = lax.pmax(head_peak, ("dp", "context"))
    head_clip_scale = clip_limit / jnp.maximum(peak_all, clip_limit)
    moe_in = rms_scale(after_attn, gain_moe).astype(jnp.bfloat16)
    pair_tokens = seqs_local * own_rows
    expert_total = capacity.shape[0]
    top_count = expert_ids.shape[2]
    slot_count = pair_tokens * top_count // expert_total
    moe_rows = moe_in.reshape(pair_tokens, model_width)
    routes = expert_ids.reshape(pair_tokens, top_count)
    choose = (
        routes[:, :, None] == jnp.arange(expert_total, dtype=jnp.int32)[None, None, :]
    ).astype(jnp.float32)
    chosen = jnp.sum(choose, axis=1).astype(jnp.int32)
    before = jnp.cumsum(chosen, axis=0) - chosen
    kept = (chosen > 0) & (before < capacity[None, :])
    share = jnp.sum(gate_values.reshape(pair_tokens, top_count)[:, :, None] * choose, axis=1)
    table_mask = kept.T[:, None, :] & (
        before.T[:, None, :] == jnp.arange(slot_count, dtype=jnp.int32)[None, :, None]
    )
    table = table_mask.astype(jnp.bfloat16)
    send_rows = jnp.einsum(
        "ecn,nd->ecd", table, moe_rows, preferred_element_type=jnp.float32
    ).astype(jnp.bfloat16)
    local_rows = lax.all_to_all(
        send_rows, ("dp", "experts"), split_axis=0, concat_axis=1, tiled=True
    )
    gate_pre = jnp.einsum("erd,edf->erf", local_rows, w_gate, preferred_element_type=jnp.float32)
    up_pre = jnp.einsum("erd,edf->erf", local_rows, w_up, preferred_element_type=jnp.float32)
    sigmoid_gate = jax.nn.sigmoid(gate_pre)
    silu_gate = gate_pre * sigmoid_gate
    activation = (silu_gate * up_pre).astype(jnp.bfloat16)
    produced = jnp.einsum(
        "erf,edf->erd", activation, w_down, preferred_element_type=jnp.float32
    ).astype(jnp.bfloat16)
    returned = lax.all_to_all(produced, ("dp", "experts"), split_axis=1, concat_axis=0, tiled=True)
    per_expert = jnp.einsum("ecn,ecd->ned", table, returned, preferred_element_type=jnp.float32)
    moe_out = jnp.sum(share[:, :, None] * per_expert, axis=1)
    layer_out = after_attn + moe_out.reshape(seqs_local, own_rows, model_width)
    out_grad = cotangent.astype(jnp.float32)
    cot_rows = cotangent.reshape(pair_tokens, model_width)
    dots = jnp.sum(per_expert * out_grad.reshape(pair_tokens, 1, model_width), axis=2)
    gate_grad = jnp.sum(choose * dots[:, None, :], axis=2).reshape(seqs_local, own_rows, top_count)
    slot_share = jnp.sum(table.astype(jnp.float32) * share.T[:, None, :], axis=2)
    slot_rows = jnp.einsum("ecn,nd->ecd", table, cot_rows, preferred_element_type=jnp.float32)
    grad_send = (slot_rows * slot_share[:, :, None]).astype(jnp.bfloat16)
    grad_rows = lax.all_to_all(
        grad_send, ("dp", "experts"), split_axis=0, concat_axis=1, tiled=True
    )
    act_back = jnp.einsum("erd,edf->erf", grad_rows, w_down, preferred_element_type=jnp.float32)
    gate_back = (act_back * up_pre * sigmoid_gate * (1.0 + gate_pre * (1.0 - sigmoid_gate))).astype(
        jnp.bfloat16
    )
    up_back = (act_back * silu_gate).astype(jnp.bfloat16)
    row_back = jnp.einsum("erf,edf->erd", gate_back, w_gate, preferred_element_type=jnp.float32)
    row_back = (
        row_back + jnp.einsum("erf,edf->erd", up_back, w_up, preferred_element_type=jnp.float32)
    ).astype(jnp.bfloat16)
    back_rows = lax.all_to_all(row_back, ("dp", "experts"), split_axis=1, concat_axis=0, tiled=True)
    moe_in_grad = jnp.einsum(
        "ecn,ecd->nd", table, back_rows, preferred_element_type=jnp.float32
    ).reshape(seqs_local, own_rows, model_width)
    full_gate = jnp.einsum(
        "erd,erf->edf", local_rows, gate_back, preferred_element_type=jnp.float32
    )
    full_up = jnp.einsum("erd,erf->edf", local_rows, up_back, preferred_element_type=jnp.float32)
    full_down = jnp.einsum(
        "erd,erf->edf", grad_rows, activation, preferred_element_type=jnp.float32
    )
    w_gate_grad, w_up_grad, w_down_grad = (
        lax.psum_scatter(
            full_gate.astype(jnp.bfloat16), "context", scatter_dimension=1, tiled=True
        ).astype(jnp.float32),
        lax.psum_scatter(
            full_up.astype(jnp.bfloat16), "context", scatter_dimension=1, tiled=True
        ).astype(jnp.float32),
        lax.psum_scatter(
            full_down.astype(jnp.bfloat16), "context", scatter_dimension=1, tiled=True
        ).astype(jnp.float32),
    )
    moe_part, moe_gain_part = rms_back(moe_in_grad, after_attn, gain_moe)
    after_grad = out_grad + moe_part
    branch_grad = lax.all_gather(after_grad.astype(jnp.bfloat16), "experts", axis=1, tiled=True)
    branch_flat = branch_grad.reshape(token_count, model_width)
    heads_grad = jnp.dot(branch_flat, w_out, preferred_element_type=jnp.float32).astype(
        jnp.bfloat16
    )
    w_out_part = contract_first(branch_flat, mixed_low)
    heads_group = heads_grad.reshape(seqs_local, rows_ctx, kv_count, per_group, HEAD_SIZE)
    again_prob = jnp.exp(masked_scores() - log_total)
    again_low = again_prob.astype(jnp.bfloat16)
    prob_grad = jnp.einsum(
        "sqhgd,skhd->shqgk", heads_group, values_all, preferred_element_type=jnp.float32
    )
    delta = jnp.sum(again_prob * prob_grad, axis=-1, keepdims=True)
    score_grad = (again_prob * (prob_grad - delta)).astype(jnp.bfloat16)
    query_rot_grad = (
        jnp.einsum("shqgk,skhd->sqhgd", score_grad, keys_all, preferred_element_type=jnp.float32)
        * score_scale
    )
    key_part = (
        jnp.einsum("shqgk,sqhgd->skhd", score_grad, query_group, preferred_element_type=jnp.float32)
        * score_scale
    )
    value_part = jnp.einsum(
        "shqgk,sqhgd->skhd", again_low, heads_group, preferred_element_type=jnp.float32
    )
    key_rot_grad, value_grad = (
        lax.psum_scatter(
            key_part.astype(jnp.bfloat16), "context", scatter_dimension=1, tiled=True
        ).astype(jnp.float32),
        lax.psum_scatter(
            value_part.astype(jnp.bfloat16), "context", scatter_dimension=1, tiled=True
        ).astype(jnp.float32),
    )

    def rope_back(gradient):
        return gradient * cosine_table + turn_back(gradient * sine_table)

    query_normed_grad = rope_back(
        query_rot_grad.reshape(seqs_local, rows_ctx, head_count, HEAD_SIZE)
    )
    query_grad, query_gain_part = rms_back(query_normed_grad, query_raw, gain_query)
    key_grad, key_gain_part = rms_back(rope_back(key_rot_grad), unclipped_key, gain_key)
    query_low = query_grad.astype(jnp.bfloat16).reshape(token_count, head_count * HEAD_SIZE)
    key_low = key_grad.astype(jnp.bfloat16).reshape(token_count, kv_count * HEAD_SIZE)
    value_back = value_grad.astype(jnp.bfloat16).reshape(token_count, kv_count * HEAD_SIZE)
    normed_grad = (
        contract_last(query_low, w_query)
        + contract_last(key_low, key_weight_matrix)
        + contract_last(value_back, value_weight_matrix)
    )
    w_query_part = contract_first(normed_flat, query_low)
    w_key_part = contract_first(normed_flat, key_low)
    w_value_part = contract_first(normed_flat, value_back)
    own_normed_grad = lax.psum_scatter(
        normed_grad.reshape(seqs_local, rows_ctx, model_width).astype(jnp.bfloat16),
        "experts",
        scatter_dimension=1,
        tiled=True,
    ).astype(jnp.float32)
    input_part, attn_gain_part = rms_back(own_normed_grad, own_inputs, gain_attn)
    input_grad = after_grad + input_part
    w_query_grad, w_key_grad, w_value_grad, w_out_grad = (
        lax.psum_scatter(
            w_query_part.astype(jnp.bfloat16), ("dp", "context"), scatter_dimension=0, tiled=True
        ).astype(jnp.float32),
        lax.psum_scatter(
            w_key_part.astype(jnp.bfloat16), ("dp", "context"), scatter_dimension=0, tiled=True
        ).astype(jnp.float32),
        lax.psum_scatter(
            w_value_part.astype(jnp.bfloat16), ("dp", "context"), scatter_dimension=0, tiled=True
        ).astype(jnp.float32),
        lax.psum_scatter(
            w_out_part.astype(jnp.bfloat16), ("dp", "context"), scatter_dimension=0, tiled=True
        ).astype(jnp.float32),
    )
    attn_gain_grad, query_gain_grad, key_gain_grad, moe_gain_grad = lax.psum(
        (attn_gain_part, query_gain_part, key_gain_part, moe_gain_part),
        ("dp", "context", "experts"),
    )
    return (
        layer_out,
        input_grad,
        attn_gain_grad,
        query_gain_grad,
        key_gain_grad,
        w_query_grad,
        w_key_grad,
        w_value_grad,
        w_out_grad,
        moe_gain_grad,
        gate_grad,
        w_gate_grad,
        w_up_grad,
        w_down_grad,
        head_clip_scale,
    )


def solution(mesh):
    in_specs = (
        P("dp", "context", None),
        P("dp", None),
        P(),
        P(),
        P(),
        P(None, "experts"),
        P(None, "experts"),
        P(None, "experts"),
        P(None, "experts"),
        P(),
        P("dp", ("context", "experts"), None),
        P("dp", ("context", "experts"), None),
        P(),
        P(("dp", "experts"), None, None),
        P(("dp", "experts"), None, None),
        P(("dp", "experts"), None, None),
        P("dp", ("context", "experts"), None),
    )
    out_specs = (
        P("dp", ("context", "experts"), None),
        P("dp", ("context", "experts"), None),
        P(),
        P(),
        P(),
        P(("dp", "context"), "experts"),
        P(("dp", "context"), "experts"),
        P(("dp", "context"), "experts"),
        P(("dp", "context"), "experts"),
        P(),
        P("dp", ("context", "experts"), None),
        P(("dp", "experts"), "context", None),
        P(("dp", "experts"), "context", None),
        P(("dp", "experts"), "context", None),
        P("experts"),
    )
    return jax.shard_map(shards, mesh=mesh, in_specs=in_specs, out_specs=out_specs, check_vma=False)
```

profile of v0, /device:TPU:0, one launch (start us, length us, event | category | flops | bytes accessed | tf_op | source)
XLA Modules:
  0.0 1337.4 jit_solution(280263470778387349)
XLA Ops:
  22.7 31.8 %all_gather.10 = bf16[3,1024,1,128]{3,1,0,2:T(8,128)(2,1)} all-gather(bf16[3,128,1,128]{3,1,0,2:T(8,128)(2,1)S(1)} %fusion.73), channel_id=1, replica_groups=mesh['dp'=4,'context'=8,'experts'=4] {'context'}, dimensions={1}, use_global_device_ids=true | all-gather | bytes 884736 | tf_op jit(solution)/shard_map/all_gather | solution.py:113
  54.5 28.5 %all_gather.9 = bf16[3,1024,1,128]{1,3,0,2:T(8,128)(2,1)} all-gather(bf16[3,128,1,128]{1,3,0,2:T(8,128)(2,1)S(1)} %copy-done.31), channel_id=1, replica_groups=mesh['dp'=4,'context'=8,'experts'=4] {'context'}, dimensions={1}, use_global_device_ids=true | all-gather | bytes 884736 | tf_op jit(solution)/shard_map/all_gather | solution.py:114
  83.0 6.5 copy.202
  89.6 4.7 multiply_reduce_fusion.4
  123.1 22.1 %reduce-scatter.14.cloned.1.call-done = bf16[3,32,2048]{2,1,0:T(8,128)(2,1)} async-done(((bf16[3,128,2048]{2,1,0:T(8,128)(2,1)}), bf16[3,32,2048]{2,1,0:T(8,128)(2,1)}) %reduce-scatter.14.cloned.1.call-update) | async-done | bytes 393232 | tf_op jit(solution)/shard_map/reduce_scatter | solution.py:144
  151.0 5.6 all-to-all-start
  160.9 40.1 %all-to-all-done = bf16[16,48,2048]{2,1,0:T(8,128)(2,1)} async-done(((bf16[16,48,2048]{2,1,0:T(8,128)(2,1)}), bf16[16,48,2048]{2,1,0:T(8,128)(2,1)}, u32[]{:S(2)}, u32[]{:S(2)}) %all-to-all-start) | async-done | bytes 3145760 | tf_op jit(solution)/shard_map/all_to_all | solution.py:175
  201.0 4.9 all-to-all-start.2
  205.9 7.0 fusion.11
  212.9 5.9 fusion.15
  218.8 31.3 %all-to-all-done.2 = bf16[16,48,2048]{2,1,0:T(8,128)(2,1)} async-done(((bf16[16,48,2048]{2,1,0:T(8,128)(2,1)}), bf16[16,48,2048]{2,1,0:T(8,128)(2,1)}, u32[]{:S(2)}, u32[]{:S(2)}) %all-to-all-start.2) | async-done | bytes 3145760 | tf_op jit(solution)/shard_map/all_to_all | solution.py:197
  250.1 7.8 multiply_convert_fusion.3
  263.5 18.6 %copy.243 = bf16[1,768,2048]{2,0,1:T(2,128)(2,1)} copy(bf16[1,768,2048]{2,1,0:T(8,128)(2,1)S(1)} %fusion.23) | data formatting | bytes 6291456 | tf_op jit(solution)/shard_map/convert_element_type | solution.py:208
  282.7 20.8 %reduce.10 = bf16[768,2048]{1,0:T(8,128)(2,1)} reduce(bf16[768,1,2048]{2,1,0:T(2,128)(2,1)} %bitcast.242, bf16[]{:T(256)} %broadcast.307), dimensions={1}, to_apply=%bitcast.231.reduce_sub_computation | reduce | bytes 6291458
  303.4 7.1 reshape.520
  310.5 4.5 all-to-all-start.3
  320.6 38.7 %all-to-all-done.3 = bf16[16,2,49152]{2,1,0:T(2,128)(2,1)} async-done(((bf16[16,2,49152]{2,1,0:T(2,128)(2,1)}), bf16[16,2,49152]{2,1,0:T(2,128)(2,1)}, u32[]{:S(2)}, u32[]{:S(2)}) %all-to-all-start.3) | async-done | bytes 3145760 | tf_op jit(solution)/shard_map/all_to_all | solution.py:209
  359.3 11.5 reshape.521
  370.8 4.8 copy.212
  379.5 23.3 %all-gather.2.cloned.1.call-done = bf16[3,128,2048]{2,1,0:T(8,128)(2,1)} async-done(((bf16[3,32,2048]{2,1,0:T(8,128)(2,1)}), bf16[3,128,2048]{2,1,0:T(8,128)(2,1)}) %all-gather.2.cloned.1.call-update) | async-done | bytes 1572880 | tf_op jit(solution)/shard_map/all_gather | solution.py:233
  402.7 4.5 fusion.37
  408.2 7.5 fusion.39
  420.5 12.1 fusion.85
  433.8 6.4 multiply_convert_fusion
  446.1 6.5 fusion.22
  452.7 6.5 fusion.21
  459.7 6.6 fusion.20
  466.4 5.2 bitcast_multiply_fusion.3
  484.2 14.8 %reduce-scatter.16.cloned.1.call-done = bf16[3,128,1,128]{3,1,0,2:T(8,128)(2,1)} async-done(((bf16[3,1024,1,128]{3,1,0,2:T(8,128)(2,1)}), bf16[3,128,1,128]{3,1,0,2:T(8,128)(2,1)}) %reduce-scatter.16.cloned.1.call-update) | async-done | bytes 98320 | tf_op jit(solution)/shard_map/reduce_scatter | solution.py:259
  506.7 4.5 fusion.51
  516.8 6.0 convolution_convert_fusion
  522.9 6.1 convolution_convert_fusion.1
  529.0 4.1 fusion.17
  533.2 18.6 %copy.244 = bf16[1,768,2048]{2,0,1:T(2,128)(2,1)} copy(bf16[1,768,2048]{2,1,0:T(8,128)(2,1)S(1)} %fusion.17) | data formatting | bytes 6291456 | tf_op jit(solution)/shard_map/convert_element_type | solution.py:185
  551.8 20.6 %reduce.11 = bf16[768,2048]{1,0:T(8,128)(2,1)} reduce(bf16[768,1,2048]{2,1,0:T(2,128)(2,1)} %bitcast.243, bf16[]{:T(256)} %broadcast.307), dimensions={1}, to_apply=%bitcast.232.reduce_sub_computation | reduce | bytes 6291458
  572.4 7.0 reshape.518
  579.4 6.9 all-to-all-start.1
  587.9 47.2 %all-to-all-done.1 = bf16[16,2,49152]{2,1,0:T(2,128)(2,1)} async-done(((bf16[16,2,49152]{2,1,0:T(2,128)(2,1)}), bf16[16,2,49152]{2,1,0:T(2,128)(2,1)}, u32[]{:S(2)}, u32[]{:S(2)}) %all-to-all-start.1) | async-done | bytes 3145760 | tf_op jit(solution)/shard_map/all_to_all | solution.py:186
  635.1 11.5 reshape.519
  646.6 4.8 copy.211
  658.6 74.5 %pmax.7 = f32[8]{0:T(128)} all-reduce(f32[8]{0:T(128)} %get-tuple-element.105), channel_id=1, replica_groups=mesh['dp'=4,'context'=8,'experts'=4] {'dp','context'}, use_global_device_ids=true, to_apply=%region_39.40 | all-reduce | flops 8 | bytes 64 | tf_op jit(solution)/shard_map/pmax | solution.py:152
  738.1 15.6 %reduce-scatter.28.cloned.1.call-done = bf16[1,256,768]{2,1,0:T(8,128)(2,1)} async-done(((bf16[1,2048,768]{2,1,0:T(8,128)(2,1)}), bf16[1,256,768]{2,1,0:T(8,128)(2,1)}) %reduce-scatter.28.cloned.1.call-update) | async-done | bytes 393232 | tf_op jit(solution)/shard_map/reduce_scatter | solution.py:221
  755.7 133.9 %reduce-scatter.24.cloned.1.call-done = bf16[64,128]{1,0:T(8,128)(2,1)} async-done(((bf16[2048,128]{1,0:T(8,128)(2,1)}), bf16[64,128]{1,0:T(8,128)(2,1)}) %reduce-scatter.24.cloned.1.call-update) | async-done | bytes 16400 | tf_op jit(solution)/shard_map/reduce_scatter | solution.py:301
  890.9 130.1 %reduce-scatter.22.cloned.1.call-done = bf16[64,128]{1,0:T(8,128)(2,1)} async-done(((bf16[2048,128]{1,0:T(8,128)(2,1)}), bf16[64,128]{1,0:T(8,128)(2,1)}) %reduce-scatter.22.cloned.1.call-update) | async-done | bytes 16400 | tf_op jit(solution)/shard_map/reduce_scatter | solution.py:298
  1022.3 23.2 %reduce-scatter.18.cloned.1.call-done = bf16[3,32,2048]{2,1,0:T(8,128)(2,1)} async-done(((bf16[3,128,2048]{2,1,0:T(8,128)(2,1)}), bf16[3,32,2048]{2,1,0:T(8,128)(2,1)}) %reduce-scatter.18.cloned.1.call-update) | async-done | bytes 393232 | tf_op jit(solution)/shard_map/reduce_scatter | solution.py:286
  1047.8 67.2 %all-reduce = (f32[2048]{0:T(1024)}, f32[128]{0:T(128)}, f32[128]{0:T(128)}, f32[2048]{0:T(1024)}) all-reduce(f32[2048]{0:T(1024)} %get-tuple-element.109, f32[128]{0:T(128)} %get-tuple-element.111, f32[128]{0:T(128)} %get-tuple-element.115, ...), channel_id=1, replica_groups=mesh['dp'=4,'context'=8,'experts'=4] {'dp','context','experts'}, use_global_device_ids=true, to_apply=%region_22.23 | all-reduce | flops 4352 | bytes 34816 | tf_op jit(solution)/shard_map/psum | solution.py:308
  1119.1 69.5 %reduce-scatter.26.cloned.1.call-done = bf16[64,1024]{1,0:T(8,128)(2,1)} async-done(((bf16[2048,1024]{1,0:T(8,128)(2,1)}), bf16[64,1024]{1,0:T(8,128)(2,1)}) %reduce-scatter.26.cloned.1.call-update) | async-done | bytes 131088 | tf_op jit(solution)/shard_map/reduce_scatter | solution.py:304
  1190.2 138.5 %reduce-scatter.20.cloned.1.call-done = bf16[64,1024]{1,0:T(8,128)(2,1)} async-done(((bf16[2048,1024]{1,0:T(8,128)(2,1)}), bf16[64,1024]{1,0:T(8,128)(2,1)}) %reduce-scatter.20.cloned.1.call-update) | async-done | bytes 131088 | tf_op jit(solution)/shard_map/reduce_scatter | solution.py:295
  (267 shorter events, 136.5 us)
Async XLA Ops:
  7.2 242.9 %copy-start = (bf16[1,2048,768]{2,1,0:T(8,128)(2,1)S(1)}, bf16[1,2048,768]{2,1,0:T(8,128)(2,1)}, u32[]{:S(2)}) copy-start(bf16[1,2048,768]{2,1,0:T(8,128)(2,1)} %param.32) | copy-start | bytes 9437188
  7.2 138.0 %reduce-scatter.14.cloned.1.call-start = ((), (), s32[]{:S(2)}) async-start(), calls=%async_computation.15 | async-start | bytes 1966080 | tf_op jit(solution)/shard_map/reduce_scatter | solution.py:144
  9.9 12.2 copy-start.53
  12.4 9.5 copy-start.36
  12.7 84.7 %copy-start.21 = (f32[128,128]{0,1:T(8,128)}, f32[128,128]{0,1:T(8,128)S(1)}, u32[]{:S(2)}) copy-start(f32[128,128]{0,1:T(8,128)S(1)} %get-tuple-element.145) | copy-start | bytes 196612
  12.7 84.7 %copy-start.22 = (f32[128,128]{0,1:T(8,128)}, f32[128,128]{0,1:T(8,128)S(1)}, u32[]{:S(2)}) copy-start(f32[128,128]{0,1:T(8,128)S(1)} %get-tuple-element.144) | copy-start | bytes 196612
  12.8 9.3 copy-start.29
  12.9 9.2 copy-start.30
  19.7 34.9 %copy-start.31 = (bf16[3,128,1,128]{1,3,0,2:T(8,128)(2,1)S(1)}, bf16[3,128,1,128]{1,3,0,2:T(8,128)(2,1)}, u32[]{:S(2)}) copy-start(bf16[3,128,1,128]{1,3,0,2:T(8,128)(2,1)} %copy.169) | copy-start | bytes 294916
  89.6 5.8 copy-start.56
  121.4 26.9 %copy-start.38 = (f32[2048]{0:T(1024)}, f32[2048]{0:T(1024)S(1)}, u32[]{:S(2)}) copy-start(f32[2048]{0:T(1024)S(1)} %convert_element_type.234) | copy-start | bytes 24580
  123.1 25.2 %copy-start.32 = (s32[96,16]{0,1:T(8,128)}, s32[96,16]{0,1:T(8,128)S(1)}, u32[]{:S(2)}) copy-start(s32[96,16]{0,1:T(8,128)S(1)} %get-tuple-element.127) | copy-start | bytes 18436
  123.1 25.2 %copy-start.45 = (pred[16,96]{1,0:T(8,128)(4,1)}, pred[16,96]{1,0:T(8,128)(4,1)S(1)}, u32[]{:S(2)}) copy-start(pred[16,96]{1,0:T(8,128)(4,1)S(1)} %get-tuple-element.125) | copy-start | bytes 4612
  151.0 6.5 copy-start.13
  151.0 50.0 %all-to-all-start = ((bf16[16,48,2048]{2,1,0:T(8,128)(2,1)}), bf16[16,48,2048]{2,1,0:T(8,128)(2,1)}, u32[]{:S(2)}, u32[]{:S(2)}) async-start(bf16[16,48,2048]{2,1,0:T(8,128)(2,1)} %convolution_convert_fusion.6), calls=%async_computation.1 | async-start | bytes 6291456 | tf_op jit(solution)/shard_map/all_to_all | solution.py:175
  201.0 49.1 %all-to-all-start.2 = ((bf16[16,48,2048]{2,1,0:T(8,128)(2,1)}), bf16[16,48,2048]{2,1,0:T(8,128)(2,1)}, u32[]{:S(2)}, u32[]{:S(2)}) async-start(bf16[16,48,2048]{2,1,0:T(8,128)(2,1)} %multiply_convert_fusion.1), calls=%async_computation.3 | async-start | bytes 6291456 | tf_op jit(solution)/shard_map/all_to_all | solution.py:197
  205.9 7.0 copy-start.62
  250.1 7.8 copy-start.63
  310.5 48.8 %all-to-all-start.3 = ((bf16[16,2,49152]{2,1,0:T(2,128)(2,1)}), bf16[16,2,49152]{2,1,0:T(2,128)(2,1)}, u32[]{:S(2)}, u32[]{:S(2)}) async-start(bf16[16,2,49152]{2,1,0:T(2,128)(2,1)} %reshape.520), calls=%async_computation.4 | async-start | bytes 6291456 | tf_op jit(solution)/shard_map/all_to_all | solution.py:209
  315.0 87.7 %all-gather.2.cloned.1.call-start = ((), (), s32[]{:S(2)}) async-start(), calls=%async_computation.16 | async-start | bytes 1966080 | tf_op jit(solution)/shard_map/all_gather | solution.py:233
  370.8 4.9 copy-start.39
  370.8 4.9 copy-start.44
  370.8 4.9 copy-start.48
  370.8 4.9 copy-start.58
  379.4 98.8 %reduce-scatter.34.cloned.1.call-start = ((), (), s32[]{:S(2)}) async-start(), calls=%async_computation.26 | async-start | bytes 884736
  420.4 78.7 %reduce-scatter.16.cloned.1.call-start = ((), (), s32[]{:S(2)}) async-start(), calls=%async_computation.17 | async-start | bytes 884736 | tf_op jit(solution)/shard_map/reduce_scatter | solution.py:259
  420.4 12.1 slice-start
  420.5 12.1 slice-start.1
  420.5 13.3 slice-start.2
  420.5 13.3 copy-start.35
  433.8 9.0 copy-start.12
  446.0 288.3 %reduce-scatter.32.cloned.1.call-start = ((), (), s32[]{:S(2)}) async-start(), calls=%async_computation.25 | async-start | bytes 3538944 | tf_op jit(solution)/shard_map/reduce_scatter | solution.py:227
  452.6 283.6 %reduce-scatter.30.cloned.1.call-start = ((), (), s32[]{:S(2)}) async-start(), calls=%async_computation.24 | async-start | bytes 3538944 | tf_op jit(solution)/shard_map/reduce_scatter | solution.py:224
  459.3 294.5 %reduce-scatter.28.cloned.1.call-start = ((), (), s32[]{:S(2)}) async-start(), calls=%async_computation.23 | async-start | bytes 3538944 | tf_op jit(solution)/shard_map/reduce_scatter | solution.py:221
  466.3 423.2 %reduce-scatter.24.cloned.1.call-start = ((), (), s32[]{:S(2)}) async-start(), calls=%async_computation.21 | async-start | bytes 540672 | tf_op jit(solution)/shard_map/reduce_scatter | solution.py:301
  475.8 24.3 %copy-start.54 = (f32[128]{0:T(128)S(1)}, f32[128]{0:T(128)}, u32[]{:S(2)}) copy-start(f32[128]{0:T(128)} %copy-done.53) | copy-start | bytes 1540
  484.2 536.8 %reduce-scatter.22.cloned.1.call-start = ((), (), s32[]{:S(2)}) async-start(), calls=%async_computation.20 | async-start | bytes 540672 | tf_op jit(solution)/shard_map/reduce_scatter | solution.py:298
  506.6 539.0 %reduce-scatter.18.cloned.1.call-start = ((), (), s32[]{:S(2)}) async-start(), calls=%async_computation.18 | async-start | bytes 1966080 | tf_op jit(solution)/shard_map/reduce_scatter | solution.py:286
  514.2 674.4 %reduce-scatter.26.cloned.1.call-start = ((), (), s32[]{:S(2)}) async-start(), calls=%async_computation.22 | async-start | bytes 4325376 | tf_op jit(solution)/shard_map/reduce_scatter | solution.py:304
  522.9 805.9 %reduce-scatter.20.cloned.1.call-start = ((), (), s32[]{:S(2)}) async-start(), calls=%async_computation.19 | async-start | bytes 4325376 | tf_op jit(solution)/shard_map/reduce_scatter | solution.py:295
  579.4 7.9 copy-start.55
  579.4 55.6 %all-to-all-start.1 = ((bf16[16,2,49152]{2,1,0:T(2,128)(2,1)}), bf16[16,2,49152]{2,1,0:T(2,128)(2,1)}, u32[]{:S(2)}, u32[]{:S(2)}) async-start(bf16[16,2,49152]{2,1,0:T(2,128)(2,1)} %reshape.518), calls=%async_computation.2 | async-start | bytes 6291456 | tf_op jit(solution)/shard_map/all_to_all | solution.py:186
  646.6 4.9 copy-start.28
  646.6 4.9 copy-start.33
  646.6 4.9 copy-start.46
  646.6 4.9 copy-start.47
  655.2 390.3 %copy-start.37 = (f32[2048]{0:T(1024)S(1)}, f32[2048]{0:T(1024)}, u32[]{:S(2)}) copy-start(f32[2048]{0:T(1024)} %copy-done.36) | copy-start | bytes 24580
  655.3 460.3 %copy-start.40 = (f32[2048]{0:T(1024)S(1)}, f32[2048]{0:T(1024)}, u32[]{:S(2)}) copy-start(f32[2048]{0:T(1024)} %copy-done.38) | copy-start | bytes 24580
  (38 other events, 87.1 us)
Sparse Core Ops, SparseCore 0:
  118.0 27.1 reduce-scatter.13
  379.5 23.1 all-gather.1
  420.5 38.4 reduce-scatter.33
  462.0 37.0 reduce-scatter.15
  501.4 69.1 reduce-scatter.31
  572.9 105.6 reduce-scatter.29
  681.0 72.7 reduce-scatter.27
  756.1 133.4 reduce-scatter.23
  892.0 128.8 reduce-scatter.21
  1023.2 22.2 reduce-scatter.17
  1048.0 140.5 reduce-scatter.25
  1190.8 137.8 reduce-scatter.19
where the time goes:
time: 1350 us; the launch traced here: 1340 us
  waiting for transfers between devices  728 us (54%)
  blocking collectives  202 us (15%)
  matrix products  135 us (10%)
  local copies, waits for them, and re-layouts  130 us (10%)
  other arithmetic  104 us (8%)
  starting transfers between devices  23 us (2%)
  between operations  15.3 us (1%)
    reduce_scatter x1, waiting for transfers between devices, shards(): lax.psum_scatter(w_query_part.astype(jnp.bfloat16), ('dp', 'context'), sc...  138 us
    reduce_scatter x1, waiting for transfers between devices, shards(): lax.psum_scatter(w_value_part.astype(jnp.bfloat16), ('dp', 'context'), sc...  134 us
    reduce_scatter x1, waiting for transfers between devices, shards(): lax.psum_scatter(w_key_part.astype(jnp.bfloat16), ('dp', 'context'), scat...  130 us
    pmax x1, blocking collectives, shards(): peak_all = lax.pmax(head_peak, ('dp', 'context'))  74.5 us
    unnamed x154, local copies, waits for them, and re-layouts  72.1 us
    reduce_scatter x1, waiting for transfers between devices, shards(): lax.psum_scatter(w_out_part.astype(jnp.bfloat16), ('dp', 'context'), scat...  69.5 us
    psum x1, blocking collectives, shards(): lax.psum((attn_gain_part, query_gain_part, key_gain_part, moe_gain_part),...  67.2 us
    all_to_all x1, waiting for transfers between devices, shards(): lax.all_to_all(produced, ('dp', 'experts'), split_axis=1, concat_axis=0,...  47.2 us
  transfers between devices with their start and end apart: 16, of which 13 were waited for; matrix products, arithmetic and copies ran while one was open for 15% of the time, Pallas kernels for 0%

commit v1 on v0

--- a/solution.py
+++ b/solution.py
@@ -1,9 +1,16 @@
+import functools
+import itertools
+
 import jax
 import jax.numpy as jnp
 from jax import lax
+from jax.experimental import pallas as pl
+from jax.experimental.pallas import tpu as pltpu
 from jax.sharding import PartitionSpec as P
 
 HEAD_SIZE = 128
+MESH = pl.DeviceIdType.MESH
+VMEM = pl.BlockSpec(memory_space=pltpu.VMEM)
 
 
 epsilon = 1e-06
@@ -51,6 +58,280 @@
 def contract_first(left, right):
     return lax.dot_general(
         left, right, (((0,), (0,)), ((), ())), preferred_element_type=jnp.float32
+    )
+
+
+class Place:
+    def __init__(self):
+        dp = lax.axis_index("dp")
+        context = lax.axis_index("context")
+        self.dp, self.context, self.y = dp, context, lax.axis_index("experts")
+        self.core, self.z_hi = lax.rem(dp, 2), dp // 2
+        self.x, self.z_lo = context // 2, lax.rem(context, 2)
+        self.z = self.z_hi * 2 + self.z_lo
+
+    def at(self, x=None, y=None, z=None, core=None):
+        x = self.x if x is None else x
+        y = self.y if y is None else y
+        z = self.z if z is None else z
+        core = self.core if core is None else core
+        return (z // 2 * 2 + core, x * 2 + lax.rem(z, 2), y)
+
+    def x_by(self, step):
+        return lax.rem(self.x + step, 4)
+
+    def y_by(self, step):
+        return lax.rem(self.y + step, 4)
+
+    def z_by(self, step):
+        return lax.rem(self.z + step, 4)
+
+
+class Net:
+    def __init__(self, send, recv):
+        self.send, self.recv, self.copies = send, recv, []
+
+    def copy(self, src, dst, device):
+        spot = len(self.copies)
+        made = pltpu.make_async_remote_copy(
+            src_ref=src,
+            dst_ref=dst,
+            send_sem=self.send.at[spot],
+            recv_sem=self.recv.at[spot],
+            device_id=device,
+            device_id_type=MESH,
+        )
+        made.start()
+        self.copies.append(made)
+        return made
+
+    def finish(self):
+        for made in self.copies:
+            made.wait_send()
+
+
+def greet(devices):
+    barrier = pltpu.get_barrier_semaphore()
+    for device in devices:
+        pl.semaphore_signal(barrier, inc=1, device_id=device, device_id_type=MESH)
+    pl.semaphore_wait(barrier, len(devices))
+
+
+def add_into(target, parts, block=32):
+    rows = target.shape[-2]
+    block = min(block, rows)
+    for lead in itertools.product(*[range(size) for size in target.shape[:-2]]):
+
+        def body(step, carry, lead=lead):
+            spot = lead + (pl.ds(pl.multiple_of(step * block, block), block),)
+            total = parts[0][spot].astype(jnp.float32)
+            for part in parts[1:]:
+                total = total + part[spot].astype(jnp.float32)
+            target[spot] = total.astype(target.dtype)
+            return carry
+
+        lax.fori_loop(0, rows // block, body, 0)
+
+
+def ring_reduce(net, plus, minus, own, slots, target):
+    first_plus = net.copy(own(2, 0), slots.at[0], plus)
+    first_minus = net.copy(own(2, 1), slots.at[2], minus)
+    side_plus = net.copy(own(1, 1), slots.at[1], plus)
+    side_minus = net.copy(own(3, 0), slots.at[3], minus)
+    yield
+    first_plus.wait_recv()
+    add_into(slots.at[0], [slots.at[0], own(1, 0)])
+    last_plus = net.copy(slots.at[0], slots.at[4], plus)
+    first_minus.wait_recv()
+    add_into(slots.at[2], [slots.at[2], own(3, 1)])
+    last_minus = net.copy(slots.at[2], slots.at[5], minus)
+    yield
+    side_minus.wait_recv()
+    last_plus.wait_recv()
+    add_into(target(0), [own(0, 0), slots.at[3], slots.at[4]])
+    side_plus.wait_recv()
+    last_minus.wait_recv()
+    add_into(target(1), [own(0, 1), slots.at[1], slots.at[5]])
+
+
+def expert_x_first(net, me, source, slots, middle, other, out):
+    ring = ring_reduce(
+        net,
+        me.at(x=me.x_by(1)),
+        me.at(x=me.x_by(3)),
+        lambda step, half: source.at[me.x_by(step), half],
+        slots,
+        lambda half: middle.at[half],
+    )
+    yield from ring
+    across = net.copy(middle.at[1 - me.z_lo], other, me.at(z=me.z + 1 - 2 * me.z_lo))
+    yield
+    across.wait_recv()
+    add_into(out, [middle.at[me.z_lo], other])
+
+
+def expert_z_first(net, me, source, other, middle, slots, out):
+    across = net.copy(source.at[:, 1 - me.z_lo], other, me.at(z=me.z + 1 - 2 * me.z_lo))
+    yield
+    across.wait_recv()
+    add_into(middle, [source.at[:, me.z_lo], other])
+    half_rows = middle.shape[1] // 2
+    yield from ring_reduce(
+        net,
+        me.at(x=me.x_by(1)),
+        me.at(x=me.x_by(3)),
+        lambda step, half: middle.at[me.x_by(step), pl.ds(half * half_rows, half_rows)],
+        slots,
+        lambda half: out.at[pl.ds(half * half_rows, half_rows)],
+    )
+
+
+def core_pair(net, me, source, other, middle):
+    across = net.copy(source.at[:, 1 - me.core], other, me.at(core=1 - me.core))
+    yield
+    across.wait_recv()
+    add_into(middle, [source.at[:, me.core], other])
+
+
+def dense_x_first(net, me, source, other, middle, slots, corner, last, out):
+    yield from core_pair(net, me, source, other, middle)
+    yield from ring_reduce(
+        net,
+        me.at(x=me.x_by(1)),
+        me.at(x=me.x_by(3)),
+        lambda step, half: middle.at[half, me.x_by(step)],
+        slots,
+        lambda half: corner.at[half],
+    )
+    half_rows = corner.shape[2] // 2
+    yield from ring_reduce(
+        net,
+        me.at(z=me.z_by(1)),
+        me.at(z=me.z_by(3)),
+        lambda step, half: corner.at[
+            me.z_by(step) // 2, lax.rem(me.z_by(step), 2), pl.ds(half * half_rows, half_rows)
+        ],
+        last,
+        lambda half: out.at[pl.ds(half * half_rows, half_rows)],
+    )
+
+
+def dense_z_first(net, me, source, other, middle, slots, corner, last, out):
+    yield from core_pair(net, me, source, other, middle)
+    yield from ring_reduce(
+        net,
+        me.at(z=me.z_by(1)),
+        me.at(z=me.z_by(3)),
+        lambda step, half: middle.at[
+            me.z_by(step) // 2, pl.ds(half * 2, 2), lax.rem(me.z_by(step), 2)
+        ],
+        slots,
+        lambda half: corner.at[pl.ds(half * 2, 2)],
+    )
+    half_rows = corner.shape[1] // 2
+    yield from ring_reduce(
+        net,
+        me.at(x=me.x_by(1)),
+        me.at(x=me.x_by(3)),
+        lambda step, half: corner.at[me.x_by(step), pl.ds(half * half_rows, half_rows)],
+        last,
+        lambda half: out.at[pl.ds(half * half_rows, half_rows)],
+    )
+
+
+def in_turn(tasks):
+    tasks = list(tasks)
+    while tasks:
+        for task in list(tasks):
+            if next(task, "end") == "end":
+                tasks.remove(task)
+
+
+def reduce_kernel(counts, *refs):
+    refs = list(refs)
+
+    def take(number):
+        taken = refs[:number]
+        del refs[:number]
+        return taken
+
+    gate, up, down, query, key_value, out_w = take(6)
+    gate_out, up_out, down_out, query_out, key_value_out, out_w_out = take(6)
+    scratch = [take(count) for count in counts]
+    send, recv = take(2)
+    me = Place()
+    greet(
+        [
+            me.at(x=me.x_by(1)),
+            me.at(x=me.x_by(3)),
+            me.at(z=me.z_by(1)),
+            me.at(z=me.z_by(3)),
+            me.at(core=1 - me.core),
+        ]
+    )
+    net = Net(send, recv)
+    in_turn(
+        [
+            dense_z_first(net, me, out_w, *scratch[5], out_w_out),
+            dense_x_first(net, me, query, *scratch[3], query_out),
+            dense_x_first(net, me, key_value, *scratch[4], key_value_out),
+            expert_z_first(net, me, down, *scratch[2], down_out),
+            expert_x_first(net, me, gate, *scratch[0], gate_out),
+            expert_x_first(net, me, up, *scratch[1], up_out),
+        ]
+    )
+    net.finish()
+
+
+def reduce_weights(gate, up, down, query, key_value, out_w):
+    low = jnp.bfloat16
+    x_first = [
+        pltpu.VMEM((6, 256, 768), low),
+        pltpu.VMEM((2, 256, 768), low),
+        pltpu.VMEM((256, 768), low),
+    ]
+    z_first = [
+        pltpu.VMEM((4, 256, 768), low),
+        pltpu.VMEM((4, 256, 768), low),
+        pltpu.VMEM((6, 128, 768), low),
+    ]
+
+    def dense(columns, x_first):
+        return [
+            pltpu.VMEM((2, 4, 2, 64, columns), low),
+            pltpu.VMEM((2, 4, 2, 64, columns), low),
+            pltpu.VMEM((6, 2, 64, columns), low),
+            pltpu.VMEM((2, 2, 64, columns) if x_first else (4, 64, columns), low),
+            pltpu.VMEM((6, 32, columns), low),
+        ]
+
+    groups = [x_first, x_first, z_first, dense(1024, True), dense(256, True), dense(1024, False)]
+    copies = 64
+    return pl.pallas_call(
+        functools.partial(reduce_kernel, [len(group) for group in groups]),
+        out_shape=[
+            jax.ShapeDtypeStruct((256, 768), jnp.float32),
+            jax.ShapeDtypeStruct((256, 768), jnp.float32),
+            jax.ShapeDtypeStruct((256, 768), jnp.float32),
+            jax.ShapeDtypeStruct((64, 1024), jnp.float32),
+            jax.ShapeDtypeStruct((64, 256), jnp.float32),
+            jax.ShapeDtypeStruct((64, 1024), jnp.float32),
+        ],
+        in_specs=[VMEM] * 6,
+        out_specs=[VMEM] * 6,
+        scratch_shapes=[one for group in groups for one in group]
+        + [pltpu.SemaphoreType.DMA((copies,)), pltpu.SemaphoreType.DMA((copies,))],
+        compiler_params=pltpu.CompilerParams(
+            collective_id=0, has_side_effects=True, vmem_limit_bytes=56 << 20
+        ),
+        name="reduce_weights",
+    )(
+        gate.reshape(4, 2, 256, 768),
+        up.reshape(4, 2, 256, 768),
+        down.reshape(4, 2, 256, 768),
+        query.reshape(2, 2, 4, 2, 64, 1024),
+        key_value.reshape(2, 2, 4, 2, 64, 256),
+        out_w.reshape(2, 2, 4, 2, 64, 1024),
     )
 
 
@@ -217,17 +498,6 @@
     full_down = jnp.einsum(
         "erd,erf->edf", grad_rows, activation, preferred_element_type=jnp.float32
     )
-    w_gate_grad, w_up_grad, w_down_grad = (
-        lax.psum_scatter(
-            full_gate.astype(jnp.bfloat16), "context", scatter_dimension=1, tiled=True
-        ).astype(jnp.float32),
-        lax.psum_scatter(
-            full_up.astype(jnp.bfloat16), "context", scatter_dimension=1, tiled=True
-        ).astype(jnp.float32),
-        lax.psum_scatter(
-            full_down.astype(jnp.bfloat16), "context", scatter_dimension=1, tiled=True
-        ).astype(jnp.float32),
-    )
     moe_part, moe_gain_part = rms_back(moe_in_grad, after_attn, gain_moe)
     after_grad = out_grad + moe_part
     branch_grad = lax.all_gather(after_grad.astype(jnp.bfloat16), "experts", axis=1, tiled=True)
@@ -291,20 +561,19 @@
     ).astype(jnp.float32)
     input_part, attn_gain_part = rms_back(own_normed_grad, own_inputs, gain_attn)
     input_grad = after_grad + input_part
-    w_query_grad, w_key_grad, w_value_grad, w_out_grad = (
-        lax.psum_scatter(
-            w_query_part.astype(jnp.bfloat16), ("dp", "context"), scatter_dimension=0, tiled=True
-        ).astype(jnp.float32),
-        lax.psum_scatter(
-            w_key_part.astype(jnp.bfloat16), ("dp", "context"), scatter_dimension=0, tiled=True
-        ).astype(jnp.float32),
-        lax.psum_scatter(
-            w_value_part.astype(jnp.bfloat16), ("dp", "context"), scatter_dimension=0, tiled=True
-        ).astype(jnp.float32),
-        lax.psum_scatter(
-            w_out_part.astype(jnp.bfloat16), ("dp", "context"), scatter_dimension=0, tiled=True
-        ).astype(jnp.float32),
-    )
+    key_value_part = jnp.concatenate([w_key_part, w_value_part], axis=1)
+    w_gate_grad, w_up_grad, w_down_grad, w_query_grad, w_key_value_grad, w_out_grad = (
+        reduce_weights(
+            full_gate.astype(jnp.bfloat16),
+            full_up.astype(jnp.bfloat16),
+            full_down.astype(jnp.bfloat16),
+            w_query_part.astype(jnp.bfloat16),
+            key_value_part.astype(jnp.bfloat16),
+            w_out_part.astype(jnp.bfloat16),
+        )
+    )
+    w_key_grad, w_value_grad = w_key_value_grad[:, :128], w_key_value_grad[:, 128:]
+    w_gate_grad, w_up_grad, w_down_grad = w_gate_grad[None], w_up_grad[None], w_down_grad[None]
     attn_gain_grad, query_gain_grad, key_gain_grad, moe_gain_grad = lax.psum(
         (attn_gain_part, query_gain_part, key_gain_part, moe_gain_part),
         ("dp", "context", "experts"),

time: 1350 us -> 850 us (0.63)
  waiting for transfers between devices: 728 us -> 167 us
  Pallas kernels: 0 us -> 103 us
  blocking collectives: 202 us -> 186 us
    reduce_scatter x7 -> x0, waiting for transfers between devices: 488 us -> none  [the longest x1 138 us: shards(): lax.psum_scatter(w_query_part.astype(jnp.bfloat16), ('dp', 'context'), sc...]
    pallas_call x0 -> x1, Pallas kernels: none -> 103 us  [reduce_weights(): pl.pallas_call(functools.partial(reduce_kernel, [len(group) for group in...]
    all_to_all x1, waiting for transfers between devices: 47.2 us -> 0.01 us  [shards(): lax.all_to_all(produced, ('dp', 'experts'), split_axis=1, concat_axis=0,...]
    all_gather x1, waiting for transfers between devices: 23.3 us -> 0.01 us  [shards(): lax.all_gather(after_grad.astype(jnp.bfloat16), 'experts', axis=1, tiled=...]
    reduce_scatter x1, waiting for transfers between devices: 23.2 us -> 0.01 us  [shards(): lax.psum_scatter(normed_grad.reshape(seqs_local, rows_ctx, model_width).a...]
    reduce_scatter x1, waiting for transfers between devices: 14.8 us -> 34.3 us  [shards(): lax.psum_scatter(key_part.astype(jnp.bfloat16), 'context', scatter_dimens...]
    unnamed x154 -> x201, local copies, waits for them, and re-layouts: 72.1 us -> 68.3 us
  transfers between devices with their start and end apart: 16 -> 9, of which waited for: 13 -> 5; matrix products, arithmetic and copies ran while one was open for 15% -> 23% of each run, Pallas kernels for 0% -> 12%
where the time goes in v1:
time: 850 us; the launch traced here: 841 us
  blocking collectives  186 us (22%)
  waiting for transfers between devices  167 us (20%)
  matrix products  132 us (16%)
  local copies, waits for them, and re-layouts  127 us (15%)
  Pallas kernels  103 us (12%)
  other arithmetic  91.8 us (11%)
  starting transfers between devices  20.3 us (2%)
  between operations  15.3 us (2%)
    pallas_call x1, Pallas kernels, reduce_weights(): pl.pallas_call(functools.partial(reduce_kernel, [len(group) for group in...  103 us
    unnamed x201, local copies, waits for them, and re-layouts  68.3 us
    psum x1, blocking collectives, shards(): lax.psum((attn_gain_part, query_gain_part, key_gain_part, moe_gain_part),...  64.1 us
    pmax x1, blocking collectives, shards(): peak_all = lax.pmax(head_peak, ('dp', 'context'))  62.9 us
    all_to_all x1, waiting for transfers between devices, shards(): lax.all_to_all(send_rows, ('dp', 'experts'), split_axis=0, concat_axis=1,...  40.1 us
    unnamed x3, other arithmetic  39.6 us
    all_to_all x1, waiting for transfers between devices, shards(): lax.all_to_all(row_back, ('dp', 'experts'), split_axis=1, concat_axis=0,...  38.7 us
    reduce_scatter x1, waiting for transfers between devices, shards(): lax.psum_scatter(key_part.astype(jnp.bfloat16), 'context', scatter_dimens...  34.3 us
  transfers between devices with their start and end apart: 9, of which 5 were waited for; matrix products, arithmetic and copies ran while one was open for 23% of the time, Pallas kernels for 12%

profile of v1, /device:TPU:0, one launch (start us, length us, event | category | flops | bytes accessed | tf_op | source)
XLA Modules:
  0.0 840.7 jit_solution(4455151886098998393)
XLA Ops:
  17.7 31.8 %all_gather.10 = bf16[3,1024,1,128]{3,1,0,2:T(8,128)(2,1)} all-gather(bf16[3,128,1,128]{3,1,0,2:T(8,128)(2,1)S(1)} %fusion.70), channel_id=1, replica_groups=mesh['dp'=4,'context'=8,'experts'=4] {'context'}, dimensions={1}, use_global_device_ids=true | all-gather | bytes 884736 | tf_op jit(solution)/shard_map/all_gather | solution.py:394
  49.5 6.5 copy.211
  56.0 4.7 multiply_reduce_fusion.4
  67.3 4.4 fusion.87
  76.3 3.9 fusion.2
  80.9 26.9 %all_gather.9 = bf16[3,1024,1,128]{1,3,0,2:T(8,128)(2,1)S(1)} all-gather(bf16[3,128,1,128]{1,3,0,2:T(8,128)(2,1)S(1)} %copy.175), channel_id=1, replica_groups=mesh['dp'=4,'context'=8,'experts'=4] {'context'}, dimensions={1}, use_global_device_ids=true | all-gather | bytes 884736 | tf_op jit(solution)/shard_map/all_gather | solution.py:395
  107.7 5.3 convolution_convert_fusion.8
  117.0 3.4 convert_element_type.186
  122.2 22.1 %reduce-scatter.7.cloned.1.call-done = bf16[3,32,2048]{2,1,0:T(8,128)(2,1)} async-done(((bf16[3,128,2048]{2,1,0:T(8,128)(2,1)}), bf16[3,32,2048]{2,1,0:T(8,128)(2,1)}) %reduce-scatter.7.cloned.1.call-update) | async-done | bytes 393232 | tf_op jit(solution)/shard_map/reduce_scatter | solution.py:425
  150.0 5.6 all-to-all-start
  156.6 3.4 multiply_convert_fusion.1
  159.9 40.1 %all-to-all-done = bf16[16,48,2048]{2,1,0:T(8,128)(2,1)} async-done(((bf16[16,48,2048]{2,1,0:T(8,128)(2,1)}), bf16[16,48,2048]{2,1,0:T(8,128)(2,1)}, u32[]{:S(2)}, u32[]{:S(2)}) %all-to-all-start) | async-done | bytes 3145760 | tf_op jit(solution)/shard_map/all_to_all | solution.py:456
  200.0 4.7 all-to-all-start.2
  204.7 7.0 fusion.11
  211.6 5.9 fusion.15
  217.6 31.3 %all-to-all-done.2 = bf16[16,48,2048]{2,1,0:T(8,128)(2,1)} async-done(((bf16[16,48,2048]{2,1,0:T(8,128)(2,1)}), bf16[16,48,2048]{2,1,0:T(8,128)(2,1)}, u32[]{:S(2)}, u32[]{:S(2)}) %all-to-all-start.2) | async-done | bytes 3145760 | tf_op jit(solution)/shard_map/all_to_all | solution.py:478
  248.9 7.7 multiply_convert_fusion.3
  262.2 18.6 %copy.252 = bf16[1,768,2048]{2,0,1:T(2,128)(2,1)} copy(bf16[1,768,2048]{2,1,0:T(8,128)(2,1)S(1)} %fusion.20) | data formatting | bytes 6291456 | tf_op jit(solution)/shard_map/convert_element_type | solution.py:489
  281.3 20.7 %reduce.10 = bf16[768,2048]{1,0:T(8,128)(2,1)} reduce(bf16[768,1,2048]{2,1,0:T(2,128)(2,1)} %bitcast.250, bf16[]{:T(256)} %broadcast.307), dimensions={1}, to_apply=%bitcast.244.reduce_sub_computation | reduce | bytes 6291458
  302.1 7.0 reshape.550
  309.1 4.5 all-to-all-start.3
  319.2 38.7 %all-to-all-done.3 = bf16[16,2,49152]{2,1,0:T(2,128)(2,1)} async-done(((bf16[16,2,49152]{2,1,0:T(2,128)(2,1)}), bf16[16,2,49152]{2,1,0:T(2,128)(2,1)}, u32[]{:S(2)}, u32[]{:S(2)}) %all-to-all-start.3) | async-done | bytes 3145760 | tf_op jit(solution)/shard_map/all_to_all | solution.py:490
  357.9 11.5 %reshape.551 = bf16[768,1,2048]{2,1,0:T(2,128)(2,1)} reshape(bf16[16,2,49152]{2,1,0:T(2,128)(2,1)} %all-to-all-done.3) | data formatting | bytes 6291456
  369.4 4.8 copy.221
  385.3 4.1 fusion.17
  389.4 18.6 %copy.253 = bf16[1,768,2048]{2,0,1:T(2,128)(2,1)} copy(bf16[1,768,2048]{2,1,0:T(8,128)(2,1)S(1)} %fusion.17) | data formatting | bytes 6291456 | tf_op jit(solution)/shard_map/convert_element_type | solution.py:466
  408.0 18.9 %reduce.11 = bf16[768,2048]{1,0:T(8,128)(2,1)S(1)} reduce(bf16[768,1,2048]{2,1,0:T(2,128)(2,1)} %bitcast.251, bf16[]{:T(256)} %broadcast.307), dimensions={1}, to_apply=%bitcast.245.reduce_sub_computation | reduce | bytes 6291458
  426.9 4.5 reshape.548
  431.5 5.0 all-to-all-start.1
  436.6 6.3 convolution_convert_fusion.4
  442.9 6.3 convolution_convert_fusion.3
  449.1 4.5 fusion.34
  453.8 7.6 fusion.36
  464.4 11.3 %fusion.82 = (f32[8]{0:T(128)}, f32[3,128,8]{1,2,0:T(8,128)S(1)}, f32[3,128,8,1024]{3,1,2,0:T(8,128)}) fusion(f32[3,128,8,1024]{3,1,2,0:T(8,128)} %copy-done.2, f32[3,128,8]{1,2,0:T(8,128)S(1)} %copy-done.46, bf16[3,1024,1,128]{1,3,0,2:T(8,128)(2,1)S(1)} %copy-done.13, bf16[3,128,8,128]{3,2,1,0:T(8,128)(2,1)S(1)} %bitcast.275), kind=kOutput, calls=%fused_computation.161 | convolution fusion | flops 817886208 | bytes 26763296 | tf_op jit(solution)/shard_map/sqhgd,skhd->shqgk/dot_general | solution.py:512
  477.0 6.3 multiply_convert_fusion
  489.1 6.2 bitcast_multiply_fusion.3
  502.3 6.0 fusion.48
  509.9 34.3 %reduce-scatter.9.cloned.1.call-done = bf16[3,128,1,128]{3,1,0,2:T(8,128)(2,1)} async-done(((bf16[3,1024,1,128]{3,1,0,2:T(8,128)(2,1)}), bf16[3,128,1,128]{3,1,0,2:T(8,128)(2,1)}) %reduce-scatter.9.cloned.1.call-update) | async-done | bytes 98320 | tf_op jit(solution)/shard_map/reduce_scatter | solution.py:529
  551.4 6.5 convolution_convert_fusion.2
  558.0 11.5 %reshape.549 = bf16[768,1,2048]{2,1,0:T(2,128)(2,1)} reshape(bf16[16,2,49152]{2,1,0:T(2,128)(2,1)} %all-to-all-done.1) | data formatting | bytes 6291456
  569.5 4.9 copy.220
  574.4 3.8 fusion.1
  578.9 62.9 %pmax.7 = f32[8]{0:T(128)S(1)} all-reduce(f32[8]{0:T(128)S(1)} %copy-done.75), channel_id=1, replica_groups=mesh['dp'=4,'context'=8,'experts'=4] {'dp','context'}, use_global_device_ids=true, to_apply=%region_32.33 | all-reduce | flops 8 | bytes 64 | tf_op jit(solution)/shard_map/pmax | solution.py:433
  642.4 4.4 convolution_convert_fusion.1
  646.8 4.4 convolution_convert_fusion
  653.6 102.8 %reduce_weights.1 = (f32[256,768]{1,0:T(8,128)}, f32[256,768]{1,0:T(8,128)}, f32[256,768]{1,0:T(8,128)}, f32[64,1024]{1,0:T(8,128)}, f32[64,256]{1,0:T(8,128)}, /*index=5*/f32[64,1024]{1,0:T(8,128)}) custom-call(bf16[4,2,256,768]{3,2,1,0:T(8,128)(2,1)} %bitcast.276, bf16[4,2,256,768]{3,2,1,0:T(8,128)(2,1)} %bitcast.277, bf16[4,2,256,768]{3,2,1,0:T(8,128)(2,1)} %bitcast.278, ...), custom_call_target="tpu_custom_call" | custom-call | tf_op jit(solution)/shard_map/reduce_weights/pallas_call | solution.py:310
  760.0 64.1 %all-reduce = (f32[2048]{0:T(1024)}, f32[128]{0:T(128)}, f32[128]{0:T(128)}, f32[2048]{0:T(1024)}) all-reduce(f32[2048]{0:T(1024)S(1)} %get-tuple-element.121, f32[128]{0:T(128)S(1)} %copy-done.74, f32[128]{0:T(128)S(1)} %copy-done.73, f32[2048]{0:T(1024)S(1)} %copy-done.65), channel_id=1, replica_groups=mesh['dp'=4,'context'=8,'experts'=4] {'dp','context','experts'}, use_global_device_ids=true, to_apply=%region_22.23 | all-reduce | flops 4352 | bytes 34816 | tf_op jit(solution)/shard_map/psum | solution.py:577
  824.1 3.6 fusion.43
  (290 shorter events, 96.4 us)
Async XLA Ops:
  7.2 241.7 %copy-start = (bf16[1,2048,768]{2,1,0:T(8,128)(2,1)S(1)}, bf16[1,2048,768]{2,1,0:T(8,128)(2,1)}, u32[]{:S(2)}) copy-start(bf16[1,2048,768]{2,1,0:T(8,128)(2,1)} %param.32) | copy-start | bytes 9437188
  7.2 137.0 %reduce-scatter.7.cloned.1.call-start = ((), (), s32[]{:S(2)}) async-start(), calls=%async_computation.8 | async-start | bytes 1966080 | tf_op jit(solution)/shard_map/reduce_scatter | solution.py:425
  7.2 5.9 copy-start.23
  8.1 5.6 copy-start.47
  8.1 5.7 copy-start.82
  13.8 42.2 %copy-start.18 = (f32[384,128]{1,0:T(8,128)}, f32[384,128]{1,0:T(8,128)S(1)}, u32[]{:S(2)}) copy-start(f32[384,128]{1,0:T(8,128)S(1)} %get-tuple-element.163) | copy-start | bytes 589828
  13.8 42.2 %copy-start.66 = (f32[128]{0:T(128)}, f32[128]{0:T(128)S(1)}, u32[]{:S(2)}) copy-start(f32[128]{0:T(128)S(1)} %convert_element_type.193) | copy-start | bytes 1540
  15.6 48.1 %copy-start.26 = (f32[128,128]{0,1:T(8,128)}, f32[128,128]{0,1:T(8,128)S(1)}, u32[]{:S(2)}) copy-start(f32[128,128]{0,1:T(8,128)S(1)} %get-tuple-element.159) | copy-start | bytes 196612
  15.6 48.1 %copy-start.27 = (f32[128,128]{0,1:T(8,128)}, f32[128,128]{0,1:T(8,128)S(1)}, u32[]{:S(2)}) copy-start(f32[128,128]{0,1:T(8,128)S(1)} %get-tuple-element.158) | copy-start | bytes 196612
  15.7 40.2 %copy-start.40 = (f32[128,128]{1,0:T(8,128)}, f32[128,128]{1,0:T(8,128)S(1)}, u32[]{:S(2)}) copy-start(f32[128,128]{1,0:T(8,128)S(1)} %copy.177) | copy-start | bytes 196612
  107.7 6.2 copy-start.77
  120.4 26.9 %copy-start.49 = (f32[2048]{0:T(1024)}, f32[2048]{0:T(1024)S(1)}, u32[]{:S(2)}) copy-start(f32[2048]{0:T(1024)S(1)} %convert_element_type.203) | copy-start | bytes 24580
  122.2 25.2 %copy-start.43 = (s32[96,16]{0,1:T(8,128)}, s32[96,16]{0,1:T(8,128)S(1)}, u32[]{:S(2)}) copy-start(s32[96,16]{0,1:T(8,128)S(1)} %get-tuple-element.139) | copy-start | bytes 18436
  122.2 25.2 %copy-start.56 = (pred[16,96]{1,0:T(8,128)(4,1)}, pred[16,96]{1,0:T(8,128)(4,1)S(1)}, u32[]{:S(2)}) copy-start(pred[16,96]{1,0:T(8,128)(4,1)S(1)} %get-tuple-element.137) | copy-start | bytes 4612
  150.0 6.5 copy-start.17
  150.0 50.0 %all-to-all-start = ((bf16[16,48,2048]{2,1,0:T(8,128)(2,1)}), bf16[16,48,2048]{2,1,0:T(8,128)(2,1)}, u32[]{:S(2)}, u32[]{:S(2)}) async-start(bf16[16,48,2048]{2,1,0:T(8,128)(2,1)} %convolution_convert_fusion.6), calls=%async_computation.1 | async-start | bytes 6291456 | tf_op jit(solution)/shard_map/all_to_all | solution.py:456
  200.0 48.9 %all-to-all-start.2 = ((bf16[16,48,2048]{2,1,0:T(8,128)(2,1)}), bf16[16,48,2048]{2,1,0:T(8,128)(2,1)}, u32[]{:S(2)}, u32[]{:S(2)}) async-start(bf16[16,48,2048]{2,1,0:T(8,128)(2,1)} %multiply_convert_fusion.1), calls=%async_computation.3 | async-start | bytes 6291456 | tf_op jit(solution)/shard_map/all_to_all | solution.py:478
  204.7 7.0 copy-start.78
  248.9 7.7 copy-start.79
  309.1 48.8 %all-to-all-start.3 = ((bf16[16,2,49152]{2,1,0:T(2,128)(2,1)}), bf16[16,2,49152]{2,1,0:T(2,128)(2,1)}, u32[]{:S(2)}, u32[]{:S(2)}) async-start(bf16[16,2,49152]{2,1,0:T(2,128)(2,1)} %reshape.550), calls=%async_computation.4 | async-start | bytes 6291456 | tf_op jit(solution)/shard_map/all_to_all | solution.py:490
  313.6 135.5 %all-gather.2.cloned.1.call-start = ((), (), s32[]{:S(2)}) async-start(), calls=%async_computation.9 | async-start | bytes 1966080 | tf_op jit(solution)/shard_map/all_gather | solution.py:503
  431.5 126.5 %all-to-all-start.1 = ((bf16[16,2,49152]{2,1,0:T(2,128)(2,1)}), bf16[16,2,49152]{2,1,0:T(2,128)(2,1)}, u32[]{:S(2)}, u32[]{:S(2)}) async-start(bf16[16,2,49152]{2,1,0:T(2,128)(2,1)} %reshape.548), calls=%async_computation.2 | async-start | bytes 6291456 | tf_op jit(solution)/shard_map/all_to_all | solution.py:467
  436.5 6.4 copy-start.87
  436.5 71.8 %reduce-scatter.13.cloned.1.call-start = ((), (), s32[]{:S(2)}) async-start(), calls=%async_computation.12 | async-start | bytes 884736
  464.1 80.1 %reduce-scatter.9.cloned.1.call-start = ((), (), s32[]{:S(2)}) async-start(), calls=%async_computation.10 | async-start | bytes 884736 | tf_op jit(solution)/shard_map/reduce_scatter | solution.py:529
  464.3 11.4 %slice-start = ((s8[12582912]{0:T(1024)(128)(4,1)}), s8[4194304]{0:T(1024)(128)(4,1)S(1)}, s32[]{:S(2)}) async-start(s8[12582912]{0:T(1024)(128)(4,1)} %bitcast.248), calls=%async_computation.13 | async-start | bytes 8388608
  464.4 11.4 %slice-start.1 = ((s8[12582912]{0:T(1024)(128)(4,1)}), s8[4194304]{0:T(1024)(128)(4,1)S(1)}, s32[]{:S(2)}) async-start(s8[12582912]{0:T(1024)(128)(4,1)} %bitcast.248), calls=%async_computation.14 | async-start | bytes 8388608
  464.4 12.6 %slice-start.2 = ((s8[12582912]{0:T(1024)(128)(4,1)}), s8[4194304]{0:T(1024)(128)(4,1)S(1)}, s32[]{:S(2)}) async-start(s8[12582912]{0:T(1024)(128)(4,1)} %bitcast.248), calls=%async_computation.15 | async-start | bytes 8388608
  477.0 9.0 %copy-start.16 = (bf16[3,128,8,128]{1,3,2,0:T(8,128)(2,1)S(1)}, bf16[3,128,8,128]{1,3,2,0:T(8,128)(2,1)}, u32[]{:S(2)}) copy-start(bf16[3,128,8,128]{1,3,2,0:T(8,128)(2,1)} %fusion.28) | copy-start | bytes 2359300
  495.3 262.4 %reduce-scatter.11.cloned.1.call-start = ((), (), s32[]{:S(2)}) async-start(), calls=%async_computation.11 | async-start | bytes 1966080 | tf_op jit(solution)/shard_map/reduce_scatter | solution.py:556
  502.2 6.1 copy-start.35
  502.2 42.0 %copy-start.42 = (f32[128,128]{1,0:T(8,128)S(1)}, f32[128,128]{1,0:T(8,128)}, u32[]{:S(2)}) copy-start(f32[128,128]{1,0:T(8,128)} %copy.178) | copy-start | bytes 196612
  502.2 43.1 %copy-start.19 = (f32[384,128]{1,0:T(8,128)S(1)}, f32[384,128]{1,0:T(8,128)}, u32[]{:S(2)}) copy-start(f32[384,128]{1,0:T(8,128)} %copy-done.18) | copy-start | bytes 589828
  502.2 43.1 %copy-start.41 = (f32[128,128]{1,0:T(8,128)S(1)}, f32[128,128]{1,0:T(8,128)}, u32[]{:S(2)}) copy-start(f32[128,128]{1,0:T(8,128)} %copy-done.40) | copy-start | bytes 196612
  502.2 43.1 %copy-start.67 = (f32[128]{0:T(128)S(1)}, f32[128]{0:T(128)}, u32[]{:S(2)}) copy-start(f32[128]{0:T(128)} %copy-done.66) | copy-start | bytes 1540
  544.2 5.4 copy-start.25
  544.2 5.4 copy-start.29
  574.4 68.0 %copy-start.8 = (bf16[3,128,2048]{2,1,0:T(8,128)(2,1)S(1)}, bf16[3,128,2048]{2,1,0:T(8,128)(2,1)}, u32[]{:S(2)}) copy-start(bf16[3,128,2048]{2,1,0:T(8,128)(2,1)} %copy-done.6) | copy-start | bytes 4718596
  574.4 68.0 %copy-start.36 = (bf16[3,128,8,128]{3,2,1,0:T(8,128)(2,1)S(1)}, bf16[3,128,8,128]{3,2,1,0:T(8,128)(2,1)}, u32[]{:S(2)}) copy-start(bf16[3,128,8,128]{3,2,1,0:T(8,128)(2,1)} %copy-done.35) | copy-start | bytes 2359300
  653.5 104.2 %copy-start.48 = (f32[2048]{0:T(1024)S(1)}, f32[2048]{0:T(1024)}, u32[]{:S(2)}) copy-start(f32[2048]{0:T(1024)} %copy-done.47) | copy-start | bytes 24580
  653.5 104.2 %copy-start.62 = (f32[3,32]{1,0:T(4,128)S(1)}, f32[3,32]{1,0:T(4,128)}, u32[]{:S(2)}) copy-start(f32[3,32]{1,0:T(4,128)} %add_rsqrt_fusion.1) | copy-start | bytes 1156
  653.5 106.4 %copy-start.65 = (f32[2048]{0:T(1024)S(1)}, f32[2048]{0:T(1024)}, u32[]{:S(2)}) copy-start(f32[2048]{0:T(1024)} %get-tuple-element.125) | copy-start | bytes 24580
  653.5 106.4 %copy-start.73 = (f32[128]{0:T(128)S(1)}, f32[128]{0:T(128)}, u32[]{:S(2)}) copy-start(f32[128]{0:T(128)} %get-tuple-element.127) | copy-start | bytes 1540
  653.5 106.4 %copy-start.74 = (f32[128]{0:T(128)S(1)}, f32[128]{0:T(128)}, u32[]{:S(2)}) copy-start(f32[128]{0:T(128)} %get-tuple-element.123) | copy-start | bytes 1540
  653.6 170.5 %copy-start.51 = (f32[2048]{0:T(1024)S(1)}, f32[2048]{0:T(1024)}, u32[]{:S(2)}) copy-start(f32[2048]{0:T(1024)} %copy-done.49) | copy-start | bytes 24580
  824.0 7.0 copy-start.39
  824.0 7.9 copy-start.38
  824.1 9.7 %copy-start.1 = (bf16[1,2048,768]{2,1,0:T(8,128)(2,1)S(1)}, bf16[1,2048,768]{2,1,0:T(8,128)(2,1)}, u32[]{:S(2)}) copy-start(bf16[1,2048,768]{2,1,0:T(8,128)(2,1)} %param.32) | copy-start | bytes 9437188
  (52 other events, 176.3 us)
Sparse Core Ops, SparseCore 0:
  117.1 27.0 reduce-scatter.6
  378.1 23.1 all-gather.1
  464.2 39.8 reduce-scatter.12
  507.0 37.0 reduce-scatter.8
  551.6 24.3 reduce-scatter.10

commit v2 on v1

--- a/solution.py
+++ b/solution.py
@@ -105,9 +105,14 @@
         self.copies.append(made)
         return made
 
+    def sent(self, made):
+        made.wait_send()
+        self.copies = [None if one is made else one for one in self.copies]
+
     def finish(self):
         for made in self.copies:
-            made.wait_send()
+            if made is not None:
+                made.wait_send()
 
 
 def greet(devices):
@@ -239,6 +244,75 @@
     )
 
 
+def all_sum(net, devices, spot, own, slots, most):
+    slots[spot] = own[...]
+    sent = [net.copy(own, slots.at[spot], device) for device in devices]
+    yield
+    for made in sent:
+        made.wait_recv()
+    count = slots.shape[0]
+    total = slots[0]
+    peak = slots[0, most:]
+    for step in range(1, count):
+        total = total + slots[step]
+        peak = jnp.maximum(peak, slots[step, most:])
+    for made in sent:
+        net.sent(made)
+    own[:most] = total[:most]
+    own[most:] = peak
+
+
+def all_small(net, me, small, working, by_core, by_x, by_z, by_y, out):
+    working[...] = small[...]
+    yield from all_sum(net, [me.at(core=1 - me.core)], me.core, working, by_core, 40)
+    yield from all_sum(net, [me.at(x=me.x_by(s)) for s in (1, 2, 3)], me.x, working, by_x, 40)
+    yield from all_sum(net, [me.at(z=me.z_by(s)) for s in (1, 2, 3)], me.z, working, by_z, 40)
+    out[40:] = working[40:]
+    yield from all_sum(net, [me.at(y=me.y_by(s)) for s in (1, 2, 3)], me.y, working, by_y, 40)
+    out[:40] = working[:40]
+
+
+def peers(me):
+    offsets = [(a, b) for a in (2, 3, 0, 1) for b in (1, 3, 2, 0) if a or b]
+    return [(a, b) + peer(me, a, b) for a, b in offsets]
+
+
+def peer(me, a, b):
+    z = me.z if a < 2 else lax.rem(me.z + 2, 4)
+    core = me.core if a % 2 == 0 else 1 - me.core
+    y = me.y_by(b)
+    return z // 2 * 2 + core, y, me.at(z=z, core=core, y=y)
+
+
+def bring_home(net, me, produced, home, table, after, out):
+    sent = []
+    for a, b, dp, y, device in peers(me):
+        sent.append(net.copy(produced.at[dp, y], home.at[me.dp, me.y], device))
+    home[me.dp, me.y] = produced[me.dp, me.y]
+    for step in range(5):
+        yield
+    for made in sent:
+        made.wait_recv()
+    gather_rows(
+        table,
+        home,
+        lambda columns, total: out.__setitem__(
+            (slice(None), columns), after[:, columns] + total
+        ),
+    )
+
+
+def gather_rows(table, home, store):
+    def body(step, carry):
+        columns = pl.ds(pl.multiple_of(step * 256, 256), 256)
+        rows = home[:, :, :, columns].reshape(768, 256)
+        total = contract_first(table[...], rows)
+        store(columns, total[:96])
+        return carry
+
+    lax.fori_loop(0, home.shape[3] // 256, body, 0)
+
+
 def in_turn(tasks):
     tasks = list(tasks)
     while tasks:
@@ -255,8 +329,8 @@
         del refs[:number]
         return taken
 
-    gate, up, down, query, key_value, out_w = take(6)
-    gate_out, up_out, down_out, query_out, key_value_out, out_w_out = take(6)
+    gate, up, down, query, key_value, out_w, small, produced, table, after = take(10)
+    gate_out, up_out, down_out, query_out, key_value_out, out_w_out, small_out, layer = take(8)
     scratch = [take(count) for count in counts]
     send, recv = take(2)
     me = Place()
@@ -266,24 +340,28 @@
             me.at(x=me.x_by(3)),
             me.at(z=me.z_by(1)),
             me.at(z=me.z_by(3)),
-            me.at(core=1 - me.core),
+            me.at(x=me.x_by(2)),
+            me.at(z=me.z_by(2)),
         ]
+        + [one[4] for one in peers(me) if one[:2] != (2, 0)]
     )
     net = Net(send, recv)
     in_turn(
         [
+            all_small(net, me, small, *scratch[6], small_out),
             dense_z_first(net, me, out_w, *scratch[5], out_w_out),
             dense_x_first(net, me, query, *scratch[3], query_out),
             dense_x_first(net, me, key_value, *scratch[4], key_value_out),
             expert_z_first(net, me, down, *scratch[2], down_out),
             expert_x_first(net, me, gate, *scratch[0], gate_out),
             expert_x_first(net, me, up, *scratch[1], up_out),
+            bring_home(net, me, produced, *scratch[7], table, after, layer),
         ]
     )
     net.finish()
 
 
-def reduce_weights(gate, up, down, query, key_value, out_w):
+def reduce_weights(gate, up, down, query, key_value, out_w, small, produced, table, after):
     low = jnp.bfloat16
     x_first = [
         pltpu.VMEM((6, 256, 768), low),
@@ -305,8 +383,12 @@
             pltpu.VMEM((6, 32, columns), low),
         ]
 
+    smalls = [pltpu.VMEM(small.shape, jnp.float32)] + [
+        pltpu.VMEM((count,) + small.shape, jnp.float32) for count in (2, 4, 4, 4)
+    ]
     groups = [x_first, x_first, z_first, dense(1024, True), dense(256, True), dense(1024, False)]
-    copies = 64
+    groups += [smalls, [pltpu.VMEM((4, 4, 48, 2048), low)]]
+    copies = 90
     return pl.pallas_call(
         functools.partial(reduce_kernel, [len(group) for group in groups]),
         out_shape=[
@@ -316,9 +398,11 @@
             jax.ShapeDtypeStruct((64, 1024), jnp.float32),
             jax.ShapeDtypeStruct((64, 256), jnp.float32),
             jax.ShapeDtypeStruct((64, 1024), jnp.float32),
+            jax.ShapeDtypeStruct(small.shape, jnp.float32),
+            jax.ShapeDtypeStruct(after.shape, jnp.float32),
         ],
-        in_specs=[VMEM] * 6,
-        out_specs=[VMEM] * 6,
+        in_specs=[VMEM] * 10,
+        out_specs=[VMEM] * 8,
         scratch_shapes=[one for group in groups for one in group]
         + [pltpu.SemaphoreType.DMA((copies,)), pltpu.SemaphoreType.DMA((copies,))],
         compiler_params=pltpu.CompilerParams(
@@ -332,7 +416,241 @@
         query.reshape(2, 2, 4, 2, 64, 1024),
         key_value.reshape(2, 2, 4, 2, 64, 256),
         out_w.reshape(2, 2, 4, 2, 64, 1024),
-    )
+        small,
+        produced,
+        table,
+        after,
+    )
+
+
+def moe_kernel(
+    after,
+    cotangent,
+    gain,
+    ids,
+    gates,
+    capacity,
+    w_gate,
+    w_up,
+    w_down,
+    after_grad,
+    gain_part,
+    gate_grad,
+    produced,
+    table,
+    full_gate,
+    full_up,
+    full_down,
+    rows,
+    sending,
+    sending_grad,
+    info,
+    info_in,
+    local,
+    grads,
+    act,
+    gate_back,
+    up_back,
+    back,
+    home,
+    dots,
+    dots_in,
+    send,
+    recv,
+):
+    low, full = jnp.bfloat16, jnp.float32
+    me = Place()
+    greet([one[4] for one in peers(me)])
+    net = Net(send, recv)
+
+    expert = lax.broadcasted_iota(jnp.int32, (16, 128), 0)
+    chosen = jnp.zeros((16, 128), full)
+    share = jnp.zeros((16, 128), full)
+    for k in range(8):
+        named = ids[k : k + 1, :] == expert
+        chosen = chosen + jnp.where(named, 1.0, 0.0)
+        share = share + jnp.where(named, gates[k : k + 1, :], 0.0)
+    earlier = lax.broadcasted_iota(jnp.int32, (128, 128), 0) < lax.broadcasted_iota(
+        jnp.int32, (128, 128), 1
+    )
+    before = jnp.dot(
+        chosen.astype(low), jnp.where(earlier, 1.0, 0.0).astype(low), preferred_element_type=full
+    )
+    slot = jnp.where((chosen > 0.0) & (before < capacity[...]), before, -1.0)
+    spot = lax.broadcasted_iota(jnp.int32, (48, 128), 0).astype(full)
+    for e in range(16):
+        mask = jnp.where(slot[e : e + 1, :] == spot, 1.0, 0.0)
+        table[e * 48 : e * 48 + 48, :] = mask.astype(low)
+        info[e // 4, e % 4] = jnp.concatenate(
+            [slot[e : e + 1, :], share[e : e + 1, :], jnp.zeros((6, 128), full)], axis=0
+        )
+
+    def dispatch(sender):
+        for a, b, dp, y, device in peers(me):
+            if b == 1:
+                rest = table[pl.ds(pl.multiple_of(dp * 192, 192), 192), :]
+                columns = 512
+                for step in range(2048 // columns):
+                    run = slice(step * columns, (step + 1) * columns)
+                    picked = jnp.dot(rest, rows[:, run], preferred_element_type=full)
+                    sender[dp, :, :, run] = picked.astype(low).reshape(4, 48, columns)
+            yield a, b, dp, y, device
+
+    told, came, grad_came = {}, {}, {}
+    for a, b, dp, y, device in peers(me):
+        told[a, b] = net.copy(info.at[dp, y], info_in.at[me.dp, me.y], device)
+    info_in[me.dp, me.y] = info[me.dp, me.y]
+    values = after[...]
+    inverse = lax.rsqrt(jnp.mean(values * values, axis=-1, keepdims=True) + epsilon)
+    rows[96:, :] = jnp.zeros((32, 2048), low)
+    rows[:96, :] = (values * inverse * gain[...]).astype(low)
+    for a, b, dp, y, device in dispatch(sending):
+        came[a, b] = net.copy(sending.at[dp, y], local.at[me.dp, me.y], device)
+    local[me.dp, me.y] = sending[me.dp, me.y]
+    rows[:96, :] = cotangent[...]
+    for a, b, dp, y, device in dispatch(sending_grad):
+        grad_came[a, b] = net.copy(sending_grad.at[dp, y], grads.at[me.dp, me.y], device)
+    grads[me.dp, me.y] = sending_grad[me.dp, me.y]
+
+    back_came, dots_came = {}, {}
+    for a in (0, 1, 2, 3):
+        group = peer(me, a, 0)[0]
+        for b in range(4):
+            if a or b:
+                told[a, b].wait_recv()
+                came[a, b].wait_recv()
+                grad_came[a, b].wait_recv()
+        masks, shares = [], []
+        for y in range(4):
+            mask = info_in[group, y, 0:1, :] == spot
+            masks.append(mask)
+            shares.append(
+                jnp.sum(jnp.where(mask, info_in[group, y, 1:2, :], 0.0), axis=1, keepdims=True)
+            )
+        shared = jnp.concatenate(shares, axis=0)
+
+        def inner(step, carry, group=group, shared=shared):
+            columns = pl.ds(pl.multiple_of(step * 256, 256), 256)
+            entered = local[group].reshape(192, 2048)
+            gate_pre = jnp.dot(entered, w_gate[:, columns], preferred_element_type=full)
+            up_pre = jnp.dot(entered, w_up[:, columns], preferred_element_type=full)
+            scaled = (grads[group].reshape(192, 2048).astype(full) * shared).astype(low)
+            act_back = jnp.dot(scaled, w_down[:, columns], preferred_element_type=full)
+            sigmoid = 1.0 / (1.0 + jnp.exp(-gate_pre))
+            silu = gate_pre * sigmoid
+            act[group, :, columns] = (silu * up_pre).astype(low)
+            gate_back[group, :, columns] = (
+                act_back * up_pre * sigmoid * (1.0 + gate_pre * (1.0 - sigmoid))
+            ).astype(low)
+            up_back[group, :, columns] = (act_back * silu).astype(low)
+            return carry
+
+        lax.fori_loop(0, 3, inner, 0)
+
+        def outer(step, dot, group=group, shared=shared):
+            columns = pl.ds(pl.multiple_of(step * 256, 256), 256)
+            made = contract_last(act[group], w_down[columns, :]).astype(low).astype(full)
+            produced[group, :, :, columns] = (made * shared).astype(low).reshape(4, 48, 256)
+            incoming = grads[group, :, :, columns].reshape(192, 256).astype(full)
+            dot = dot + jnp.sum(made * incoming, axis=1, keepdims=True)
+            grads[group, :, :, columns] = (incoming * shared).astype(low).reshape(4, 48, 256)
+            row_back = contract_last(gate_back[group], w_gate[columns, :]) + contract_last(
+                up_back[group], w_up[columns, :]
+            )
+            back[group, :, :, columns] = row_back.astype(low).reshape(4, 48, 256)
+            return dot
+
+        dot = lax.fori_loop(0, 8, outer, jnp.zeros((192, 1), full))
+        for y in range(4):
+            line = jnp.sum(
+                jnp.where(masks[y], dot[y * 48 : y * 48 + 48], 0.0), axis=0, keepdims=True
+            )
+            dots[group, y] = jnp.broadcast_to(line, (8, 128))
+        for b in (2, 1, 3, 0):
+            if a or b:
+                dp, y, device = peer(me, a, b)
+                back_came[a, b] = net.copy(back.at[dp, y], home.at[me.dp, me.y], device)
+                dots_came[a, b] = net.copy(dots.at[dp, y], dots_in.at[me.dp, me.y], device)
+    home[me.dp, me.y] = back[me.dp, me.y]
+    dots_in[me.dp, me.y] = dots[me.dp, me.y]
+
+    def weigh(step, carry):
+        columns = pl.ds(pl.multiple_of(step * 256, 256), 256)
+        entered = local[:, :, :, columns].reshape(768, 256)
+        full_gate[columns, :] = contract_first(entered, gate_back[...].reshape(768, 768)).astype(low)
+        full_up[columns, :] = contract_first(entered, up_back[...].reshape(768, 768)).astype(low)
+        incoming = grads[:, :, :, columns].reshape(768, 256)
+        full_down[columns, :] = contract_first(incoming, act[...].reshape(768, 768)).astype(low)
+        return carry
+
+    lax.fori_loop(0, 8, weigh, 0)
+
+    for a, b, *_ in peers(me):
+        back_came[a, b].wait_recv()
+        dots_came[a, b].wait_recv()
+    chosen_dots = [jnp.zeros((1, 128), full) for k in range(8)]
+    for e in range(16):
+        line = dots_in[e // 4, e % 4, 0:1, :]
+        for k in range(8):
+            chosen_dots[k] = chosen_dots[k] + jnp.where(ids[k : k + 1, :] == e, line, 0.0)
+    gate_grad[...] = jnp.concatenate(chosen_dots, axis=0)
+
+    def keep(columns, total):
+        after_grad[:, columns] = total
+
+    gather_rows(table, home, keep)
+    gradient = after_grad[...]
+    values = after[...]
+    inverse = lax.rsqrt(jnp.mean(values * values, axis=-1, keepdims=True) + epsilon)
+    normal = values * inverse
+    gain_part[...] = jnp.sum(gradient * normal, axis=0, keepdims=True)
+    scaled = gradient * gain[...]
+    mean = jnp.mean(scaled * normal, axis=-1, keepdims=True)
+    after_grad[...] = cotangent[...].astype(full) + inverse * (scaled - normal * mean)
+    net.finish()
+
+
+def moe(after, cotangent, gain, ids, gates, capacity, w_gate, w_up, w_down):
+    low, full = jnp.bfloat16, jnp.float32
+    copies = 75
+    shape = jax.ShapeDtypeStruct
+    return pl.pallas_call(
+        moe_kernel,
+        out_shape=[
+            shape((96, 2048), full),
+            shape((1, 2048), full),
+            shape((8, 128), full),
+            shape((4, 4, 48, 2048), low),
+            shape((768, 128), low),
+            shape((2048, 768), low),
+            shape((2048, 768), low),
+            shape((2048, 768), low),
+        ],
+        in_specs=[VMEM] * 9,
+        out_specs=[VMEM] * 8,
+        scratch_shapes=[
+            pltpu.VMEM((128, 2048), low),
+            pltpu.VMEM((4, 4, 48, 2048), low),
+            pltpu.VMEM((4, 4, 48, 2048), low),
+            pltpu.VMEM((4, 4, 8, 128), full),
+            pltpu.VMEM((4, 4, 8, 128), full),
+            pltpu.VMEM((4, 4, 48, 2048), low),
+            pltpu.VMEM((4, 4, 48, 2048), low),
+            pltpu.VMEM((4, 192, 768), low),
+            pltpu.VMEM((4, 192, 768), low),
+            pltpu.VMEM((4, 192, 768), low),
+            pltpu.VMEM((4, 4, 48, 2048), low),
+            pltpu.VMEM((4, 4, 48, 2048), low),
+            pltpu.VMEM((4, 4, 8, 128), full),
+            pltpu.VMEM((4, 4, 8, 128), full),
+            pltpu.SemaphoreType.DMA((copies,)),
+            pltpu.SemaphoreType.DMA((copies,)),
+        ],
+        compiler_params=pltpu.CompilerParams(
+            collective_id=1, has_side_effects=True, vmem_limit_bytes=60 << 20
+        ),
+        name="moe",
+    )(after, cotangent, gain, ids, gates, capacity, w_gate, w_up, w_down)
 
 
 def shards(
@@ -430,76 +748,25 @@
     ).astype(jnp.float32)
     own_inputs = lax.dynamic_slice_in_dim(inputs, own_index * own_rows, own_rows, 1)
     after_attn = own_inputs + branch
-    peak_all = lax.pmax(head_peak, ("dp", "context"))
-    head_clip_scale = clip_limit / jnp.maximum(peak_all, clip_limit)
-    moe_in = rms_scale(after_attn, gain_moe).astype(jnp.bfloat16)
     pair_tokens = seqs_local * own_rows
-    expert_total = capacity.shape[0]
     top_count = expert_ids.shape[2]
-    slot_count = pair_tokens * top_count // expert_total
-    moe_rows = moe_in.reshape(pair_tokens, model_width)
-    routes = expert_ids.reshape(pair_tokens, top_count)
-    choose = (
-        routes[:, :, None] == jnp.arange(expert_total, dtype=jnp.int32)[None, None, :]
-    ).astype(jnp.float32)
-    chosen = jnp.sum(choose, axis=1).astype(jnp.int32)
-    before = jnp.cumsum(chosen, axis=0) - chosen
-    kept = (chosen > 0) & (before < capacity[None, :])
-    share = jnp.sum(gate_values.reshape(pair_tokens, top_count)[:, :, None] * choose, axis=1)
-    table_mask = kept.T[:, None, :] & (
-        before.T[:, None, :] == jnp.arange(slot_count, dtype=jnp.int32)[None, :, None]
-    )
-    table = table_mask.astype(jnp.bfloat16)
-    send_rows = jnp.einsum(
-        "ecn,nd->ecd", table, moe_rows, preferred_element_type=jnp.float32
-    ).astype(jnp.bfloat16)
-    local_rows = lax.all_to_all(
-        send_rows, ("dp", "experts"), split_axis=0, concat_axis=1, tiled=True
-    )
-    gate_pre = jnp.einsum("erd,edf->erf", local_rows, w_gate, preferred_element_type=jnp.float32)
-    up_pre = jnp.einsum("erd,edf->erf", local_rows, w_up, preferred_element_type=jnp.float32)
-    sigmoid_gate = jax.nn.sigmoid(gate_pre)
-    silu_gate = gate_pre * sigmoid_gate
-    activation = (silu_gate * up_pre).astype(jnp.bfloat16)
-    produced = jnp.einsum(
-        "erf,edf->erd", activation, w_down, preferred_element_type=jnp.float32
-    ).astype(jnp.bfloat16)
-    returned = lax.all_to_all(produced, ("dp", "experts"), split_axis=1, concat_axis=0, tiled=True)
-    per_expert = jnp.einsum("ecn,ecd->ned", table, returned, preferred_element_type=jnp.float32)
-    moe_out = jnp.sum(share[:, :, None] * per_expert, axis=1)
-    layer_out = after_attn + moe_out.reshape(seqs_local, own_rows, model_width)
-    out_grad = cotangent.astype(jnp.float32)
-    cot_rows = cotangent.reshape(pair_tokens, model_width)
-    dots = jnp.sum(per_expert * out_grad.reshape(pair_tokens, 1, model_width), axis=2)
-    gate_grad = jnp.sum(choose * dots[:, None, :], axis=2).reshape(seqs_local, own_rows, top_count)
-    slot_share = jnp.sum(table.astype(jnp.float32) * share.T[:, None, :], axis=2)
-    slot_rows = jnp.einsum("ecn,nd->ecd", table, cot_rows, preferred_element_type=jnp.float32)
-    grad_send = (slot_rows * slot_share[:, :, None]).astype(jnp.bfloat16)
-    grad_rows = lax.all_to_all(
-        grad_send, ("dp", "experts"), split_axis=0, concat_axis=1, tiled=True
-    )
-    act_back = jnp.einsum("erd,edf->erf", grad_rows, w_down, preferred_element_type=jnp.float32)
-    gate_back = (act_back * up_pre * sigmoid_gate * (1.0 + gate_pre * (1.0 - sigmoid_gate))).astype(
-        jnp.bfloat16
-    )
-    up_back = (act_back * silu_gate).astype(jnp.bfloat16)
-    row_back = jnp.einsum("erf,edf->erd", gate_back, w_gate, preferred_element_type=jnp.float32)
-    row_back = (
-        row_back + jnp.einsum("erf,edf->erd", up_back, w_up, preferred_element_type=jnp.float32)
-    ).astype(jnp.bfloat16)
-    back_rows = lax.all_to_all(row_back, ("dp", "experts"), split_axis=1, concat_axis=0, tiled=True)
-    moe_in_grad = jnp.einsum(
-        "ecn,ecd->nd", table, back_rows, preferred_element_type=jnp.float32
-    ).reshape(seqs_local, own_rows, model_width)
-    full_gate = jnp.einsum(
-        "erd,erf->edf", local_rows, gate_back, preferred_element_type=jnp.float32
-    )
-    full_up = jnp.einsum("erd,erf->edf", local_rows, up_back, preferred_element_type=jnp.float32)
-    full_down = jnp.einsum(
-        "erd,erf->edf", grad_rows, activation, preferred_element_type=jnp.float32
-    )
-    moe_part, moe_gain_part = rms_back(moe_in_grad, after_attn, gain_moe)
-    after_grad = out_grad + moe_part
+    token_lanes = ((0, 0), (0, 128 - pair_tokens))
+    ids = jnp.pad(expert_ids.reshape(pair_tokens, top_count).T, token_lanes, constant_values=-1)
+    gates = jnp.pad(gate_values.reshape(pair_tokens, top_count).T, token_lanes)
+    after_flat = after_attn.reshape(pair_tokens, model_width)
+    after_grad, moe_gain_part, gate_grad, produced, table, full_gate, full_up, full_down = moe(
+        after_flat,
+        cotangent.reshape(pair_tokens, model_width),
+        gain_moe[None],
+        ids,
+        gates,
+        jnp.broadcast_to(capacity.astype(jnp.float32)[:, None], (capacity.shape[0], 128)),
+        w_gate[0],
+        w_up[0],
+        w_down[0],
+    )
+    after_grad = after_grad.reshape(seqs_local, own_rows, model_width)
+    gate_grad = gate_grad[:, :pair_tokens].T.reshape(seqs_local, own_rows, top_count)
     branch_grad = lax.all_gather(after_grad.astype(jnp.bfloat16), "experts", axis=1, tiled=True)
     branch_flat = branch_grad.reshape(token_count, model_width)
     heads_grad = jnp.dot(branch_flat, w_out, preferred_element_type=jnp.float32).astype(
@@ -562,22 +829,45 @@
     input_part, attn_gain_part = rms_back(own_normed_grad, own_inputs, gain_attn)
     input_grad = after_grad + input_part
     key_value_part = jnp.concatenate([w_key_part, w_value_part], axis=1)
-    w_gate_grad, w_up_grad, w_down_grad, w_query_grad, w_key_value_grad, w_out_grad = (
-        reduce_weights(
-            full_gate.astype(jnp.bfloat16),
-            full_up.astype(jnp.bfloat16),
-            full_down.astype(jnp.bfloat16),
-            w_query_part.astype(jnp.bfloat16),
-            key_value_part.astype(jnp.bfloat16),
-            w_out_part.astype(jnp.bfloat16),
-        )
-    )
+    small = jnp.concatenate(
+        [
+            attn_gain_part.reshape(16, 128),
+            moe_gain_part.reshape(16, 128),
+            query_gain_part[None],
+            key_gain_part[None],
+            jnp.zeros((6, 128), jnp.float32),
+            jnp.broadcast_to(head_peak[:, None], (head_count, 128)),
+        ],
+        axis=0,
+    )
+    (
+        w_gate_grad,
+        w_up_grad,
+        w_down_grad,
+        w_query_grad,
+        w_key_value_grad,
+        w_out_grad,
+        small,
+        layer_out,
+    ) = reduce_weights(
+        full_gate,
+        full_up,
+        full_down,
+        w_query_part.astype(jnp.bfloat16),
+        key_value_part.astype(jnp.bfloat16),
+        w_out_part.astype(jnp.bfloat16),
+        small,
+        produced,
+        table,
+        after_flat,
+    )
+    layer_out = layer_out.reshape(seqs_local, own_rows, model_width)
     w_key_grad, w_value_grad = w_key_value_grad[:, :128], w_key_value_grad[:, 128:]
     w_gate_grad, w_up_grad, w_down_grad = w_gate_grad[None], w_up_grad[None], w_down_grad[None]
-    attn_gain_grad, query_gain_grad, key_gain_grad, moe_gain_grad = lax.psum(
-        (attn_gain_part, query_gain_part, key_gain_part, moe_gain_part),
-        ("dp", "context", "experts"),
-    )
+    attn_gain_grad = small[:16].reshape(model_width)
+    moe_gain_grad = small[16:32].reshape(model_width)
+    query_gain_grad, key_gain_grad = small[32], small[33]
+    head_clip_scale = clip_limit / jnp.maximum(small[40:, 0], clip_limit)
     return (
         layer_out,
         input_grad,

time: 850 us -> 597 us (0.70)
  Pallas kernels: 103 us -> 279 us
  blocking collectives: 186 us -> 58.6 us
  local copies, waits for them, and re-layouts: 127 us -> 43 us
  waiting for transfers between devices: 167 us -> 90 us
  matrix products: 132 us -> 64.6 us
  other arithmetic: 91.8 us -> 42.8 us
  starting transfers between devices: 20.3 us -> 0.78 us
    pallas_call x0 -> x1, Pallas kernels: none -> 151 us  [moe(): pl.pallas_call(moe_kernel, out_shape=[shape((96, 2048), full), shape((1,...]
    all_to_all x4 -> x0, waiting for transfers between devices: 110 us -> none  [the longest x1 40.1 us: shards(): lax.all_to_all(send_rows, ('dp', 'experts'), split_axis=0, concat_axis=1,...]
    psum x1 -> x0, blocking collectives: 64.1 us -> none  [shards(): lax.psum((attn_gain_part, query_gain_part, key_gain_part, moe_gain_part),...]
    pmax x1 -> x0, blocking collectives: 62.9 us -> none  [shards(): peak_all = lax.pmax(head_peak, ('dp', 'context'))]
    dot_general x13 -> x0, matrix products: 60.9 us -> none  [the longest x1 7.7 us: shards(): jnp.einsum('erd,edf->erf', grad_rows, w_down, preferred_element_type=jnp....]
    unnamed x201 -> x137, local copies, waits for them, and re-layouts: 68.3 us -> 23.5 us
    unnamed x3 -> x2, other arithmetic: 39.6 us -> 0.01 us
    convert_element_type x3 -> x0, local copies, waits for them, and re-layouts: 37.3 us -> none  [the longest x1 18.6 us: shards(): row_back = (row_back + jnp.einsum('erf,edf->erd', up_back, w_up, preferre...]
  transfers between devices with their start and end apart: 9 -> 5, of which waited for: 5 -> 4; matrix products, arithmetic and copies ran while one was open for 23% -> 10% of each run, Pallas kernels for 12% -> 0%
where the time goes in v2:
time: 597 us; the launch traced here: 594 us
  Pallas kernels  279 us (47%)
  waiting for transfers between devices  90 us (15%)
  matrix products  64.6 us (11%)
  blocking collectives  58.6 us (10%)
  local copies, waits for them, and re-layouts  43 us (7%)
  other arithmetic  42.8 us (7%)
  between operations  14.8 us (2%)
    pallas_call x1, Pallas kernels, moe(): pl.pallas_call(moe_kernel, out_shape=[shape((96, 2048), full), shape((1,...  151 us
    pallas_call x1, Pallas kernels, reduce_weights(): pl.pallas_call(functools.partial(reduce_kernel, [len(group) for group in...  128 us
    reduce_scatter x1, waiting for transfers between devices, shards(): lax.psum_scatter(key_part.astype(jnp.bfloat16), 'context', scatter_dimens...  35.5 us
    all_gather x1, blocking collectives, shards(): lax.all_gather(key_rot, 'context', axis=1, tiled=True)  31.8 us
    all_gather x1, blocking collectives, shards(): lax.all_gather(value_reduced, 'context', axis=1, tiled=True)  26.8 us
    all_gather x1, waiting for transfers between devices, shards(): lax.all_gather(after_grad.astype(jnp.bfloat16), 'experts', axis=1, tiled=...  25.9 us
    unnamed x137, local copies, waits for them, and re-layouts  23.5 us
    reduce_scatter x1, waiting for transfers between devices, shards(): lax.psum_scatter(branch_part.reshape(seqs_local, rows_ctx, model_width).a...  21.5 us
  transfers between devices with their start and end apart: 5, of which 4 were waited for; matrix products, arithmetic and copies ran while one was open for 10% of the time, Pallas kernels for 0%

profile of v2, /device:TPU:0, one launch (start us, length us, event | category | flops | bytes accessed | tf_op | source)
XLA Modules:
  0.0 593.6 jit_solution(14202993433759238302)
XLA Ops:
  7.3 1.2 convert_element_type.125
  9.2 1.8 multiply_reduce_fusion.1
  13.0 1.8 multiply_convert_fusion.1
  17.0 31.8 %all_gather.10 = bf16[3,1024,1,128]{3,1,0,2:T(8,128)(2,1)} all-gather(bf16[3,128,1,128]{3,1,0,2:T(8,128)(2,1)S(1)} %fusion.41), channel_id=1, replica_groups=mesh['dp'=4,'context'=8,'experts'=4] {'context'}, dimensions={1}, use_global_device_ids=true | all-gather | bytes 884736 | tf_op jit(solution)/shard_map/all_gather | solution.py:712
  48.8 26.8 %all_gather.9 = bf16[3,1024,1,128]{1,3,0,2:T(8,128)(2,1)S(1)} all-gather(bf16[3,128,1,128]{1,3,0,2:T(8,128)(2,1)S(1)} %copy.65), channel_id=1, replica_groups=mesh['dp'=4,'context'=8,'experts'=4] {'context'}, dimensions={1}, use_global_device_ids=true | all-gather | bytes 884736 | tf_op jit(solution)/shard_map/all_gather | solution.py:713
  75.6 6.5 %copy.94 = bf16[1024,2048]{1,0:T(8,128)(2,1)} copy(bf16[1024,2048]{0,1:T(8,128)(2,1)} %bitcast.211) | data formatting | bytes 8388608 | tf_op jit(solution)/shard_map/dot_general | solution.py:693
  82.1 4.7 multiply_reduce_fusion.4
  87.1 1.3 slice_negate_fusion.1
  90.2 1.9 fusion.9
  92.1 3.0 fusion.51
  95.1 2.8 exponential_reduce_fusion
  98.0 1.7 copy-done.1
  100.3 1.9 fusion
  102.2 2.3 convolution_convert_fusion.3
  106.9 3.0 fusion.5
  111.3 2.0 convert_element_type.121
  115.3 21.5 %reduce-scatter.7.cloned.1.call-done = bf16[3,32,2048]{2,1,0:T(8,128)(2,1)} async-done(((bf16[3,128,2048]{2,1,0:T(8,128)(2,1)}), bf16[3,32,2048]{2,1,0:T(8,128)(2,1)}) %reduce-scatter.7.cloned.1.call-update) | async-done | bytes 393232 | tf_op jit(solution)/shard_map/reduce_scatter | solution.py:743
  136.8 2.8 multiply_reduce_fusion.5
  140.3 151.4 %moe.1 = (f32[96,2048]{1,0:T(8,128)}, f32[1,2048]{1,0:T(1,128)}, f32[8,128]{1,0:T(8,128)}, bf16[4,4,48,2048]{3,2,1,0:T(8,128)(2,1)}, bf16[768,128]{1,0:T(8,128)(...) custom-call(f32[96,2048]{1,0:T(8,128)} %bitcast.201, ...), custom_call_target="tpu_custom_call" | custom-call | tf_op jit(solution)/shard_map/moe/pallas_call | solution.py:617
  291.7 2.1 convert_element_type.137
  293.9 25.9 %all-gather.2.cloned.1.call-done = bf16[3,128,2048]{2,1,0:T(8,128)(2,1)} async-done(((bf16[3,32,2048]{2,1,0:T(8,128)(2,1)}), bf16[3,128,2048]{2,1,0:T(8,128)(2,1)}) %all-gather.2.cloned.1.call-update) | async-done | bytes 1572880 | tf_op jit(solution)/shard_map/all_gather | solution.py:770
  319.8 4.6 fusion.15
  325.5 4.9 fusion.17
  330.4 1.7 copy.100
  333.5 11.3 %fusion.46 = (f32[8]{0:T(128)}, f32[3,128,8]{1,2,0:T(8,128)S(1)}, f32[3,128,8,1024]{3,1,2,0:T(8,128)}) fusion(f32[3,128,8,1024]{3,1,2,0:T(8,128)} %copy-done.1, f32[3,128,8]{1,2,0:T(8,128)S(1)} %copy-done.40, bf16[3,1024,1,128]{1,3,0,2:T(8,128)(2,1)S(1)} %all_gather.9, bf16[3,128,8,128]{3,2,1,0:T(8,128)(2,1)S(1)} %bitcast.216), kind=kOutput, calls=%fused_computation.106 | convolution fusion | flops 817886208 | bytes 26763296 | tf_op jit(solution)/shard_map/sqhgd,skhd->shqgk/dot_general | solution.py:779
  344.8 1.3 slice-done.2
  346.1 6.3 %multiply_convert_fusion = bf16[3,128,8,1024]{3,1,2,0:T(8,128)(2,1)S(1)} fusion(f32[3,128,8,1024]{3,1,2,0:T(8,128)} %get-tuple-element.126, f32[3,128,8,1024]{3,1,2,0:T(8,128)S(1)} %bitcast.192, f32[3,128,8]{1,2,0:T(8,128)S(1)} %get-tuple-element.93, f32[3,128,8]{1,2,0:T(8,128)S(1)} %copy-done.40), kind=kLoop, calls=%fused_computation | loop fusion | flops 12582912 | bytes 31481856 | tf_op jit(solution)/shard_map/convert_element_type | solution.py:783
  352.4 2.7 copy-done.2
  355.1 3.2 fusion.16
  358.3 6.7 %bitcast_multiply_fusion.1 = (f32[3,128,8,128]{1,3,2,0:T(8,128)}, f32[3,128,128,8]{2,1,3,0:T(8,128)}) fusion(f32[128,128]{0,1:T(8,128)S(1)} %get-tuple-element.115, bf16[3,128,8,1024]{3,1,2,0:T(8,128)(2,1)} %copy-done.2, bf16[3,1024,1,128]{3,1,0,2:T(8,128)(2,1)S(1)} %copy-done.11), kind=kOutput, calls=%fused_computation.25 | convolution fusion | flops 806092800 | bytes 10289152 | tf_op jit(solution)/shard_map/shqgk,skhd->sqhgd/dot_general | solution.py:785
  365.1 1.7 fusion.48
  369.4 6.0 %fusion.28 = f32[384,2048]{1,0:T(8,128)} fusion(bf16[2048,1024]{1,0:T(8,128)(2,1)} %param.22, bf16[48,8,8,128]{3,2,1,0:T(8,128)(2,1)S(1)} %bitcast.230), kind=kOutput, calls=%fused_computation.54 | convolution fusion | flops 1610612736 | bytes 8126464 | tf_op jit(solution)/shard_map/dot_general | solution.py:53
  376.4 35.5 %reduce-scatter.9.cloned.1.call-done = bf16[3,128,1,128]{3,1,0,2:T(8,128)(2,1)} async-done(((bf16[3,1024,1,128]{3,1,0,2:T(8,128)(2,1)}), bf16[3,128,1,128]{3,1,0,2:T(8,128)(2,1)}) %reduce-scatter.9.cloned.1.call-update) | async-done | bytes 98320 | tf_op jit(solution)/shard_map/reduce_scatter | solution.py:796
  416.2 1.8 add_convert_fusion
  418.0 1.4 copy-done.7
  419.4 1.8 copy.77
  421.2 1.3 copy.81
  423.2 5.6 convolution_convert_fusion.1
  428.8 4.4 convolution_convert_fusion
  435.6 6.9 %reduce-scatter.11.cloned.1.call-done = bf16[3,32,2048]{2,1,0:T(8,128)(2,1)} async-done(((bf16[3,128,2048]{2,1,0:T(8,128)(2,1)}), bf16[3,32,2048]{2,1,0:T(8,128)(2,1)}) %reduce-scatter.11.cloned.1.call-update) | async-done | bytes 393232 | tf_op jit(solution)/shard_map/reduce_scatter | solution.py:823
  442.5 1.6 fusion.22
  444.1 2.4 concatenate.41.refs_6_
  446.5 127.6 %reduce_weights.1 = (f32[256,768]{1,0:T(8,128)}, f32[256,768]{1,0:T(8,128)}, f32[256,768]{1,0:T(8,128)}, f32[64,1024]{1,0:T(8,128)}, f32[64,256]{1,0:T(8,128)}, ...) custom-call(bf16[4,2,256,768]{3,2,1,0:T(8,128)(2,1)} %bitcast.217, bf16[4,2,256,768]{3,2,1,0:T(8,128)(2,1)} %bitcast.218, ...), custom_call_target="tpu_custom_call" | custom-call | tf_op jit(solution)/shard_map/reduce_weights/pallas_call | solution.py:392
  574.2 1.4 divide_reduce_fusion
  575.5 1.3 slice_bitcast_fusion.3
  576.8 1.3 slice_bitcast_fusion
  578.1 1.4 fusion.50
  579.6 2.4 fusion.24
  (194 shorter events, 32.0 us)
Async XLA Ops:
  7.2 8.4 %copy-start = (bf16[2048,128]{1,0:T(8,128)(2,1)S(1)}, bf16[2048,128]{1,0:T(8,128)(2,1)}, u32[]{:S(2)}) copy-start(bf16[2048,128]{1,0:T(8,128)(2,1)} %param.23) | copy-start | bytes 1572868
  7.2 129.6 %reduce-scatter.7.cloned.1.call-start = ((), (), s32[]{:S(2)}) async-start(), calls=%async_computation.4 | async-start | bytes 1966080 | tf_op jit(solution)/shard_map/reduce_scatter | solution.py:743
  9.2 7.4 %copy-start.47 = (f32[128]{0:T(128)}, f32[128]{0:T(128)S(1)}, u32[]{:S(2)}) copy-start(f32[128]{0:T(128)S(1)} %convert_element_type.128) | copy-start | bytes 1540
  10.9 4.0 copy-start.23
  11.7 3.2 copy-start.41
  12.1 4.4 copy-start.32
  12.2 4.3 copy-start.34
  82.1 4.7 copy-start.49
  86.8 3.4 copy-start.4
  92.1 3.0 copy-start.13
  95.1 4.5 copy-start.1
  102.1 3.2 copy-start.3
  102.1 4.7 copy-start.54
  109.9 209.9 %all-gather.2.cloned.1.call-start = ((), (), s32[]{:S(2)}) async-start(), calls=%async_computation.5 | async-start | bytes 1966080 | tf_op jit(solution)/shard_map/all_gather | solution.py:770
  291.7 33.8 %slice-start.3 = ((s8[6291456]{0:T(1024)(128)(4,1)}), s8[2097152]{0:T(1024)(128)(4,1)S(1)}, s32[]{:S(2)}) async-start(s8[6291456]{0:T(1024)(128)(4,1)} %bitcast.193), calls=%async_computation.12 | async-start | bytes 4194304
  293.8 81.6 %reduce-scatter.13.cloned.1.call-start = ((), (), s32[]{:S(2)}) async-start(), calls=%async_computation.8 | async-start | bytes 884736
  319.8 5.7 slice-start.4
  330.4 3.0 copy-start.20
  330.4 3.0 copy-start.40
  333.2 78.7 %reduce-scatter.9.cloned.1.call-start = ((), (), s32[]{:S(2)}) async-start(), calls=%async_computation.6 | async-start | bytes 884736 | tf_op jit(solution)/shard_map/reduce_scatter | solution.py:796
  333.4 11.4 %slice-start = ((s8[12582912]{0:T(1024)(128)(4,1)}), s8[4194304]{0:T(1024)(128)(4,1)S(1)}, s32[]{:S(2)}) async-start(s8[12582912]{0:T(1024)(128)(4,1)} %bitcast.191), calls=%async_computation.9 | async-start | bytes 8388608
  333.4 11.4 %slice-start.1 = ((s8[12582912]{0:T(1024)(128)(4,1)}), s8[4194304]{0:T(1024)(128)(4,1)S(1)}, s32[]{:S(2)}) async-start(s8[12582912]{0:T(1024)(128)(4,1)} %bitcast.191), calls=%async_computation.10 | async-start | bytes 8388608
  333.5 12.6 %slice-start.2 = ((s8[12582912]{0:T(1024)(128)(4,1)}), s8[4194304]{0:T(1024)(128)(4,1)S(1)}, s32[]{:S(2)}) async-start(s8[12582912]{0:T(1024)(128)(4,1)} %bitcast.191), calls=%async_computation.11 | async-start | bytes 8388608
  346.1 9.0 %copy-start.14 = (bf16[3,128,8,128]{1,3,2,0:T(8,128)(2,1)S(1)}, bf16[3,128,8,128]{1,3,2,0:T(8,128)(2,1)}, u32[]{:S(2)}) copy-start(bf16[3,128,8,128]{1,3,2,0:T(8,128)(2,1)} %copy-done.13) | copy-start | bytes 2359300
  355.1 3.2 copy-start.11
  365.1 77.4 %reduce-scatter.11.cloned.1.call-start = ((), (), s32[]{:S(2)}) async-start(), calls=%async_computation.7 | async-start | bytes 1966080 | tf_op jit(solution)/shard_map/reduce_scatter | solution.py:823
  369.3 6.1 %copy-start.26 = (bf16[3,128,8,128]{3,2,1,0:T(8,128)(2,1)}, bf16[3,128,8,128]{3,2,1,0:T(8,128)(2,1)S(1)}, u32[]{:S(2)}) copy-start(bf16[3,128,8,128]{3,2,1,0:T(8,128)(2,1)S(1)} %copy.76) | copy-start | bytes 2359300
  369.3 42.6 %copy-start.35 = (f32[128,128]{1,0:T(8,128)S(1)}, f32[128,128]{1,0:T(8,128)}, u32[]{:S(2)}) copy-start(f32[128,128]{1,0:T(8,128)} %copy-done.34) | copy-start | bytes 196612
  369.3 43.6 %copy-start.16 = (f32[384,128]{1,0:T(8,128)S(1)}, f32[384,128]{1,0:T(8,128)}, u32[]{:S(2)}) copy-start(f32[384,128]{1,0:T(8,128)} %copy-done.15) | copy-start | bytes 589828
  369.4 43.6 %copy-start.33 = (f32[128,128]{1,0:T(8,128)S(1)}, f32[128,128]{1,0:T(8,128)}, u32[]{:S(2)}) copy-start(f32[128,128]{1,0:T(8,128)} %copy-done.32) | copy-start | bytes 196612
  369.4 43.6 %copy-start.48 = (f32[128]{0:T(128)S(1)}, f32[128]{0:T(128)}, u32[]{:S(2)}) copy-start(f32[128]{0:T(128)} %copy-done.47) | copy-start | bytes 1540
  418.0 3.2 copy-start.18
  419.4 3.1 copy-start.52
  419.4 3.8 copy-start.45
  423.1 5.7 copy-start.31
  423.1 5.7 copy-start.55
  428.8 4.4 copy-start.8
  433.8 8.7 %copy-start.42 = (f32[2048]{0:T(1024)S(1)}, f32[2048]{0:T(1024)}, u32[]{:S(2)}) copy-start(f32[2048]{0:T(1024)} %copy-done.41) | copy-start | bytes 24580
  434.4 9.7 %copy-start.53 = (f32[8]{0:T(128)S(1)}, f32[8]{0:T(128)}, u32[]{:S(2)}) copy-start(f32[8]{0:T(128)} %get-tuple-element.92) | copy-start | bytes 100
  434.4 9.7 %copy-start.46 = (f32[1,2048]{1,0:T(1,128)S(1)}, f32[1,2048]{1,0:T(1,128)}, u32[]{:S(2)}) copy-start(f32[1,2048]{1,0:T(1,128)} %get-tuple-element.35) | copy-start | bytes 24580
  446.5 133.0 %copy-start.22 = (f32[96,2048]{1,0:T(8,128)S(1)}, f32[96,2048]{1,0:T(8,128)}, u32[]{:S(2)}) copy-start(f32[96,2048]{1,0:T(8,128)} %get-tuple-element.34) | copy-start | bytes 2359300
  446.5 133.0 %copy-start.25 = (bf16[3,32,2048]{2,1,0:T(8,128)(2,1)S(1)}, bf16[3,32,2048]{2,1,0:T(8,128)(2,1)}, u32[]{:S(2)}) copy-start(bf16[3,32,2048]{2,1,0:T(8,128)(2,1)} %reduce-scatter.11.cloned.1.call-done) | copy-start | bytes 1179652
  574.1 7.8 %copy-start.30 = (f32[96,2048]{1,0:T(8,128)S(1)}, f32[96,2048]{1,0:T(8,128)}, u32[]{:S(2)}) copy-start(f32[96,2048]{1,0:T(8,128)} %get-tuple-element.38) | copy-start | bytes 2359300
  579.5 3.3 copy-start.38
  579.5 4.0 copy-start.37
  579.6 4.7 copy-start.29
  581.9 3.2 copy-start.28
  582.8 3.2 copy-start.27
  (19 other events, 33.2 us)
Sparse Core Ops, SparseCore 0:
  110.0 26.7 reduce-scatter.6
  293.9 25.8 all-gather.1
  333.3 38.5 reduce-scatter.12
  374.9 37.0 reduce-scatter.8
  418.1 24.3 reduce-scatter.10

commit v3 on v2

--- a/solution.py
+++ b/solution.py
@@ -1,5 +1,6 @@
 import functools
 import itertools
+import types
 
 import jax
 import jax.numpy as jnp
@@ -11,6 +12,7 @@
 HEAD_SIZE = 128
 MESH = pl.DeviceIdType.MESH
 VMEM = pl.BlockSpec(memory_space=pltpu.VMEM)
+ANY = pl.BlockSpec(memory_space=pl.ANY)
 
 
 epsilon = 1e-06
@@ -23,22 +25,9 @@
     return values * lax.rsqrt(jnp.mean(values * values, axis=-1, keepdims=True) + epsilon) * factor
 
 
-def rms_back(gradient, values, factor):
-    inverse = lax.rsqrt(jnp.mean(values * values, axis=-1, keepdims=True) + epsilon)
-    normal = values * inverse
-    scaled = gradient * factor
-    result = inverse * (scaled - normal * jnp.mean(scaled * normal, axis=-1, keepdims=True))
-    return (result, jnp.sum(gradient * normal, axis=tuple(range(values.ndim - 1))))
-
-
 def turn(values):
     middle = values.shape[-1] // 2
     return jnp.concatenate([-values[..., middle:], values[..., :middle]], axis=-1)
-
-
-def turn_back(values):
-    middle = values.shape[-1] // 2
-    return jnp.concatenate([values[..., middle:], -values[..., :middle]], axis=-1)
 
 
 def rotary(offset, amount):
@@ -88,8 +77,9 @@
 
 
 class Net:
-    def __init__(self, send, recv):
+    def __init__(self, send, recv, here=None):
         self.send, self.recv, self.copies = send, recv, []
+        self.here, self.loads = here, 0
 
     def copy(self, src, dst, device):
         spot = len(self.copies)
@@ -105,6 +95,12 @@
         self.copies.append(made)
         return made
 
+    def load(self, src, dst):
+        made = pltpu.make_async_copy(src, dst, self.here.at[self.loads])
+        self.loads += 1
+        made.start()
+        return made
+
     def sent(self, made):
         made.wait_send()
         self.copies = [None if one is made else one for one in self.copies]
@@ -138,28 +134,40 @@
         lax.fori_loop(0, rows // block, body, 0)
 
 
-def ring_reduce(net, plus, minus, own, slots, target):
+def ring_reduce(net, plus, minus, own, slots, target, held=None):
+    held = own if held is None else held
     first_plus = net.copy(own(2, 0), slots.at[0], plus)
     first_minus = net.copy(own(2, 1), slots.at[2], minus)
     side_plus = net.copy(own(1, 1), slots.at[1], plus)
     side_minus = net.copy(own(3, 0), slots.at[3], minus)
     yield
     first_plus.wait_recv()
-    add_into(slots.at[0], [slots.at[0], own(1, 0)])
+    add_into(slots.at[0], [slots.at[0], held(1, 0)])
     last_plus = net.copy(slots.at[0], slots.at[4], plus)
     first_minus.wait_recv()
-    add_into(slots.at[2], [slots.at[2], own(3, 1)])
+    add_into(slots.at[2], [slots.at[2], held(3, 1)])
     last_minus = net.copy(slots.at[2], slots.at[5], minus)
     yield
     side_minus.wait_recv()
     last_plus.wait_recv()
-    add_into(target(0), [own(0, 0), slots.at[3], slots.at[4]])
+    add_into(target(0), [held(0, 0), slots.at[3], slots.at[4]])
     side_plus.wait_recv()
     last_minus.wait_recv()
-    add_into(target(1), [own(0, 1), slots.at[1], slots.at[5]])
-
-
-def expert_x_first(net, me, source, slots, middle, other, out):
+    add_into(target(1), [held(0, 1), slots.at[1], slots.at[5]])
+
+
+def x_first(net, me, source, slots, middle, other, out, held=None):
+    staged = None
+    if held is not None:
+        order = {(1, 0): 0, (3, 1): 1, (0, 0): 2, (0, 1): 3}
+        loads = [
+            net.load(source.at[me.x_by(step), half], held.at[spot])
+            for (step, half), spot in order.items()
+        ]
+
+        def staged(step, half):
+            return held.at[order[step, half]]
+
     ring = ring_reduce(
         net,
         me.at(x=me.x_by(1)),
@@ -167,7 +175,13 @@
         lambda step, half: source.at[me.x_by(step), half],
         slots,
         lambda half: middle.at[half],
-    )
+        staged,
+    )
+    next(ring)
+    yield
+    if held is not None:
+        for load in loads:
+            load.wait()
     yield from ring
     across = net.copy(middle.at[1 - me.z_lo], other, me.at(z=me.z + 1 - 2 * me.z_lo))
     yield
@@ -175,11 +189,13 @@
     add_into(out, [middle.at[me.z_lo], other])
 
 
-def expert_z_first(net, me, source, other, middle, slots, out):
+def z_first(net, me, source, other, middle, slots, out):
     across = net.copy(source.at[:, 1 - me.z_lo], other, me.at(z=me.z + 1 - 2 * me.z_lo))
+    load = net.load(source.at[:, me.z_lo], middle)
     yield
+    load.wait()
     across.wait_recv()
-    add_into(middle, [source.at[:, me.z_lo], other])
+    add_into(middle, [middle, other])
     half_rows = middle.shape[1] // 2
     yield from ring_reduce(
         net,
@@ -191,15 +207,16 @@
     )
 
 
-def core_pair(net, me, source, other, middle):
-    across = net.copy(source.at[:, 1 - me.core], other, me.at(core=1 - me.core))
+def core_pair(net, me, sending, other, middle):
+    across = net.copy(sending, other, me.at(core=1 - me.core))
     yield
+    net.sent(across)
     across.wait_recv()
-    add_into(middle, [source.at[:, me.core], other])
-
-
-def dense_x_first(net, me, source, other, middle, slots, corner, last, out):
-    yield from core_pair(net, me, source, other, middle)
+    add_into(middle, [middle, other])
+
+
+def dense_x_first(net, me, sending, other, middle, slots, corner, last, out):
+    yield from core_pair(net, me, sending, other, middle)
     yield from ring_reduce(
         net,
         me.at(x=me.x_by(1)),
@@ -221,8 +238,8 @@
     )
 
 
-def dense_z_first(net, me, source, other, middle, slots, corner, last, out):
-    yield from core_pair(net, me, source, other, middle)
+def dense_z_first(net, me, sending, other, middle, slots, corner, last, out):
+    yield from core_pair(net, me, sending, other, middle)
     yield from ring_reduce(
         net,
         me.at(z=me.z_by(1)),
@@ -262,8 +279,7 @@
     own[most:] = peak
 
 
-def all_small(net, me, small, working, by_core, by_x, by_z, by_y, out):
-    working[...] = small[...]
+def all_small(net, me, working, by_core, by_x, by_z, by_y, out):
     yield from all_sum(net, [me.at(core=1 - me.core)], me.core, working, by_core, 40)
     yield from all_sum(net, [me.at(x=me.x_by(s)) for s in (1, 2, 3)], me.x, working, by_x, 40)
     yield from all_sum(net, [me.at(z=me.z_by(s)) for s in (1, 2, 3)], me.z, working, by_z, 40)
@@ -282,24 +298,6 @@
     core = me.core if a % 2 == 0 else 1 - me.core
     y = me.y_by(b)
     return z // 2 * 2 + core, y, me.at(z=z, core=core, y=y)
-
-
-def bring_home(net, me, produced, home, table, after, out):
-    sent = []
-    for a, b, dp, y, device in peers(me):
-        sent.append(net.copy(produced.at[dp, y], home.at[me.dp, me.y], device))
-    home[me.dp, me.y] = produced[me.dp, me.y]
-    for step in range(5):
-        yield
-    for made in sent:
-        made.wait_recv()
-    gather_rows(
-        table,
-        home,
-        lambda columns, total: out.__setitem__(
-            (slice(None), columns), after[:, columns] + total
-        ),
-    )
 
 
 def gather_rows(table, home, store):
@@ -313,26 +311,29 @@
     lax.fori_loop(0, home.shape[3] // 256, body, 0)
 
 
-def in_turn(tasks):
-    tasks = list(tasks)
-    while tasks:
-        for task in list(tasks):
-            if next(task, "end") == "end":
-                tasks.remove(task)
-
-
-def reduce_kernel(counts, *refs):
-    refs = list(refs)
-
-    def take(number):
-        taken = refs[:number]
-        del refs[:number]
-        return taken
-
-    gate, up, down, query, key_value, out_w, small, produced, table, after = take(10)
-    gate_out, up_out, down_out, query_out, key_value_out, out_w_out, small_out, layer = take(8)
-    scratch = [take(count) for count in counts]
-    send, recv = take(2)
+def turned(values):
+    return pltpu.roll(values, 64, 1)
+
+
+def column_of(row):
+    eye = lax.broadcasted_iota(jnp.int32, (128, 128), 0) == lax.broadcasted_iota(
+        jnp.int32, (128, 128), 1
+    )
+    return jnp.sum(jnp.where(eye, row, 0.0), axis=1, keepdims=True)
+
+
+def norm_back(gradient, raw, gain):
+    inverse = lax.rsqrt(jnp.mean(raw * raw, axis=-1, keepdims=True) + epsilon)
+    normal = raw * inverse
+    scaled = gradient * gain
+    result = inverse * (scaled - normal * jnp.mean(scaled * normal, axis=-1, keepdims=True))
+    return result, jnp.sum(gradient * normal, axis=0, keepdims=True)
+
+
+def back_kernel(names, *refs):
+    r = types.SimpleNamespace(**dict(zip(names, refs, strict=True)))
+    low, full = jnp.bfloat16, jnp.float32
+    score_scale = HEAD_SIZE ** (-0.5)
     me = Place()
     greet(
         [
@@ -341,86 +342,370 @@
             me.at(z=me.z_by(1)),
             me.at(z=me.z_by(3)),
             me.at(x=me.x_by(2)),
-            me.at(z=me.z_by(2)),
         ]
-        + [one[4] for one in peers(me) if one[:2] != (2, 0)]
-    )
-    net = Net(send, recv)
-    in_turn(
-        [
-            all_small(net, me, small, *scratch[6], small_out),
-            dense_z_first(net, me, out_w, *scratch[5], out_w_out),
-            dense_x_first(net, me, query, *scratch[3], query_out),
-            dense_x_first(net, me, key_value, *scratch[4], key_value_out),
-            expert_z_first(net, me, down, *scratch[2], down_out),
-            expert_x_first(net, me, gate, *scratch[0], gate_out),
-            expert_x_first(net, me, up, *scratch[1], up_out),
-            bring_home(net, me, produced, *scratch[7], table, after, layer),
-        ]
-    )
+        + [one[4] for one in peers(me)]
+    )
+    net = Net(r.send, r.recv, r.here)
+
+    branch, whole = r.branch, r.whole
+    above, below = me.at(y=me.y_by(1)), me.at(y=me.y_by(3))
+    to_above = net.copy(branch, whole.at[:, me.y], above)
+    to_below = net.copy(branch, whole.at[:, me.y], below)
+    own_branch = net.load(branch, whole.at[:, me.y])
+    weight = r.weight
+    load_out = net.load(r.w_out, weight)
+    gate = x_first(
+        net, me, r.gate, r.gate_slots, r.gate_middle, r.gate_other,
+        r.gate_out, r.gate_held,
+    )
+    up = x_first(
+        net, me, r.up, r.up_slots, r.up_middle, r.up_other,
+        r.up_out, r.up_held,
+    )
+    down = z_first(
+        net, me, r.down, r.down_other, r.down_middle, r.down_slots,
+        r.down_out,
+    )
+    for task in (gate, up, down):
+        next(task)
+
+    hidden, inverse = r.hidden, r.inverse
+    for s in range(3):
+        rows = slice(s * 128, s * 128 + 128)
+        values = hidden[rows, :].astype(full)
+        root = lax.rsqrt(jnp.mean(values * values, axis=-1, keepdims=True) + epsilon)
+        inverse[rows, :] = jnp.broadcast_to(root, (128, 128))
+
+    first, second = pl.ds(0, 1024), pl.ds(1024, 1024)
+    to_above.wait_recv()
+    passed = whole.at[:, me.y_by(3), :, first]
+    far_above = net.copy(passed, passed, above)
+    to_below.wait_recv()
+    passed = whole.at[:, me.y_by(1), :, second]
+    far_below = net.copy(passed, passed, below)
+    own_branch.wait()
+    load_out.wait()
+    far_above.wait_recv()
+    far_below.wait_recv()
+
+    heads_grad, mixed = r.heads_grad, r.mixed
+
+    def heads_step(step, carry):
+        columns = pl.ds(pl.multiple_of(step * 256, 256), 256)
+        heads_grad[:, columns] = jnp.dot(
+            whole[...].reshape(384, 2048), weight[:, columns], preferred_element_type=full
+        ).astype(low)
+        return carry
+
+    lax.fori_loop(0, 4, heads_step, 0)
+    load_query = net.load(r.w_query, weight)
+
+    produced, home, table = r.produced, r.home, r.table
+    mine = pl.ds(pl.multiple_of(me.dp * 192 + me.y * 48, 16), 48)
+    home_came = [
+        net.copy(produced.at[dp, y], home.at[mine], device) for a, b, dp, y, device in peers(me)
+    ]
+    home_own = net.load(produced.at[me.dp, me.y], home.at[mine])
+
+    query, query_raw, pair = r.query, r.query_raw, r.pair
+    cosine, sine = r.cosine, r.sine
+    gain_query, gain_key = r.gain_query, r.gain_key
+    bias, key_sum, value_sum = r.bias, r.key_sum, r.value_sum
+    pair_grad, gain_part = r.pair_grad, r.gain_part
+    gain_part[...] = jnp.zeros((8, 128), full)
+
+    def rope_back(gradient):
+        return gradient * cosine[...] + turned(gradient) * sine[...]
+
+    def attend(s):
+        here = pl.ds(s * 128, 128)
+        spot = me.context * 128 + lax.broadcasted_iota(jnp.int32, (128, 1024), 0)
+        allowed = (column_of(r.seg_query[s]) == r.seg_key[s]) & (
+            lax.broadcasted_iota(jnp.int32, (128, 1024), 1) <= spot
+        )
+        bias[...] = jnp.where(allowed, 0.0, masked_value)
+        key_sum[...] = jnp.zeros_like(key_sum)
+        value_sum[...] = jnp.zeros_like(value_sum)
+
+        def two_heads(step, carry):
+            columns = pl.ds(pl.multiple_of(step * 256, 256), 256)
+
+            def stacked(ref):
+                both = ref[here, columns]
+                return jnp.concatenate([both[:, :128], both[:, 128:]], axis=0)
+
+            q, d = stacked(query), stacked(heads_grad)
+            keys, values = pair[0, s], pair[1, s]
+            lines = r.log_sum
+            logs = jnp.concatenate(
+                [column_of(lines[s * 8 + step * 2]), column_of(lines[s * 8 + step * 2 + 1])], axis=0
+            )
+            score = contract_last(q, keys) * score_scale
+            score = score + jnp.concatenate([bias[...], bias[...]], axis=0)
+            prob = jnp.exp(score - logs)
+            prob_grad = contract_last(d, values)
+            delta = jnp.sum(prob * prob_grad, axis=-1, keepdims=True)
+            score_grad = (prob * (prob_grad - delta)).astype(low)
+            value_sum[...] += contract_first(prob.astype(low), d)
+            key_sum[...] += contract_first(score_grad, q)
+            turned_grad = jnp.dot(score_grad, keys, preferred_element_type=full) * score_scale
+            for half in range(2):
+                run = pl.ds(pl.multiple_of(step * 256 + half * 128, 128), 128)
+                grad, part = norm_back(
+                    rope_back(turned_grad[half * 128 : half * 128 + 128]),
+                    query_raw[here, run],
+                    gain_query[...],
+                )
+                heads_grad[here, run] = grad.astype(low)
+                gain_part[0:1, :] += part
+            return carry
+
+        lax.fori_loop(0, 4, two_heads, 0)
+        pair_grad[:, :, 0, s] = (key_sum[...] * score_scale).astype(low).reshape(4, 2, 128, 128)
+        pair_grad[:, :, 1, s] = value_sum[...].astype(low).reshape(4, 2, 128, 128)
+
+    attend(0)
+    attend(1)
+    next(gate)
+    next(up)
+    attend(2)
+    pairs = x_first(
+        net, me, pair_grad, r.pair_slots, r.pair_middle, r.pair_other,
+        r.pair_out,
+    )
+    next(pairs)
+
+    query_low = heads_grad
+    gain_attn = r.gain_attn
+
+    def normed(columns):
+        values = hidden[:, columns].astype(full)
+        return (values * inverse[:, 0:1] * gain_attn[:, columns]).astype(low)
+
+    def whole_part(columns):
+        return whole[:, :, :, columns].reshape(384, 256)
+
+    def weigh(core, left, right, target):
+        def body(step, carry):
+            z_hi, part = step // 2, lax.rem(step, 2)
+            columns = pl.ds(pl.multiple_of((z_hi * 2 + core) * 512 + part * 256, 256), 256)
+            made = contract_first(left(columns), right[...]).astype(low)
+            target[z_hi, pl.ds(part * 2, 2)] = made.reshape(2, 2, 64, right.shape[1])
+            return carry
+
+        lax.fori_loop(0, 4, body, 0)
+
+    def dense(order, left, right, sending, other, middle, *more):
+        weigh(1 - me.core, left, right, sending)
+        task = order(net, me, sending, other, middle, *more)
+        next(task)
+        weigh(me.core, left, right, middle)
+        return task
+
+    out_w = dense(
+        dense_z_first, whole_part, mixed, r.sending, r.out_w_other, r.out_w_middle, r.out_w_slots, r.out_w_corner,
+        r.out_w_last, r.out_w_out,
+    )
+    next(pairs)
+    next(down)
+    next(out_w)
+    query_w = dense(
+        dense_x_first, normed, query_low, r.sending, r.query_w_other, r.query_w_middle, r.query_w_slots, r.query_w_corner,
+        r.query_w_last, r.query_w_out,
+    )
+    next(pairs)
+    next(gate)
+    next(up)
+
+    pair_out, key_raw, pair_low = r.pair_out, r.key_raw, r.pair_low
+    next(pairs, None)
+    for s in range(3):
+        rows = slice(s * 128, s * 128 + 128)
+        grad, part = norm_back(rope_back(pair_out[0, s]), key_raw[rows, :], gain_key[...])
+        gain_part[1:2, :] += part
+        pair_low[rows, :128] = grad.astype(low)
+        pair_low[rows, 128:] = pair_out[1, s].astype(low)
+
+    load_query.wait()
+    net.sent(far_above)
+    net.sent(far_below)
+    small = r.small
+    normed_part = r.normed_part
+
+    def normed_step(step, carry):
+        columns = pl.ds(pl.multiple_of(step * 256, 256), 256)
+        made = contract_last(query_low[...], weight[columns, :])
+        made = made + contract_last(pair_low[:, :128], r.w_key[columns, :])
+        made = made + contract_last(pair_low[:, 128:], r.w_value[columns, :])
+        normal = hidden[:, columns].astype(full) * inverse[:, 0:1]
+        normed_part[:, columns] = jnp.sum(made * normal, axis=0, keepdims=True)
+        whole[:, :, :, columns] = made.astype(low).reshape(3, 4, 32, 256)
+        return carry
+
+    lax.fori_loop(0, 8, normed_step, 0)
+    normed_out = r.normed_out
+    normed_sum = ring_reduce(
+        net,
+        above,
+        below,
+        lambda step, half: whole.at[:, me.y_by(step), :, pl.ds(half * 1024, 1024)],
+        r.normed_slots,
+        lambda half: normed_out.at[:, :, pl.ds(half * 1024, 1024)],
+    )
+    next(normed_sum)
+    for step in range(16):
+        run = slice(step * 128, step * 128 + 128)
+        small[step : step + 1, :] = normed_part[:, run]
+        small[16 + step : 17 + step, :] = r.moe_gain_part[:, run]
+    small[32:40, :] = gain_part[...]
+    small[40:, :] = r.peaks[...]
+    smalls = all_small(
+        net, me, small, r.by_core, r.by_x, r.by_z, r.by_y, r.small_out
+    )
+    next(smalls)
+    pair_w = dense(
+        dense_x_first, normed, pair_low, r.pair_sending, r.pair_w_other, r.pair_w_middle, r.pair_w_slots, r.pair_w_corner,
+        r.pair_w_last, r.pair_w_out,
+    )
+    next(query_w)
+    next(smalls)
+
+    def rest(*tasks):
+        for task in tasks:
+            next(task, None)
+
+    rest(normed_sum, out_w, pair_w, smalls, gate, up, down, query_w)
+
+    next(normed_sum, None)
+    for s in range(3):
+        rows = pl.ds(pl.multiple_of(s * 128 + me.y * 32, 32), 32)
+        grad, _ = norm_back(normed_out[s], hidden[rows, :].astype(full), gain_attn[...])
+        normed_out[s] = grad
+
+    rest(out_w, pair_w, smalls, down, gate, up, query_w)
+    rest(pair_w, out_w, smalls, query_w)
+
+    for made in home_came:
+        made.wait_recv()
+    home_own.wait()
+    home_loads = [
+        net.load(home.at[:, pl.ds(half * 1024, 1024)], weight.at[pl.ds(half * 768, 768)])
+        for half in range(2)
+    ]
+    rest(pair_w, out_w, smalls, query_w, gate, up, down)
+    moe_out = r.moe_out
+    for half in range(2):
+        home_loads[half].wait()
+
+        def gather(step, carry, half=half):
+            columns = pl.ds(pl.multiple_of(step * 256, 256), 256)
+            total = contract_first(table[...], weight[half * 768 : half * 768 + 768, columns])
+            moe_out[:, pl.ds(pl.multiple_of(half * 1024 + step * 256, 256), 256)] = total[:96]
+            return carry
+
+        lax.fori_loop(0, 4, gather, 0)
+    tasks = [pair_w, out_w, smalls, query_w, gate, up, down]
+    while tasks:
+        for task in list(tasks):
+            if next(task, "end") == "end":
+                tasks.remove(task)
     net.finish()
 
 
-def reduce_weights(gate, up, down, query, key_value, out_w, small, produced, table, after):
+def dense_slots(columns, corner):
     low = jnp.bfloat16
-    x_first = [
-        pltpu.VMEM((6, 256, 768), low),
-        pltpu.VMEM((2, 256, 768), low),
-        pltpu.VMEM((256, 768), low),
+    return [
+        pltpu.VMEM((2, 4, 2, 64, columns), low),
+        pltpu.VMEM((2, 4, 2, 64, columns), low),
+        pltpu.VMEM((6, 2, 64, columns), low),
+        pltpu.VMEM(corner + (64, columns), low),
+        pltpu.VMEM((6, 32, columns), low),
     ]
-    z_first = [
-        pltpu.VMEM((4, 256, 768), low),
-        pltpu.VMEM((4, 256, 768), low),
-        pltpu.VMEM((6, 128, 768), low),
-    ]
-
-    def dense(columns, x_first):
-        return [
-            pltpu.VMEM((2, 4, 2, 64, columns), low),
-            pltpu.VMEM((2, 4, 2, 64, columns), low),
-            pltpu.VMEM((6, 2, 64, columns), low),
-            pltpu.VMEM((2, 2, 64, columns) if x_first else (4, 64, columns), low),
-            pltpu.VMEM((6, 32, columns), low),
-        ]
-
-    smalls = [pltpu.VMEM(small.shape, jnp.float32)] + [
-        pltpu.VMEM((count,) + small.shape, jnp.float32) for count in (2, 4, 4, 4)
-    ]
-    groups = [x_first, x_first, z_first, dense(1024, True), dense(256, True), dense(1024, False)]
-    groups += [smalls, [pltpu.VMEM((4, 4, 48, 2048), low)]]
-    copies = 90
-    return pl.pallas_call(
-        functools.partial(reduce_kernel, [len(group) for group in groups]),
-        out_shape=[
-            jax.ShapeDtypeStruct((256, 768), jnp.float32),
-            jax.ShapeDtypeStruct((256, 768), jnp.float32),
-            jax.ShapeDtypeStruct((256, 768), jnp.float32),
-            jax.ShapeDtypeStruct((64, 1024), jnp.float32),
-            jax.ShapeDtypeStruct((64, 256), jnp.float32),
-            jax.ShapeDtypeStruct((64, 1024), jnp.float32),
-            jax.ShapeDtypeStruct(small.shape, jnp.float32),
-            jax.ShapeDtypeStruct(after.shape, jnp.float32),
-        ],
-        in_specs=[VMEM] * 10,
-        out_specs=[VMEM] * 8,
-        scratch_shapes=[one for group in groups for one in group]
-        + [pltpu.SemaphoreType.DMA((copies,)), pltpu.SemaphoreType.DMA((copies,))],
+
+
+def back(far, near):
+    low, full = jnp.bfloat16, jnp.float32
+    outs = dict(
+        gate_out=(256, 768),
+        up_out=(256, 768),
+        down_out=(256, 768),
+        query_w_out=(64, 1024),
+        pair_w_out=(64, 256),
+        out_w_out=(64, 1024),
+        small_out=(48, 128),
+        normed_out=(3, 32, 2048),
+        moe_out=(96, 2048),
+    )
+    scratch = dict(
+        whole=pltpu.VMEM((3, 4, 32, 2048), low),
+        weight=pltpu.VMEM((2048, 1024), low),
+        inverse=pltpu.VMEM((384, 128), full),
+        heads_grad=pltpu.VMEM((384, 1024), low),
+        bias=pltpu.VMEM((128, 1024), full),
+        key_sum=pltpu.VMEM((1024, 128), full),
+        value_sum=pltpu.VMEM((1024, 128), full),
+        pair_grad=pltpu.VMEM((4, 2, 2, 3, 128, 128), low),
+        pair_slots=pltpu.VMEM((6, 2, 3, 128, 128), low),
+        pair_middle=pltpu.VMEM((2, 2, 3, 128, 128), low),
+        pair_other=pltpu.VMEM((2, 3, 128, 128), low),
+        pair_out=pltpu.VMEM((2, 3, 128, 128), full),
+        pair_low=pltpu.VMEM((384, 256), low),
+        gain_part=pltpu.VMEM((8, 128), full),
+        normed_part=pltpu.VMEM((1, 2048), full),
+        normed_slots=pltpu.VMEM((6, 3, 32, 1024), low),
+        small=pltpu.VMEM((48, 128), full),
+        by_core=pltpu.VMEM((2, 48, 128), full),
+        by_x=pltpu.VMEM((4, 48, 128), full),
+        by_z=pltpu.VMEM((4, 48, 128), full),
+        by_y=pltpu.VMEM((4, 48, 128), full),
+        down_other=pltpu.VMEM((4, 256, 768), low),
+        down_middle=pltpu.VMEM((4, 256, 768), low),
+        down_slots=pltpu.VMEM((6, 128, 768), low),
+        gate_slots=pltpu.VMEM((6, 256, 768), low),
+        gate_middle=pltpu.VMEM((2, 256, 768), low),
+        gate_other=pltpu.VMEM((256, 768), low),
+        gate_held=pltpu.VMEM((4, 256, 768), low),
+        up_slots=pltpu.VMEM((6, 256, 768), low),
+        up_middle=pltpu.VMEM((2, 256, 768), low),
+        up_other=pltpu.VMEM((256, 768), low),
+        up_held=pltpu.VMEM((4, 256, 768), low),
+        sending=pltpu.VMEM((2, 4, 2, 64, 1024), low),
+        pair_sending=pltpu.VMEM((2, 4, 2, 64, 256), low),
+        query_w_other=None,
+        query_w_middle=None,
+        query_w_slots=None,
+        query_w_corner=None,
+        query_w_last=None,
+        pair_w_other=None,
+        pair_w_middle=None,
+        pair_w_slots=None,
+        pair_w_corner=None,
+        pair_w_last=None,
+        out_w_other=None,
+        out_w_middle=None,
+        out_w_slots=None,
+        out_w_corner=None,
+        out_w_last=None,
+        send=pltpu.SemaphoreType.DMA((104,)),
+        recv=pltpu.SemaphoreType.DMA((104,)),
+        here=pltpu.SemaphoreType.DMA((20,)),
+    )
+    dense = dense_slots(1024, (2, 2)) + dense_slots(256, (2, 2)) + dense_slots(1024, (4,))
+    scratch = {name: one or dense.pop(0) for name, one in scratch.items()}
+    names = list(far) + list(near) + list(outs) + list(dict(home=0)) + list(scratch)
+    results = pl.pallas_call(
+        functools.partial(back_kernel, names),
+        out_shape=[jax.ShapeDtypeStruct(size, full) for size in outs.values()]
+        + [jax.ShapeDtypeStruct((768, 2048), low)],
+        in_specs=[ANY] * len(far) + [VMEM] * len(near),
+        out_specs=[VMEM] * len(outs) + [ANY],
+        scratch_shapes=list(scratch.values()),
         compiler_params=pltpu.CompilerParams(
-            collective_id=0, has_side_effects=True, vmem_limit_bytes=56 << 20
+            collective_id=0, has_side_effects=True, vmem_limit_bytes=62 << 20
         ),
-        name="reduce_weights",
-    )(
-        gate.reshape(4, 2, 256, 768),
-        up.reshape(4, 2, 256, 768),
-        down.reshape(4, 2, 256, 768),
-        query.reshape(2, 2, 4, 2, 64, 1024),
-        key_value.reshape(2, 2, 4, 2, 64, 256),
-        out_w.reshape(2, 2, 4, 2, 64, 1024),
-        small,
-        produced,
-        table,
-        after,
-    )
+        name="back",
+    )(*far.values(), *near.values())
+    return types.SimpleNamespace(**dict(zip(outs, results[:-1], strict=True)))
 
 
 def moe_kernel(
@@ -714,6 +999,7 @@
     )
     query_group = query_rot.reshape(seqs_local, rows_ctx, kv_count, per_group, HEAD_SIZE)
     seg_query = lax.dynamic_slice_in_dim(segments, ctx_index * rows_ctx, rows_ctx, 1)
+    seg_float_query = seg_query.astype(jnp.float32)
     query_spot = ctx_index * rows_ctx + jnp.arange(rows_ctx, dtype=jnp.int32)
     key_spot = jnp.arange(seq_length, dtype=jnp.int32)
     allowed = (seg_query[:, :, None] == segments[:, None, :]) & (
@@ -767,103 +1053,51 @@
     )
     after_grad = after_grad.reshape(seqs_local, own_rows, model_width)
     gate_grad = gate_grad[:, :pair_tokens].T.reshape(seqs_local, own_rows, top_count)
-    branch_grad = lax.all_gather(after_grad.astype(jnp.bfloat16), "experts", axis=1, tiled=True)
-    branch_flat = branch_grad.reshape(token_count, model_width)
-    heads_grad = jnp.dot(branch_flat, w_out, preferred_element_type=jnp.float32).astype(
-        jnp.bfloat16
-    )
-    w_out_part = contract_first(branch_flat, mixed_low)
-    heads_group = heads_grad.reshape(seqs_local, rows_ctx, kv_count, per_group, HEAD_SIZE)
-    again_prob = jnp.exp(masked_scores() - log_total)
-    again_low = again_prob.astype(jnp.bfloat16)
-    prob_grad = jnp.einsum(
-        "sqhgd,skhd->shqgk", heads_group, values_all, preferred_element_type=jnp.float32
-    )
-    delta = jnp.sum(again_prob * prob_grad, axis=-1, keepdims=True)
-    score_grad = (again_prob * (prob_grad - delta)).astype(jnp.bfloat16)
-    query_rot_grad = (
-        jnp.einsum("shqgk,skhd->sqhgd", score_grad, keys_all, preferred_element_type=jnp.float32)
-        * score_scale
-    )
-    key_part = (
-        jnp.einsum("shqgk,sqhgd->skhd", score_grad, query_group, preferred_element_type=jnp.float32)
-        * score_scale
-    )
-    value_part = jnp.einsum(
-        "shqgk,sqhgd->skhd", again_low, heads_group, preferred_element_type=jnp.float32
-    )
-    key_rot_grad, value_grad = (
-        lax.psum_scatter(
-            key_part.astype(jnp.bfloat16), "context", scatter_dimension=1, tiled=True
-        ).astype(jnp.float32),
-        lax.psum_scatter(
-            value_part.astype(jnp.bfloat16), "context", scatter_dimension=1, tiled=True
-        ).astype(jnp.float32),
-    )
-
-    def rope_back(gradient):
-        return gradient * cosine_table + turn_back(gradient * sine_table)
-
-    query_normed_grad = rope_back(
-        query_rot_grad.reshape(seqs_local, rows_ctx, head_count, HEAD_SIZE)
-    )
-    query_grad, query_gain_part = rms_back(query_normed_grad, query_raw, gain_query)
-    key_grad, key_gain_part = rms_back(rope_back(key_rot_grad), unclipped_key, gain_key)
-    query_low = query_grad.astype(jnp.bfloat16).reshape(token_count, head_count * HEAD_SIZE)
-    key_low = key_grad.astype(jnp.bfloat16).reshape(token_count, kv_count * HEAD_SIZE)
-    value_back = value_grad.astype(jnp.bfloat16).reshape(token_count, kv_count * HEAD_SIZE)
-    normed_grad = (
-        contract_last(query_low, w_query)
-        + contract_last(key_low, key_weight_matrix)
-        + contract_last(value_back, value_weight_matrix)
-    )
-    w_query_part = contract_first(normed_flat, query_low)
-    w_key_part = contract_first(normed_flat, key_low)
-    w_value_part = contract_first(normed_flat, value_back)
-    own_normed_grad = lax.psum_scatter(
-        normed_grad.reshape(seqs_local, rows_ctx, model_width).astype(jnp.bfloat16),
-        "experts",
-        scatter_dimension=1,
-        tiled=True,
-    ).astype(jnp.float32)
-    input_part, attn_gain_part = rms_back(own_normed_grad, own_inputs, gain_attn)
-    input_grad = after_grad + input_part
-    key_value_part = jnp.concatenate([w_key_part, w_value_part], axis=1)
-    small = jnp.concatenate(
-        [
-            attn_gain_part.reshape(16, 128),
-            moe_gain_part.reshape(16, 128),
-            query_gain_part[None],
-            key_gain_part[None],
-            jnp.zeros((6, 128), jnp.float32),
-            jnp.broadcast_to(head_peak[:, None], (head_count, 128)),
-        ],
-        axis=0,
-    )
-    (
-        w_gate_grad,
-        w_up_grad,
-        w_down_grad,
-        w_query_grad,
-        w_key_value_grad,
-        w_out_grad,
-        small,
-        layer_out,
-    ) = reduce_weights(
-        full_gate,
-        full_up,
-        full_down,
-        w_query_part.astype(jnp.bfloat16),
-        key_value_part.astype(jnp.bfloat16),
-        w_out_part.astype(jnp.bfloat16),
-        small,
-        produced,
-        table,
-        after_flat,
-    )
-    layer_out = layer_out.reshape(seqs_local, own_rows, model_width)
-    w_key_grad, w_value_grad = w_key_value_grad[:, :128], w_key_value_grad[:, 128:]
-    w_gate_grad, w_up_grad, w_down_grad = w_gate_grad[None], w_up_grad[None], w_down_grad[None]
+    cosine_row, sine_row = cosine_table[0, :, 0], sine_table[0, :, 0]
+    turn_sign = jnp.where(jnp.arange(HEAD_SIZE) < HEAD_SIZE // 2, 1.0, -1.0)
+    seg_float = segments.astype(jnp.float32)
+    done = back(
+        dict(
+            branch=after_grad.astype(jnp.bfloat16),
+            w_out=w_out,
+            w_query=w_query,
+            gate=full_gate.reshape(4, 2, 256, 768),
+            up=full_up.reshape(4, 2, 256, 768),
+            down=full_down.reshape(4, 2, 256, 768),
+            produced=produced,
+        ),
+        dict(
+            w_key=key_weight_matrix,
+            w_value=value_weight_matrix,
+            table=table,
+            hidden=hidden_in.reshape(token_count, model_width),
+            mixed=mixed_low,
+            query=query_rot.reshape(token_count, head_count * HEAD_SIZE),
+            query_raw=query_raw.reshape(token_count, head_count * HEAD_SIZE),
+            key_raw=unclipped_key.reshape(token_count, HEAD_SIZE),
+            pair=jnp.stack([keys_all[:, :, 0], values_all[:, :, 0]]),
+            log_sum=log_total[:, 0, :, :, 0].swapaxes(1, 2).reshape(24, 1, 128),
+            seg_query=seg_float_query[:, None, :],
+            seg_key=seg_float[:, None, :],
+            cosine=cosine_row,
+            sine=sine_row * turn_sign,
+            gain_query=gain_query[None],
+            gain_key=gain_key[None],
+            gain_attn=gain_attn[None],
+            moe_gain_part=moe_gain_part,
+            peaks=jnp.broadcast_to(head_peak[:, None], (head_count, 128)),
+        ),
+    )
+    layer_out = after_attn + done.moe_out.reshape(seqs_local, own_rows, model_width)
+    input_grad = after_grad + done.normed_out
+    w_key_grad, w_value_grad = done.pair_w_out[:, :128], done.pair_w_out[:, 128:]
+    w_query_grad, w_out_grad = done.query_w_out, done.out_w_out
+    w_gate_grad, w_up_grad, w_down_grad = (
+        done.gate_out[None],
+        done.up_out[None],
+        done.down_out[None],
+    )
+    small = done.small_out
     attn_gain_grad = small[:16].reshape(model_width)
     moe_gain_grad = small[16:32].reshape(model_width)
     query_gain_grad, key_gain_grad = small[32], small[33]

time: 597 us -> 465 us (0.78)
  waiting for transfers between devices: 90 us -> 16.6 us
  matrix products: 64.6 us -> 16.7 us
  local copies, waits for them, and re-layouts: 43 us -> 17.9 us
  Pallas kernels: 279 us -> 296 us
  other arithmetic: 42.8 us -> 33 us
    reduce_scatter x2 -> x0, waiting for transfers between devices: 42.4 us -> none  [the longest x1 35.5 us: shards(): lax.psum_scatter(key_part.astype(jnp.bfloat16), 'context', scatter_dimens...]
    dot_general x9 -> x0, matrix products: 42 us -> none  [the longest x1 11.3 us: shards(): jnp.einsum('sqhgd,skhd->shqgk', heads_group, values_all, preferred_elemen...]
    all_gather x1 -> x0, waiting for transfers between devices: 25.9 us -> none  [shards(): lax.all_gather(after_grad.astype(jnp.bfloat16), 'experts', axis=1, tiled=...]
    pallas_call x1, Pallas kernels: 128 us -> 145 us  [back(): pl.pallas_call(functools.partial(back_kernel, names), out_shape=[jax.Shap...]
    unnamed x137 -> x84, local copies, waits for them, and re-layouts: 23.5 us -> 9.43 us
    convert_element_type x6 -> x2, other arithmetic: 10.7 us -> 0.02 us  [the longest x1 0.01 us: shards(): seg_float_query = seg_query.astype(jnp.float32)]
    reduce_sum x5 -> x0, other arithmetic: 9.33 us -> none  [the longest x1 2.82 us: shards(): jnp.sum(jnp.exp(masked - row_peak), axis=-1, keepdims=True)]
    dot_general x4 -> x1, matrix products: 11.4 us -> 3.1 us  [contract_last(): lax.dot_general(left, right, (((1,), (1,)), ((), ())), preferred_element_...]
  transfers between devices with their start and end apart: 5 -> 1, of which waited for: 4 -> 1; matrix products, arithmetic and copies ran while one was open for 10% -> 2% of each run, Pallas kernels for 0% -> 0%
where the time goes in v3:
time: 465 us; the launch traced here: 457 us
  Pallas kernels  296 us (64%)
  blocking collectives  61.6 us (13%)
  other arithmetic  33 us (7%)
  local copies, waits for them, and re-layouts  17.9 us (4%)
  matrix products  16.7 us (4%)
  waiting for transfers between devices  16.6 us (4%)
  between operations  15 us (3%)
    pallas_call x1, Pallas kernels, moe(): pl.pallas_call(moe_kernel, out_shape=[shape((96, 2048), full), shape((1,...  151 us
    pallas_call x1, Pallas kernels, back(): pl.pallas_call(functools.partial(back_kernel, names), out_shape=[jax.Shap...  145 us
    all_gather x1, blocking collectives, shards(): lax.all_gather(key_rot, 'context', axis=1, tiled=True)  31.8 us
    all_gather x1, blocking collectives, shards(): lax.all_gather(value_reduced, 'context', axis=1, tiled=True)  29.8 us
    reduce_scatter x1, waiting for transfers between devices, shards(): lax.psum_scatter(branch_part.reshape(seqs_local, rows_ctx, model_width).a...  16.6 us
    unnamed x84, local copies, waits for them, and re-layouts  9.43 us
  transfers between devices with their start and end apart: 1, of which 1 were waited for; matrix products, arithmetic and copies ran while one was open for 2% of the time, Pallas kernels for 0%

profile of v3, /device:TPU:0, one launch (start us, length us, event | category | flops | bytes accessed | tf_op | source)
XLA Modules:
  0.0 457.0 jit_solution(8606578456535607483)
XLA Ops:
  7.2 0.5 negate_power_fusion
  8.3 0.7 convert_element_type.79
  9.0 1.8 multiply_reduce_fusion
  11.2 4.6 fusion.27.refs_13_
  16.2 0.8 copy-done.3
  19.2 2.2 slice_negate_fusion
  21.9 2.2 multiply_reduce_fusion.1
  24.1 0.5 convert_bitcast_fusion
  25.0 1.0 broadcast_multiply_fusion
  26.0 0.6 copy-done.13
  26.8 31.8 %all_gather.7 = bf16[3,1024,1,128]{3,1,0,2:T(8,128)(2,1)} all-gather(bf16[3,128,1,128]{3,1,0,2:T(8,128)(2,1)S(1)} %fusion.19), channel_id=1, replica_groups=mesh['dp'=4,'context'=8,'experts'=4] {'context'}, dimensions={1}, use_global_device_ids=true | all-gather | bytes 884736 | tf_op jit(solution)/shard_map/all_gather | solution.py:997
  58.6 0.8 iota_compare_fusion
  59.8 3.4 add_convert_fusion
  63.2 2.5 fusion.1
  65.7 4.2 fusion
  69.9 0.6 convolution_convert_fusion
  70.5 29.8 %all_gather.6 = bf16[3,1024,1,128]{3,1,0,2:T(8,128)(2,1)S(1)} all-gather(bf16[3,128,1,128]{3,1,0,2:T(8,128)(2,1)S(1)} %bitcast.155), channel_id=1, replica_groups=mesh['dp'=4,'context'=8,'experts'=4] {'context'}, dimensions={1}, use_global_device_ids=true | all-gather | bytes 884736 | tf_op jit(solution)/shard_map/all_gather | solution.py:998
  100.2 3.8 fusion.13
  104.1 3.1 fusion.6
  107.2 2.0 convert_element_type.78
  109.5 0.6 broadcast_in_dim.94
  110.5 1.1 copy.86
  111.6 0.5 broadcast_in_dim.83.refs_17_
  112.1 0.6 broadcast_in_dim.84.refs_18_
  112.7 0.6 pad.8.ids
  113.3 0.6 pad.9.gates
  113.9 1.3 pad_maximum_fusion.refs_15_
  115.9 0.8 copy-done.4
  117.1 1.8 fusion.9.refs_12_
  118.9 16.6 %reduce-scatter.2.cloned.1.call-done = bf16[3,32,2048]{2,1,0:T(8,128)(2,1)} async-done(((bf16[3,128,2048]{2,1,0:T(8,128)(2,1)}), bf16[3,32,2048]{2,1,0:T(8,128)(2,1)}) %reduce-scatter.2.cloned.1.call-update) | async-done | bytes 393232 | tf_op jit(solution)/shard_map/reduce_scatter | solution.py:1029
  135.5 2.2 convert_add_fusion
  137.7 0.7 broadcast_in_dim.82.capacity
  138.3 151.5 %moe.1 = (f32[96,2048]{1,0:T(8,128)}, f32[1,2048]{1,0:T(1,128)}, f32[8,128]{1,0:T(8,128)}, bf16[4,4,48,2048]{3,2,1,0:T(8,128)(2,1)}, bf16[768,128]{1,0:T(8,128)(...) custom-call(f32[96,2048]{1,0:T(8,128)} %bitcast.130, ...), custom_call_target="tpu_custom_call" | custom-call | tf_op jit(solution)/shard_map/moe/pallas_call | solution.py:902
  289.9 1.9 convert_element_type.94.refs_0_
  291.8 0.7 broadcast_in_dim.90.refs_25_
  292.4 144.8 %back.1 = (f32[256,768]{1,0:T(8,128)}, f32[256,768]{1,0:T(8,128)}, f32[256,768]{1,0:T(8,128)}, f32[64,1024]{1,0:T(8,128)}, f32[64,256]{1,0:T(8,128)}, /*index=5*...) custom-call(bf16[3,32,2048]{2,1,0:T(8,128)(2,1)} %convert_element_ty, ...), custom_call_target="tpu_custom_call" | custom-call | tf_op jit(solution)/shard_map/back/pallas_call | solution.py:696
  437.2 1.4 slice_bitcast_fusion
  438.7 1.3 slice_bitcast_fusion.3
  439.9 1.3 divide_reduce_fusion
  441.3 2.1 add.120
  443.4 1.0 add.119
  444.4 0.6 fusion.26
  445.1 0.6 copy.67
  445.7 0.7 copy.92
  446.4 0.7 copy.93
  447.1 0.9 copy.94
  448.0 0.9 copy.95
  448.9 0.9 copy.96
  (104 shorter events, 6.8 us)
Async XLA Ops:
  7.2 3.6 copy-start
  7.2 128.3 %reduce-scatter.2.cloned.1.call-start = ((), (), s32[]{:S(2)}) async-start(), calls=%async_computation.1 | async-start | bytes 1966080 | tf_op jit(solution)/shard_map/reduce_scatter | solution.py:1029
  9.0 2.3 copy-start.23
  11.2 4.6 %copy-start.1 = (bf16[3,128,2048]{2,1,0:T(8,128)(2,1)}, bf16[3,128,2048]{2,1,0:T(8,128)(2,1)S(1)}, u32[]{:S(2)}) copy-start(bf16[3,128,2048]{2,1,0:T(8,128)(2,1)S(1)} %multiply_convert_fusion) | copy-start | bytes 4718596
  15.8 1.1 copy-start.3
  17.0 0.7 copy-start.34
  18.2 0.5 copy-start.28
  21.4 2.7 copy-start.35
  21.9 3.0 copy-start.33
  21.9 3.1 copy-start.32
  24.1 34.5 %copy-start.10 = (f32[384,128]{1,0:T(8,128)}, f32[384,128]{1,0:T(8,128)S(1)}, u32[]{:S(2)}) copy-start(f32[384,128]{1,0:T(8,128)S(1)} %get-tuple-element.133.refs_14_) | copy-start | bytes 589828
  24.8 34.6 %copy-start.22 = (s32[3,1024]{1,0:T(4,128)S(1)}, s32[3,1024]{1,0:T(4,128)}, u32[]{:S(2)}) copy-start(s32[3,1024]{1,0:T(4,128)} %param.18) | copy-start | bytes 36868
  26.0 0.6 copy-start.13
  26.0 0.8 copy-start.19
  59.8 3.4 copy-start.6
  65.7 4.2 copy-start.2
  65.7 4.2 copy-start.12
  69.9 34.2 %copy-start.25 = (f32[3,128,8]{1,2,0:T(8,128)}, f32[3,128,8]{1,2,0:T(8,128)S(1)}, u32[]{:S(2)}) copy-start(f32[3,128,8]{1,2,0:T(8,128)S(1)} %log_add_fusion) | copy-start | bytes 36868
  100.2 3.8 copy-start.9
  107.2 2.1 copy-start.26
  107.2 2.1 copy-start.27
  107.2 2.2 copy-start.36
  107.2 2.2 copy-start.30
  110.1 3.8 copy-start.7
  113.9 1.3 copy-start.29
  113.9 1.3 copy-start.14
  115.3 1.4 copy-start.4
  115.3 1.9 copy-start.8
  292.4 148.8 %copy-start.11 = (f32[96,2048]{1,0:T(8,128)S(1)}, f32[96,2048]{1,0:T(8,128)}, u32[]{:S(2)}) copy-start(f32[96,2048]{1,0:T(8,128)} %get-tuple-element.32) | copy-start | bytes 2359300
  437.2 6.1 %copy-start.5 = (f32[3,32,2048]{2,1,0:T(8,128)S(1)}, f32[3,32,2048]{2,1,0:T(8,128)}, u32[]{:S(2)}) copy-start(f32[3,32,2048]{2,1,0:T(8,128)} %convert_add_fusion) | copy-start | bytes 2359300
  437.2 6.1 %copy-start.18 = (f32[96,2048]{1,0:T(8,128)S(1)}, f32[96,2048]{1,0:T(8,128)}, u32[]{:S(2)}) copy-start(f32[96,2048]{1,0:T(8,128)} %get-tuple-element.39) | copy-start | bytes 2359300
  443.4 1.0 copy-start.24
  443.4 1.6 copy-start.31
  443.4 2.3 copy-start.21
  443.4 3.0 copy-start.20
  443.4 3.7 copy-start.17
  444.4 3.6 copy-start.16
  447.1 1.8 copy-start.15
Sparse Core Ops, SparseCore 0:
  107.3 28.1 reduce-scatter.1

commit v4 on v3

--- a/solution.py
+++ b/solution.py
@@ -4,6 +4,7 @@
 
 import jax
 import jax.numpy as jnp
+import numpy as np
 from jax import lax
 from jax.experimental import pallas as pl
 from jax.experimental.pallas import tpu as pltpu
@@ -13,6 +14,7 @@
 MESH = pl.DeviceIdType.MESH
 VMEM = pl.BlockSpec(memory_space=pltpu.VMEM)
 ANY = pl.BlockSpec(memory_space=pl.ANY)
+SMEM = pl.BlockSpec(memory_space=pltpu.SMEM)
 
 
 epsilon = 1e-06
@@ -21,21 +23,16 @@
 masked_value = -1e30
 
 
-def rms_scale(values, factor):
-    return values * lax.rsqrt(jnp.mean(values * values, axis=-1, keepdims=True) + epsilon) * factor
-
-
-def turn(values):
-    middle = values.shape[-1] // 2
-    return jnp.concatenate([-values[..., middle:], values[..., :middle]], axis=-1)
-
-
-def rotary(offset, amount):
-    inverse = 1.0 / rope_base ** (jnp.arange(0, HEAD_SIZE, 2, dtype=jnp.float32) / HEAD_SIZE)
-    position = (offset + jnp.arange(amount, dtype=jnp.int32)).astype(jnp.float32)
-    angle = position[:, None] * inverse[None, :]
-    angle = jnp.concatenate([angle, angle], axis=-1)
-    return (jnp.cos(angle), jnp.sin(angle))
+def rotary():
+    inverse = 1.0 / rope_base ** (np.arange(0, HEAD_SIZE, 2) / HEAD_SIZE)
+    angle = np.arange(1024)[:, None] * inverse[None, :]
+    cosine = np.concatenate([np.cos(angle), np.cos(angle)], axis=-1)
+    sine = np.concatenate([-np.sin(angle), np.sin(angle)], axis=-1)
+    shape = (8, 128, HEAD_SIZE)
+    return (
+        jnp.asarray(cosine.reshape(shape), jnp.float32),
+        jnp.asarray(sine.reshape(shape), jnp.float32),
+    )
 
 
 def contract_last(left, right):
@@ -335,6 +332,9 @@
     low, full = jnp.bfloat16, jnp.float32
     score_scale = HEAD_SIZE ** (-0.5)
     me = Place()
+    net = Net(r.send, r.recv, r.here)
+    fetch = Fetch(net)
+    fetch.start("hidden", r.hidden, r.hidden_held)
     greet(
         [
             me.at(x=me.x_by(1)),
@@ -345,7 +345,6 @@
         ]
         + [one[4] for one in peers(me)]
     )
-    net = Net(r.send, r.recv, r.here)
 
     branch, whole = r.branch, r.whole
     above, below = me.at(y=me.y_by(1)), me.at(y=me.y_by(3))
@@ -368,11 +367,19 @@
     )
     for task in (gate, up, down):
         next(task)
-
-    hidden, inverse = r.hidden, r.inverse
+    fetch.start("pair", r.pair, r.pair_held)
+    fetch.start("query", r.query, r.query_held)
+    fetch.start("query_raw", r.query_raw, r.query_raw_held)
+    fetch.start("cosine", r.cosine.at[me.context], r.cosine_held)
+    fetch.start("sine", r.sine.at[me.context], r.sine_held)
+    fetch.start("mixed", r.mixed, r.mixed_held)
+    fetch.start("w_key", r.w_key, r.key_weight)
+    fetch.start("w_value", r.w_value, r.value_weight)
+
+    hidden, inverse = fetch.hidden, r.inverse
     for s in range(3):
         rows = slice(s * 128, s * 128 + 128)
-        values = hidden[rows, :].astype(full)
+        values = hidden[s].astype(full)
         root = lax.rsqrt(jnp.mean(values * values, axis=-1, keepdims=True) + epsilon)
         inverse[rows, :] = jnp.broadcast_to(root, (128, 128))
 
@@ -388,7 +395,7 @@
     far_above.wait_recv()
     far_below.wait_recv()
 
-    heads_grad, mixed = r.heads_grad, r.mixed
+    heads_grad = r.heads_grad
 
     def heads_step(step, carry):
         columns = pl.ds(pl.multiple_of(step * 256, 256), 256)
@@ -407,23 +414,19 @@
     ]
     home_own = net.load(produced.at[me.dp, me.y], home.at[mine])
 
-    query, query_raw, pair = r.query, r.query_raw, r.pair
-    cosine, sine = r.cosine, r.sine
-    gain_query, gain_key = r.gain_query, r.gain_key
+    query, query_raw, pair = fetch.query, fetch.query_raw, fetch.pair
+    cosine, sine, mixed = fetch.cosine, fetch.sine, fetch.mixed
+    gain_query, gain_key = r.head_gains[0:1, :], r.head_gains[1:2, :]
     bias, key_sum, value_sum = r.bias, r.key_sum, r.value_sum
     pair_grad, gain_part = r.pair_grad, r.gain_part
     gain_part[...] = jnp.zeros((8, 128), full)
 
     def rope_back(gradient):
-        return gradient * cosine[...] + turned(gradient) * sine[...]
+        return gradient * cosine[...] - turned(gradient) * sine[...]
 
     def attend(s):
         here = pl.ds(s * 128, 128)
-        spot = me.context * 128 + lax.broadcasted_iota(jnp.int32, (128, 1024), 0)
-        allowed = (column_of(r.seg_query[s]) == r.seg_key[s]) & (
-            lax.broadcasted_iota(jnp.int32, (128, 1024), 1) <= spot
-        )
-        bias[...] = jnp.where(allowed, 0.0, masked_value)
+        bias[...] = mask_bias(me, r.segments, s)
         key_sum[...] = jnp.zeros_like(key_sum)
         value_sum[...] = jnp.zeros_like(value_sum)
 
@@ -454,7 +457,7 @@
                 grad, part = norm_back(
                     rope_back(turned_grad[half * 128 : half * 128 + 128]),
                     query_raw[here, run],
-                    gain_query[...],
+                    gain_query,
                 )
                 heads_grad[here, run] = grad.astype(low)
                 gain_part[0:1, :] += part
@@ -476,11 +479,12 @@
     next(pairs)
 
     query_low = heads_grad
-    gain_attn = r.gain_attn
+
+    def own_input(columns):
+        return hidden[:, :, columns].reshape(384, 256).astype(full)
 
     def normed(columns):
-        values = hidden[:, columns].astype(full)
-        return (values * inverse[:, 0:1] * gain_attn[:, columns]).astype(low)
+        return (own_input(columns) * inverse[:, 0:1] * r.gains[0:1, columns]).astype(low)
 
     def whole_part(columns):
         return whole[:, :, :, columns].reshape(384, 256)
@@ -521,7 +525,7 @@
     next(pairs, None)
     for s in range(3):
         rows = slice(s * 128, s * 128 + 128)
-        grad, part = norm_back(rope_back(pair_out[0, s]), key_raw[rows, :], gain_key[...])
+        grad, part = norm_back(rope_back(pair_out[0, s]), key_raw[rows, :], gain_key)
         gain_part[1:2, :] += part
         pair_low[rows, :128] = grad.astype(low)
         pair_low[rows, 128:] = pair_out[1, s].astype(low)
@@ -529,15 +533,16 @@
     load_query.wait()
     net.sent(far_above)
     net.sent(far_below)
+    w_key, w_value = fetch.w_key, fetch.w_value
     small = r.small
     normed_part = r.normed_part
 
     def normed_step(step, carry):
         columns = pl.ds(pl.multiple_of(step * 256, 256), 256)
         made = contract_last(query_low[...], weight[columns, :])
-        made = made + contract_last(pair_low[:, :128], r.w_key[columns, :])
-        made = made + contract_last(pair_low[:, 128:], r.w_value[columns, :])
-        normal = hidden[:, columns].astype(full) * inverse[:, 0:1]
+        made = made + contract_last(pair_low[:, :128], w_key[columns, :])
+        made = made + contract_last(pair_low[:, 128:], w_value[columns, :])
+        normal = own_input(columns) * inverse[:, 0:1]
         normed_part[:, columns] = jnp.sum(made * normal, axis=0, keepdims=True)
         whole[:, :, :, columns] = made.astype(low).reshape(3, 4, 32, 256)
         return carry
@@ -578,8 +583,8 @@
 
     next(normed_sum, None)
     for s in range(3):
-        rows = pl.ds(pl.multiple_of(s * 128 + me.y * 32, 32), 32)
-        grad, _ = norm_back(normed_out[s], hidden[rows, :].astype(full), gain_attn[...])
+        rows = pl.ds(pl.multiple_of(me.y * 32, 32), 32)
+        grad, _ = norm_back(normed_out[s], hidden[s, rows, :].astype(full), r.gains[0:1, :])
         normed_out[s] = grad
 
     rest(out_w, pair_w, smalls, down, gate, up, query_w)
@@ -637,6 +642,15 @@
         moe_out=(96, 2048),
     )
     scratch = dict(
+        hidden_held=pltpu.VMEM((3, 128, 2048), low),
+        pair_held=pltpu.VMEM((2, 3, 1024, 128), low),
+        query_held=pltpu.VMEM((384, 1024), low),
+        query_raw_held=pltpu.VMEM((384, 1024), full),
+        cosine_held=pltpu.VMEM((128, 128), full),
+        sine_held=pltpu.VMEM((128, 128), full),
+        mixed_held=pltpu.VMEM((384, 1024), low),
+        key_weight=pltpu.VMEM((2048, 128), low),
+        value_weight=pltpu.VMEM((2048, 128), low),
         whole=pltpu.VMEM((3, 4, 32, 2048), low),
         weight=pltpu.VMEM((2048, 1024), low),
         inverse=pltpu.VMEM((384, 128), full),
@@ -688,80 +702,53 @@
         out_w_last=None,
         send=pltpu.SemaphoreType.DMA((104,)),
         recv=pltpu.SemaphoreType.DMA((104,)),
-        here=pltpu.SemaphoreType.DMA((20,)),
+        here=pltpu.SemaphoreType.DMA((28,)),
     )
     dense = dense_slots(1024, (2, 2)) + dense_slots(256, (2, 2)) + dense_slots(1024, (4,))
     scratch = {name: one or dense.pop(0) for name, one in scratch.items()}
-    names = list(far) + list(near) + list(outs) + list(dict(home=0)) + list(scratch)
-    results = pl.pallas_call(
-        functools.partial(back_kernel, names),
-        out_shape=[jax.ShapeDtypeStruct(size, full) for size in outs.values()]
-        + [jax.ShapeDtypeStruct((768, 2048), low)],
-        in_specs=[ANY] * len(far) + [VMEM] * len(near),
-        out_specs=[VMEM] * len(outs) + [ANY],
-        scratch_shapes=list(scratch.values()),
-        compiler_params=pltpu.CompilerParams(
-            collective_id=0, has_side_effects=True, vmem_limit_bytes=62 << 20
-        ),
-        name="back",
-    )(*far.values(), *near.values())
-    return types.SimpleNamespace(**dict(zip(outs, results[:-1], strict=True)))
-
-
-def moe_kernel(
-    after,
-    cotangent,
-    gain,
-    ids,
-    gates,
-    capacity,
-    w_gate,
-    w_up,
-    w_down,
-    after_grad,
-    gain_part,
-    gate_grad,
-    produced,
-    table,
-    full_gate,
-    full_up,
-    full_down,
-    rows,
-    sending,
-    sending_grad,
-    info,
-    info_in,
-    local,
-    grads,
-    act,
-    gate_back,
-    up_back,
-    back,
-    home,
-    dots,
-    dots_in,
-    send,
-    recv,
-):
+    outs = {name: jax.ShapeDtypeStruct(size, full) for name, size in outs.items()}
+    far_outs = dict(home=jax.ShapeDtypeStruct((768, 2048), low))
+    return call(back_kernel, 0, far, near, outs, far_outs, scratch)
+
+
+class Fetch:
+    def __init__(self, net):
+        self.net, self.waiting, self.held = net, {}, {}
+
+    def start(self, name, source, target):
+        self.waiting[name] = self.net.load(source, target)
+        self.held[name] = target
+
+    def __getattr__(self, name):
+        if name in self.waiting:
+            self.waiting.pop(name).wait()
+        return self.held[name]
+
+
+def token_table(ids, gates, capacity, table, info):
     low, full = jnp.bfloat16, jnp.float32
-    me = Place()
-    greet([one[4] for one in peers(me)])
-    net = Net(send, recv)
-
-    expert = lax.broadcasted_iota(jnp.int32, (16, 128), 0)
-    chosen = jnp.zeros((16, 128), full)
-    share = jnp.zeros((16, 128), full)
+    expert = lax.broadcasted_iota(jnp.int32, (96, 128), 1)
+    routes = ids[...].reshape(96, 8)
+    values = gates[...].reshape(96, 8)
+    chosen = jnp.zeros((96, 128), full)
+    share = jnp.zeros((96, 128), full)
+    limit = jnp.zeros((1, 128), full)
     for k in range(8):
-        named = ids[k : k + 1, :] == expert
+        named = routes[:, k : k + 1] == expert
         chosen = chosen + jnp.where(named, 1.0, 0.0)
-        share = share + jnp.where(named, gates[k : k + 1, :], 0.0)
-    earlier = lax.broadcasted_iota(jnp.int32, (128, 128), 0) < lax.broadcasted_iota(
-        jnp.int32, (128, 128), 1
+        share = share + jnp.where(named, values[:, k : k + 1], 0.0)
+    for e in range(16):
+        limit = jnp.where(expert[0:1] == e, capacity[e].astype(full), limit)
+    earlier = lax.broadcasted_iota(jnp.int32, (96, 96), 1) < lax.broadcasted_iota(
+        jnp.int32, (96, 96), 0
     )
     before = jnp.dot(
-        chosen.astype(low), jnp.where(earlier, 1.0, 0.0).astype(low), preferred_element_type=full
-    )
-    slot = jnp.where((chosen > 0.0) & (before < capacity[...]), before, -1.0)
+        jnp.where(earlier, 1.0, 0.0).astype(low), chosen.astype(low), preferred_element_type=full
+    )
+    slot = jnp.where((chosen > 0.0) & (before < limit), before, -1.0)
+    none = jnp.full((32, 128), -1.0, full)
+    slot = jnp.concatenate([slot, none], axis=0).T
+    share = jnp.concatenate([share, none], axis=0).T
     spot = lax.broadcasted_iota(jnp.int32, (48, 128), 0).astype(full)
     for e in range(16):
         mask = jnp.where(slot[e : e + 1, :] == spot, 1.0, 0.0)
@@ -770,47 +757,56 @@
             [slot[e : e + 1, :], share[e : e + 1, :], jnp.zeros((6, 128), full)], axis=0
         )
 
-    def dispatch(sender):
-        for a, b, dp, y, device in peers(me):
-            if b == 1:
-                rest = table[pl.ds(pl.multiple_of(dp * 192, 192), 192), :]
-                columns = 512
-                for step in range(2048 // columns):
-                    run = slice(step * columns, (step + 1) * columns)
-                    picked = jnp.dot(rest, rows[:, run], preferred_element_type=full)
-                    sender[dp, :, :, run] = picked.astype(low).reshape(4, 48, columns)
-            yield a, b, dp, y, device
-
-    told, came, grad_came = {}, {}, {}
+
+def dispatch(me, table, rows, sender):
     for a, b, dp, y, device in peers(me):
-        told[a, b] = net.copy(info.at[dp, y], info_in.at[me.dp, me.y], device)
-    info_in[me.dp, me.y] = info[me.dp, me.y]
-    values = after[...]
+        if b == 1:
+            rest = table[pl.ds(pl.multiple_of(dp * 192, 192), 192), :]
+            columns = 512
+            for step in range(2048 // columns):
+                run = slice(step * columns, (step + 1) * columns)
+                picked = jnp.dot(rest, rows[:, run], preferred_element_type=jnp.float32)
+                sender[dp, :, :, run] = picked.astype(jnp.bfloat16).reshape(4, 48, columns)
+        yield a, b, dp, y, device
+
+
+def moe_kernel(names, *refs):
+    r = types.SimpleNamespace(**dict(zip(names, refs, strict=True)))
+    low, full = jnp.bfloat16, jnp.float32
+    me = Place()
+    net = Net(r.send, r.recv, r.here)
+    fetch = Fetch(net)
+    fetch.start("w_gate", r.w_gate, r.gate_weight)
+    fetch.start("w_up", r.w_up, r.up_weight)
+    fetch.start("grads", r.grads, r.grads_held)
+    fetch.start("w_down", r.w_down, r.down_weight)
+    greet([one[4] for one in peers(me)])
+    rows, sending, local, table = r.rows, r.sending, r.local, r.table
+    values = r.after[...]
     inverse = lax.rsqrt(jnp.mean(values * values, axis=-1, keepdims=True) + epsilon)
+    gain = r.gains[1:2, :]
     rows[96:, :] = jnp.zeros((32, 2048), low)
-    rows[:96, :] = (values * inverse * gain[...]).astype(low)
-    for a, b, dp, y, device in dispatch(sending):
+    rows[:96, :] = (values * inverse * gain).astype(low)
+    came = {}
+    for a, b, dp, y, device in dispatch(me, table, rows, sending):
         came[a, b] = net.copy(sending.at[dp, y], local.at[me.dp, me.y], device)
     local[me.dp, me.y] = sending[me.dp, me.y]
-    rows[:96, :] = cotangent[...]
-    for a, b, dp, y, device in dispatch(sending_grad):
-        grad_came[a, b] = net.copy(sending_grad.at[dp, y], grads.at[me.dp, me.y], device)
-    grads[me.dp, me.y] = sending_grad[me.dp, me.y]
-
+
+    act, gate_back, up_back, back, home = r.act, r.gate_back, r.up_back, r.back, r.home
+    w_gate, w_up, grads, w_down = fetch.w_gate, fetch.w_up, fetch.grads, fetch.w_down
+    spot = lax.broadcasted_iota(jnp.int32, (48, 128), 0).astype(full)
     back_came, dots_came = {}, {}
     for a in (0, 1, 2, 3):
         group = peer(me, a, 0)[0]
         for b in range(4):
             if a or b:
-                told[a, b].wait_recv()
                 came[a, b].wait_recv()
-                grad_came[a, b].wait_recv()
         masks, shares = [], []
         for y in range(4):
-            mask = info_in[group, y, 0:1, :] == spot
+            mask = r.info_in[group, y, 0:1, :] == spot
             masks.append(mask)
             shares.append(
-                jnp.sum(jnp.where(mask, info_in[group, y, 1:2, :], 0.0), axis=1, keepdims=True)
+                jnp.sum(jnp.where(mask, r.info_in[group, y, 1:2, :], 0.0), axis=1, keepdims=True)
             )
         shared = jnp.concatenate(shares, axis=0)
 
@@ -835,7 +831,9 @@
         def outer(step, dot, group=group, shared=shared):
             columns = pl.ds(pl.multiple_of(step * 256, 256), 256)
             made = contract_last(act[group], w_down[columns, :]).astype(low).astype(full)
-            produced[group, :, :, columns] = (made * shared).astype(low).reshape(4, 48, 256)
+            r.produced_held[group, :, :, columns] = (
+                (made * shared).astype(low).reshape(4, 48, 256)
+            )
             incoming = grads[group, :, :, columns].reshape(192, 256).astype(full)
             dot = dot + jnp.sum(made * incoming, axis=1, keepdims=True)
             grads[group, :, :, columns] = (incoming * shared).astype(low).reshape(4, 48, 256)
@@ -850,92 +848,346 @@
             line = jnp.sum(
                 jnp.where(masks[y], dot[y * 48 : y * 48 + 48], 0.0), axis=0, keepdims=True
             )
-            dots[group, y] = jnp.broadcast_to(line, (8, 128))
+            r.dots[group, y] = jnp.broadcast_to(line, (8, 128))
         for b in (2, 1, 3, 0):
             if a or b:
                 dp, y, device = peer(me, a, b)
                 back_came[a, b] = net.copy(back.at[dp, y], home.at[me.dp, me.y], device)
-                dots_came[a, b] = net.copy(dots.at[dp, y], dots_in.at[me.dp, me.y], device)
+                dots_came[a, b] = net.copy(r.dots.at[dp, y], r.dots_in.at[me.dp, me.y], device)
     home[me.dp, me.y] = back[me.dp, me.y]
-    dots_in[me.dp, me.y] = dots[me.dp, me.y]
+    r.dots_in[me.dp, me.y] = r.dots[me.dp, me.y]
+    written = [net.load(r.produced_held, r.produced)]
 
     def weigh(step, carry):
         columns = pl.ds(pl.multiple_of(step * 256, 256), 256)
         entered = local[:, :, :, columns].reshape(768, 256)
-        full_gate[columns, :] = contract_first(entered, gate_back[...].reshape(768, 768)).astype(low)
-        full_up[columns, :] = contract_first(entered, up_back[...].reshape(768, 768)).astype(low)
+        r.gate_held[columns, :] = contract_first(entered, gate_back[...].reshape(768, 768)).astype(
+            low
+        )
+        r.up_held[columns, :] = contract_first(entered, up_back[...].reshape(768, 768)).astype(low)
         incoming = grads[:, :, :, columns].reshape(768, 256)
-        full_down[columns, :] = contract_first(incoming, act[...].reshape(768, 768)).astype(low)
+        r.down_held[columns, :] = contract_first(incoming, act[...].reshape(768, 768)).astype(low)
         return carry
 
     lax.fori_loop(0, 8, weigh, 0)
+    written += [
+        net.load(r.gate_held, r.full_gate),
+        net.load(r.up_held, r.full_up),
+        net.load(r.down_held, r.full_down),
+    ]
+
+    for a, b, *_ in peers(me):
+        dots_came[a, b].wait_recv()
+    lines = [r.dots_in[e // 4, e % 4, 0:1, :] for e in range(16)]
+    by_token = jnp.concatenate(lines + [jnp.zeros((112, 128), full)], axis=0).T[:96]
+    expert = lax.broadcasted_iota(jnp.int32, (96, 128), 1)
+    routes = r.ids[...].reshape(96, 8)
+    picked = [
+        jnp.sum(jnp.where(routes[:, k : k + 1] == expert, by_token, 0.0), axis=1, keepdims=True)
+        for k in range(8)
+    ]
+    r.gate_grad[...] = jnp.concatenate(picked, axis=1).reshape(3, 32, 8)
 
     for a, b, *_ in peers(me):
         back_came[a, b].wait_recv()
-        dots_came[a, b].wait_recv()
-    chosen_dots = [jnp.zeros((1, 128), full) for k in range(8)]
-    for e in range(16):
-        line = dots_in[e // 4, e % 4, 0:1, :]
-        for k in range(8):
-            chosen_dots[k] = chosen_dots[k] + jnp.where(ids[k : k + 1, :] == e, line, 0.0)
-    gate_grad[...] = jnp.concatenate(chosen_dots, axis=0)
+    after_grad = r.after_grad
 
     def keep(columns, total):
         after_grad[:, columns] = total
 
     gather_rows(table, home, keep)
     gradient = after_grad[...]
-    values = after[...]
-    inverse = lax.rsqrt(jnp.mean(values * values, axis=-1, keepdims=True) + epsilon)
-    normal = values * inverse
-    gain_part[...] = jnp.sum(gradient * normal, axis=0, keepdims=True)
-    scaled = gradient * gain[...]
-    mean = jnp.mean(scaled * normal, axis=-1, keepdims=True)
-    after_grad[...] = cotangent[...].astype(full) + inverse * (scaled - normal * mean)
+    moe_part, gain_part = norm_back(gradient, r.after[...], gain)
+    r.gain_part[...] = gain_part
+    result = r.cotangent[...].reshape(96, 2048).astype(full) + moe_part
+    after_grad[...] = result
+    r.branch[...] = result.astype(low).reshape(3, 32, 2048)
+    for one in written:
+        one.wait()
     net.finish()
 
 
-def moe(after, cotangent, gain, ids, gates, capacity, w_gate, w_up, w_down):
+def moe(far, near):
     low, full = jnp.bfloat16, jnp.float32
-    copies = 75
-    shape = jax.ShapeDtypeStruct
-    return pl.pallas_call(
-        moe_kernel,
-        out_shape=[
-            shape((96, 2048), full),
-            shape((1, 2048), full),
-            shape((8, 128), full),
-            shape((4, 4, 48, 2048), low),
-            shape((768, 128), low),
-            shape((2048, 768), low),
-            shape((2048, 768), low),
-            shape((2048, 768), low),
-        ],
-        in_specs=[VMEM] * 9,
-        out_specs=[VMEM] * 8,
-        scratch_shapes=[
-            pltpu.VMEM((128, 2048), low),
-            pltpu.VMEM((4, 4, 48, 2048), low),
-            pltpu.VMEM((4, 4, 48, 2048), low),
-            pltpu.VMEM((4, 4, 8, 128), full),
-            pltpu.VMEM((4, 4, 8, 128), full),
-            pltpu.VMEM((4, 4, 48, 2048), low),
-            pltpu.VMEM((4, 4, 48, 2048), low),
-            pltpu.VMEM((4, 192, 768), low),
-            pltpu.VMEM((4, 192, 768), low),
-            pltpu.VMEM((4, 192, 768), low),
-            pltpu.VMEM((4, 4, 48, 2048), low),
-            pltpu.VMEM((4, 4, 48, 2048), low),
-            pltpu.VMEM((4, 4, 8, 128), full),
-            pltpu.VMEM((4, 4, 8, 128), full),
-            pltpu.SemaphoreType.DMA((copies,)),
-            pltpu.SemaphoreType.DMA((copies,)),
-        ],
+    rows = (4, 4, 48, 2048)
+    outs = dict(
+        after_grad=jax.ShapeDtypeStruct((96, 2048), full),
+        branch=jax.ShapeDtypeStruct((3, 32, 2048), low),
+        gain_part=jax.ShapeDtypeStruct((1, 2048), full),
+        gate_grad=jax.ShapeDtypeStruct((3, 32, 8), full),
+    )
+    far_outs = dict(
+        produced=jax.ShapeDtypeStruct(rows, low),
+        full_gate=jax.ShapeDtypeStruct((2048, 768), low),
+        full_up=jax.ShapeDtypeStruct((2048, 768), low),
+        full_down=jax.ShapeDtypeStruct((2048, 768), low),
+    )
+    scratch = dict(
+        rows=pltpu.VMEM((128, 2048), low),
+        sending=pltpu.VMEM(rows, low),
+        local=pltpu.VMEM(rows, low),
+        grads_held=pltpu.VMEM(rows, low),
+        produced_held=pltpu.VMEM(rows, low),
+        back=pltpu.VMEM(rows, low),
+        home=pltpu.VMEM(rows, low),
+        gate_weight=pltpu.VMEM((2048, 768), low),
+        up_weight=pltpu.VMEM((2048, 768), low),
+        down_weight=pltpu.VMEM((2048, 768), low),
+        gate_held=pltpu.VMEM((2048, 768), low),
+        up_held=pltpu.VMEM((2048, 768), low),
+        down_held=pltpu.VMEM((2048, 768), low),
+        act=pltpu.VMEM((4, 192, 768), low),
+        gate_back=pltpu.VMEM((4, 192, 768), low),
+        up_back=pltpu.VMEM((4, 192, 768), low),
+        dots=pltpu.VMEM((4, 4, 8, 128), full),
+        dots_in=pltpu.VMEM((4, 4, 8, 128), full),
+        send=pltpu.SemaphoreType.DMA((45,)),
+        recv=pltpu.SemaphoreType.DMA((45,)),
+        here=pltpu.SemaphoreType.DMA((8,)),
+    )
+    return call(moe_kernel, 1, far, near, outs, far_outs, scratch)
+
+
+def call(kernel, number, far, near, outs, far_outs, scratch):
+    names = list(far) + list(near) + list(outs) + list(far_outs) + list(scratch)
+    shapes = {**outs, **far_outs}
+    results = pl.pallas_call(
+        functools.partial(kernel, names),
+        out_shape=list(shapes.values()),
+        in_specs=[ANY] * len(far)
+        + [SMEM if one.ndim == 1 else VMEM for one in near.values()],
+        out_specs=[VMEM] * len(outs) + [ANY] * len(far_outs),
+        scratch_shapes=list(scratch.values()),
         compiler_params=pltpu.CompilerParams(
-            collective_id=1, has_side_effects=True, vmem_limit_bytes=60 << 20
+            collective_id=number, has_side_effects=True, vmem_limit_bytes=62 << 20
         ),
-        name="moe",
-    )(after, cotangent, gain, ids, gates, capacity, w_gate, w_up, w_down)
+        name=kernel.__name__,
+    )(*far.values(), *near.values())
+    return types.SimpleNamespace(**dict(zip(shapes, results, strict=True)))
+
+
+def front_kernel(names, *refs):
+    r = types.SimpleNamespace(**dict(zip(names, refs, strict=True)))
+    low, full = jnp.bfloat16, jnp.float32
+    score_scale = HEAD_SIZE ** (-0.5)
+    me = Place()
+    net = Net(r.send, r.recv, r.here)
+    fetch = Fetch(net)
+    fetch.start("hidden", r.hidden, r.hidden_held)
+    fetch.start("w_pair", r.w_key, r.key_weight)
+    fetch.start("w_value", r.w_value, r.value_weight)
+    fetch.start("cosine", r.cosine.at[me.context], r.cosine_held)
+    fetch.start("sine", r.sine.at[me.context], r.sine_held)
+    fetch.start("w_query", r.w_query, r.query_weight)
+    fetch.start("cotangent", r.cotangent, r.cotangent_held)
+    fetch.start("w_out", r.w_out, r.out_weight)
+    beside = me.at(z=me.z + 1 - 2 * me.z_lo)
+    right, left = me.at(x=me.x_by(1)), me.at(x=me.x_by(3))
+    greet([right, left, beside] + [one[4] for one in peers(me)])
+
+    hidden, normed = fetch.hidden, r.normed
+    for s in range(3):
+        values = hidden[s].astype(full)
+        root = lax.rsqrt(jnp.mean(values * values, axis=-1, keepdims=True) + epsilon)
+        normed[s * 128 : s * 128 + 128, :] = (values * root * r.gains[0:1, :]).astype(low)
+
+    def rope(values):
+        cosine = jnp.concatenate([fetch.cosine[...]] * 3, axis=0)
+        sine = jnp.concatenate([fetch.sine[...]] * 3, axis=0)
+        return values * cosine + turned(values) * sine
+
+    def head_norm(raw, gain):
+        return raw * lax.rsqrt(jnp.mean(raw * raw, axis=-1, keepdims=True) + epsilon) * gain
+
+    pair, key_raw = r.pair_held, r.key_raw
+    made = jnp.dot(normed[...], fetch.w_pair[...], preferred_element_type=full)
+    key_raw[...] = made
+    keys = rope(head_norm(made, r.head_gains[1:2, :])).astype(low)
+    values = jnp.dot(normed[...], fetch.w_value[...], preferred_element_type=full).astype(low)
+    own = pl.ds(pl.multiple_of(me.context * 128, 128), 128)
+    pair[0, :, own, :] = keys.reshape(3, 128, 128)
+    pair[1, :, own, :] = values.reshape(3, 128, 128)
+
+    def block(x, z_lo):
+        return pl.ds(pl.multiple_of((x * 2 + z_lo) * 128, 128), 128)
+
+    def piece(x, z_lo, half=None):
+        rows = block(x, z_lo)
+        return pair.at[:, :, rows, :] if half is None else pair.at[half, :, rows, :]
+
+    def pass_on(view, device):
+        return net.copy(view, view, device)
+
+    own_z, other_z = me.z_lo, 1 - me.z_lo
+    from_z = pass_on(piece(me.x, own_z), beside)
+    from_left = [pass_on(piece(me.x, own_z), right)]
+    from_right = [pass_on(piece(me.x, own_z), left)]
+
+    token_table(r.ids, r.gates, r.capacity, r.table, r.info)
+    arrivals = []
+    for a, b, dp, y, device in peers(me):
+        arrivals.append(net.copy(r.info.at[dp, y], r.info_in.at[me.dp, me.y], device))
+    r.info_in[me.dp, me.y] = r.info[me.dp, me.y]
+    rows = r.rows
+    rows[96:, :] = jnp.zeros((32, 2048), low)
+    rows[:96, :] = fetch.cotangent[...].reshape(96, 2048)
+    from_z.wait_recv()
+    from_left.append(pass_on(piece(me.x, other_z), right))
+    from_right.append(pass_on(piece(me.x, other_z), left))
+    for a, b, dp, y, device in dispatch(me, r.table, rows, r.sending):
+        arrivals.append(net.copy(r.sending.at[dp, y], r.grads.at[me.dp, me.y], device))
+    own_grads = net.load(r.sending.at[me.dp, me.y], r.grads.at[me.dp, me.y])
+
+    w_query, query, query_raw = fetch.w_query, r.query_held, r.query_raw_held
+
+    def project(step, carry):
+        columns = pl.ds(pl.multiple_of(step * 256, 256), 256)
+        made = jnp.dot(normed[...], w_query[:, columns], preferred_element_type=full)
+        query_raw[:, columns] = made
+        for half in range(2):
+            run = pl.ds(pl.multiple_of(step * 256 + half * 128, 128), 128)
+            one = head_norm(made[:, half * 128 : half * 128 + 128], r.head_gains[0:1, :])
+            query[:, run] = rope(one).astype(low)
+        return carry
+
+    lax.fori_loop(0, 4, project, 0)
+    written = [net.load(query, r.query), net.load(query_raw, r.query_raw)]
+    far = [[], []]
+    for spot, zs in enumerate((own_z, other_z)):
+        from_left[spot].wait_recv()
+        far[0].append(pass_on(piece(me.x_by(3), zs, 0), right))
+        from_right[spot].wait_recv()
+        far[1].append(pass_on(piece(me.x_by(1), zs, 1), left))
+    for one in far[0] + far[1]:
+        one.wait_recv()
+    written.append(net.load(pair, r.pair))
+
+    bias, peaks, mixed = r.bias, r.peak_rows, r.mixed_held
+    peaks[...] = jnp.full((8, 1, 128), -jnp.inf, full)
+    for s in range(3):
+        here = pl.ds(s * 128, 128)
+        bias[...] = mask_bias(me, r.segments, s)
+
+        def two_heads(step, carry, s=s, here=here):
+            columns = pl.ds(pl.multiple_of(step * 256, 256), 256)
+            both = query[here, columns]
+            q = jnp.concatenate([both[:, :128], both[:, 128:]], axis=0)
+            score = contract_last(q, pair[0, s]) * score_scale
+            score = score + jnp.concatenate([bias[...], bias[...]], axis=0)
+            highest = jnp.max(score, axis=-1, keepdims=True)
+            weight = jnp.exp(score - highest)
+            total = jnp.sum(weight, axis=-1, keepdims=True)
+            prob = (weight * (1.0 / total)).astype(low)
+            logs = highest + jnp.log(total)
+            heads = jnp.dot(prob, pair[1, s], preferred_element_type=full).astype(low)
+            for half in range(2):
+                part = slice(half * 128, half * 128 + 128)
+                head = step * 2 + half
+                run = pl.ds(pl.multiple_of(step * 256 + half * 128, 128), 128)
+                mixed[here, run] = heads[part]
+                r.log_sum[s * 8 + head] = row_of(logs[part])
+                top = jnp.max(highest[part], axis=0, keepdims=True)
+                peaks[head] = jnp.maximum(peaks[head], top)
+            return carry
+
+        lax.fori_loop(0, 4, two_heads, 0)
+    for head in range(8):
+        r.peaks[head : head + 1, :] = peaks[head]
+    written.append(net.load(mixed, r.mixed))
+
+    w_out, shares = fetch.w_out, r.shares
+
+    def branch_step(step, carry):
+        columns = pl.ds(pl.multiple_of(step * 256, 256), 256)
+        made = contract_last(mixed[...], w_out[columns, :])
+        shares[:, :, :, columns] = made.astype(low).reshape(3, 4, 32, 256)
+        return carry
+
+    lax.fori_loop(0, 8, branch_step, 0)
+    after = r.after_sum
+    ring = ring_reduce(
+        net,
+        me.at(y=me.y_by(1)),
+        me.at(y=me.y_by(3)),
+        lambda step, half: shares.at[:, me.y_by(step), :, pl.ds(half * 1024, 1024)],
+        r.branch_slots,
+        lambda half: after.at[:, :, pl.ds(half * 1024, 1024)],
+    )
+    for _ in ring:
+        pass
+    own_rows = pl.ds(pl.multiple_of(me.y * 32, 32), 32)
+    for s in range(3):
+        r.after[s * 32 : s * 32 + 32, :] = after[s] + hidden[s, own_rows, :].astype(full)
+    for one in arrivals:
+        one.wait_recv()
+    own_grads.wait()
+    for one in written:
+        one.wait()
+    net.finish()
+
+
+def row_of(column):
+    eye = lax.broadcasted_iota(jnp.int32, (128, 128), 0) == lax.broadcasted_iota(
+        jnp.int32, (128, 128), 1
+    )
+    return jnp.sum(jnp.where(eye, column, 0.0), axis=0, keepdims=True)
+
+
+def mask_bias(me, segments, s):
+    spot = me.context * 128 + lax.broadcasted_iota(jnp.int32, (128, 1024), 0)
+    own = segments[s : s + 1, pl.ds(pl.multiple_of(me.context * 128, 128), 128)]
+    document = column_of(own.astype(jnp.float32))
+    allowed = (document == segments[s : s + 1, :].astype(jnp.float32)) & (
+        lax.broadcasted_iota(jnp.int32, (128, 1024), 1) <= spot
+    )
+    return jnp.where(allowed, 0.0, masked_value)
+
+
+def front(far, near):
+    low, full = jnp.bfloat16, jnp.float32
+    rows = (4, 4, 48, 2048)
+    outs = dict(
+        key_raw=jax.ShapeDtypeStruct((384, 128), full),
+        log_sum=jax.ShapeDtypeStruct((24, 1, 128), full),
+        peaks=jax.ShapeDtypeStruct((8, 128), full),
+        after=jax.ShapeDtypeStruct((96, 2048), full),
+        table=jax.ShapeDtypeStruct((768, 128), low),
+        info_in=jax.ShapeDtypeStruct((4, 4, 8, 128), full),
+    )
+    far_outs = dict(
+        query=jax.ShapeDtypeStruct((384, 1024), low),
+        query_raw=jax.ShapeDtypeStruct((384, 1024), full),
+        pair=jax.ShapeDtypeStruct((2, 3, 1024, 128), low),
+        mixed=jax.ShapeDtypeStruct((384, 1024), low),
+        grads=jax.ShapeDtypeStruct(rows, low),
+    )
+    scratch = dict(
+        hidden_held=pltpu.VMEM((3, 128, 2048), low),
+        key_weight=pltpu.VMEM((2048, 128), low),
+        value_weight=pltpu.VMEM((2048, 128), low),
+        cosine_held=pltpu.VMEM((128, 128), full),
+        sine_held=pltpu.VMEM((128, 128), full),
+        query_weight=pltpu.VMEM((2048, 1024), low),
+        cotangent_held=pltpu.VMEM((3, 32, 2048), low),
+        out_weight=pltpu.VMEM((2048, 1024), low),
+        normed=pltpu.VMEM((384, 2048), low),
+        pair_held=pltpu.VMEM((2, 3, 1024, 128), low),
+        info=pltpu.VMEM((4, 4, 8, 128), full),
+        rows=pltpu.VMEM((128, 2048), low),
+        sending=pltpu.VMEM(rows, low),
+        query_held=pltpu.VMEM((384, 1024), low),
+        query_raw_held=pltpu.VMEM((384, 1024), full),
+        bias=pltpu.VMEM((128, 1024), full),
+        peak_rows=pltpu.VMEM((8, 1, 128), full),
+        mixed_held=pltpu.VMEM((384, 1024), low),
+        shares=pltpu.VMEM((3, 4, 32, 2048), low),
+        branch_slots=pltpu.VMEM((6, 3, 32, 1024), low),
+        after_sum=pltpu.VMEM((3, 32, 2048), full),
+        send=pltpu.SemaphoreType.DMA((46,)),
+        recv=pltpu.SemaphoreType.DMA((46,)),
+        here=pltpu.SemaphoreType.DMA((16,)),
+    )
+    return call(front_kernel, 2, far, near, outs, far_outs, scratch)
 
 
 def shards(
@@ -957,139 +1209,75 @@
     w_down,
     cotangent,
 ):
-    seqs_local, rows_ctx, model_width = hidden_in.shape
-    seq_length = segments.shape[1]
-    expert_span = lax.axis_size("experts")
-    ctx_index = lax.axis_index("context")
-    own_index = lax.axis_index("experts")
-    own_rows = rows_ctx // expert_span
-    head_count = w_query.shape[1] // HEAD_SIZE
-    kv_count = key_weight_matrix.shape[1] // HEAD_SIZE
-    per_group = head_count // kv_count
-    score_scale = HEAD_SIZE ** (-0.5)
-    token_count = seqs_local * rows_ctx
-    inputs = hidden_in.astype(jnp.float32)
-    gain_attn = attn_gain.astype(jnp.float32)
-    gain_query = query_gain.astype(jnp.float32)
-    gain_key = key_gain.astype(jnp.float32)
-    gain_moe = moe_gain.astype(jnp.float32)
-    normalized_input = rms_scale(inputs, gain_attn).astype(jnp.bfloat16)
-    normed_flat = normalized_input.reshape(token_count, model_width)
-    query_raw = jnp.dot(normed_flat, w_query, preferred_element_type=jnp.float32).reshape(
-        seqs_local, rows_ctx, head_count, HEAD_SIZE
-    )
-    unclipped_key = jnp.dot(
-        normed_flat, key_weight_matrix, preferred_element_type=jnp.float32
-    ).reshape(seqs_local, rows_ctx, kv_count, HEAD_SIZE)
-    value_reduced = (
-        jnp.dot(normed_flat, value_weight_matrix, preferred_element_type=jnp.float32)
-        .astype(jnp.bfloat16)
-        .reshape(seqs_local, rows_ctx, kv_count, HEAD_SIZE)
-    )
-    cosine_table, sine_table = rotary(ctx_index * rows_ctx, rows_ctx)
-    cosine_table = cosine_table[None, :, None, :]
-    sine_table = sine_table[None, :, None, :]
-    query_normed = rms_scale(query_raw, gain_query)
-    query_rot = (query_normed * cosine_table + turn(query_normed) * sine_table).astype(jnp.bfloat16)
-    key_normed = rms_scale(unclipped_key, gain_key)
-    key_rot = (key_normed * cosine_table + turn(key_normed) * sine_table).astype(jnp.bfloat16)
-    keys_all, values_all = (
-        lax.all_gather(key_rot, "context", axis=1, tiled=True),
-        lax.all_gather(value_reduced, "context", axis=1, tiled=True),
-    )
-    query_group = query_rot.reshape(seqs_local, rows_ctx, kv_count, per_group, HEAD_SIZE)
-    seg_query = lax.dynamic_slice_in_dim(segments, ctx_index * rows_ctx, rows_ctx, 1)
-    seg_float_query = seg_query.astype(jnp.float32)
-    query_spot = ctx_index * rows_ctx + jnp.arange(rows_ctx, dtype=jnp.int32)
-    key_spot = jnp.arange(seq_length, dtype=jnp.int32)
-    allowed = (seg_query[:, :, None] == segments[:, None, :]) & (
-        key_spot[None, None, :] <= query_spot[None, :, None]
-    )
-    allowed = allowed[:, None, :, None, :]
-
-    def masked_scores():
-        raw_score = (
-            jnp.einsum(
-                "sqhgd,skhd->shqgk", query_group, keys_all, preferred_element_type=jnp.float32
-            )
-            * score_scale
-        )
-        return jnp.where(allowed, raw_score, masked_value)
-
-    masked = masked_scores()
-    row_peak = jnp.max(masked, axis=-1, keepdims=True)
-    log_total = row_peak + jnp.log(jnp.sum(jnp.exp(masked - row_peak), axis=-1, keepdims=True))
-    head_peak = jnp.max(masked, axis=(0, 2, 4)).reshape(head_count)
-    prob_low = jnp.exp(masked - log_total).astype(jnp.bfloat16)
-    mixed_heads = jnp.einsum(
-        "shqgk,skhd->sqhgd", prob_low, values_all, preferred_element_type=jnp.float32
-    )
-    mixed_low = mixed_heads.astype(jnp.bfloat16).reshape(token_count, head_count * HEAD_SIZE)
-    branch_part = contract_last(mixed_low, w_out)
-    branch = lax.psum_scatter(
-        branch_part.reshape(seqs_local, rows_ctx, model_width).astype(jnp.bfloat16),
-        "experts",
-        scatter_dimension=1,
-        tiled=True,
-    ).astype(jnp.float32)
-    own_inputs = lax.dynamic_slice_in_dim(inputs, own_index * own_rows, own_rows, 1)
-    after_attn = own_inputs + branch
-    pair_tokens = seqs_local * own_rows
-    top_count = expert_ids.shape[2]
-    token_lanes = ((0, 0), (0, 128 - pair_tokens))
-    ids = jnp.pad(expert_ids.reshape(pair_tokens, top_count).T, token_lanes, constant_values=-1)
-    gates = jnp.pad(gate_values.reshape(pair_tokens, top_count).T, token_lanes)
-    after_flat = after_attn.reshape(pair_tokens, model_width)
-    after_grad, moe_gain_part, gate_grad, produced, table, full_gate, full_up, full_down = moe(
-        after_flat,
-        cotangent.reshape(pair_tokens, model_width),
-        gain_moe[None],
-        ids,
-        gates,
-        jnp.broadcast_to(capacity.astype(jnp.float32)[:, None], (capacity.shape[0], 128)),
-        w_gate[0],
-        w_up[0],
-        w_down[0],
-    )
-    after_grad = after_grad.reshape(seqs_local, own_rows, model_width)
-    gate_grad = gate_grad[:, :pair_tokens].T.reshape(seqs_local, own_rows, top_count)
-    cosine_row, sine_row = cosine_table[0, :, 0], sine_table[0, :, 0]
-    turn_sign = jnp.where(jnp.arange(HEAD_SIZE) < HEAD_SIZE // 2, 1.0, -1.0)
-    seg_float = segments.astype(jnp.float32)
+    full = jnp.float32
+    gains = jnp.stack([attn_gain, moe_gain]).astype(full)
+    head_gains = jnp.stack([query_gain, key_gain]).astype(full)
+    cosine, sine = rotary()
+    first = front(
+        dict(
+            hidden=hidden_in,
+            w_key=key_weight_matrix,
+            w_value=value_weight_matrix,
+            cosine=cosine,
+            sine=sine,
+            w_query=w_query,
+            cotangent=cotangent,
+            w_out=w_out,
+        ),
+        dict(
+            gains=gains,
+            head_gains=head_gains,
+            segments=segments,
+            ids=expert_ids,
+            gates=gate_values,
+            capacity=capacity,
+        ),
+    )
+    second = moe(
+        dict(w_gate=w_gate[0], w_up=w_up[0], w_down=w_down[0], grads=first.grads),
+        dict(
+            after=first.after,
+            cotangent=cotangent,
+            gains=gains,
+            ids=expert_ids,
+            table=first.table,
+            info_in=first.info_in,
+        ),
+    )
     done = back(
         dict(
-            branch=after_grad.astype(jnp.bfloat16),
+            branch=second.branch,
             w_out=w_out,
             w_query=w_query,
-            gate=full_gate.reshape(4, 2, 256, 768),
-            up=full_up.reshape(4, 2, 256, 768),
-            down=full_down.reshape(4, 2, 256, 768),
-            produced=produced,
+            gate=second.full_gate.reshape(4, 2, 256, 768),
+            up=second.full_up.reshape(4, 2, 256, 768),
+            down=second.full_down.reshape(4, 2, 256, 768),
+            produced=second.produced,
+            hidden=hidden_in,
+            mixed=first.mixed,
+            query=first.query,
+            query_raw=first.query_raw,
+            pair=first.pair,
+            cosine=cosine,
+            sine=sine,
+            w_key=key_weight_matrix,
+            w_value=value_weight_matrix,
         ),
         dict(
-            w_key=key_weight_matrix,
-            w_value=value_weight_matrix,
-            table=table,
-            hidden=hidden_in.reshape(token_count, model_width),
-            mixed=mixed_low,
-            query=query_rot.reshape(token_count, head_count * HEAD_SIZE),
-            query_raw=query_raw.reshape(token_count, head_count * HEAD_SIZE),
-            key_raw=unclipped_key.reshape(token_count, HEAD_SIZE),
-            pair=jnp.stack([keys_all[:, :, 0], values_all[:, :, 0]]),
-            log_sum=log_total[:, 0, :, :, 0].swapaxes(1, 2).reshape(24, 1, 128),
-            seg_query=seg_float_query[:, None, :],
-            seg_key=seg_float[:, None, :],
-            cosine=cosine_row,
-            sine=sine_row * turn_sign,
-            gain_query=gain_query[None],
-            gain_key=gain_key[None],
-            gain_attn=gain_attn[None],
-            moe_gain_part=moe_gain_part,
-            peaks=jnp.broadcast_to(head_peak[:, None], (head_count, 128)),
+            table=first.table,
+            key_raw=first.key_raw,
+            log_sum=first.log_sum,
+            segments=segments,
+            head_gains=head_gains,
+            gains=gains,
+            moe_gain_part=second.gain_part,
+            peaks=first.peaks,
         ),
     )
-    layer_out = after_attn + done.moe_out.reshape(seqs_local, own_rows, model_width)
-    input_grad = after_grad + done.normed_out
+    own_shape = cotangent.shape
+    layer_out = first.after.reshape(own_shape) + done.moe_out.reshape(own_shape)
+    input_grad = second.after_grad.reshape(own_shape) + done.normed_out
+    gate_grad = second.gate_grad
     w_key_grad, w_value_grad = done.pair_w_out[:, :128], done.pair_w_out[:, 128:]
     w_query_grad, w_out_grad = done.query_w_out, done.out_w_out
     w_gate_grad, w_up_grad, w_down_grad = (
@@ -1098,8 +1286,8 @@
         done.down_out[None],
     )
     small = done.small_out
-    attn_gain_grad = small[:16].reshape(model_width)
-    moe_gain_grad = small[16:32].reshape(model_width)
+    attn_gain_grad = small[:16].reshape(2048)
+    moe_gain_grad = small[16:32].reshape(2048)
     query_gain_grad, key_gain_grad = small[32], small[33]
     head_clip_scale = clip_limit / jnp.maximum(small[40:, 0], clip_limit)
     return (

time: 465 us -> 344 us (0.74); the launches traced: 457 us -> 343 us
  blocking collectives: 61.6 us -> 0 us
  Pallas kernels: 296 us -> 324 us
  other arithmetic: 33 us -> 6.9 us
  matrix products: 16.7 us -> 0 us
  waiting for transfers between devices: 16.6 us -> 0 us
  between operations: 15 us -> 0.75 us
  local copies, waits for them, and re-layouts: 17.9 us -> 11.7 us
    all_gather x2 -> x0, blocking collectives: 61.6 us -> none  [the longest x1 31.8 us: shards(): lax.all_gather(key_rot, 'context', axis=1, tiled=True)]
    pallas_call x2 -> x3, Pallas kernels: 296 us -> 324 us  [call(): pl.pallas_call(functools.partial(kernel, names), out_shape=list(shapes.va...]
    dot_general x6 -> x0, matrix products: 16.7 us -> none  [the longest x1 4.56 us: shards(): jnp.dot(normed_flat, w_query, preferred_element_type=jnp.float32)]
    reduce_scatter x1 -> x0, waiting for transfers between devices: 16.6 us -> none  [shards(): lax.psum_scatter(branch_part.reshape(seqs_local, rows_ctx, model_width).a...]
    convert_element_type x10 -> x2, other arithmetic: 10.4 us -> 1.87 us  [the longest x1 1.24 us: shards(): head_gains = jnp.stack([query_gain, key_gain]).astype(full)]
    unnamed x84 -> x26, local copies, waits for them, and re-layouts: 9.43 us -> 8.54 us
  transfers between devices with their start and end apart: 1 -> 0, of which waited for: 1 -> 0; matrix products, arithmetic and copies ran while one was open for 2% -> 0% of each run, Pallas kernels for 0% -> 0%
where the time goes in v4:
time: 344 us; the launch traced here: 343 us
  Pallas kernels  324 us (94%)
  local copies, waits for them, and re-layouts  11.7 us (3%)
  other arithmetic  6.9 us (2%)
    pallas_call x3, Pallas kernels, call(): pl.pallas_call(functools.partial(kernel, names), out_shape=list(shapes.va...  324 us
    unnamed x26, local copies, waits for them, and re-layouts  8.54 us

profile of v4, /device:TPU:0, one launch (start us, length us, event | category | flops | bytes accessed | tf_op | source)
XLA Modules:
  0.0 343.2 jit_solution(15356219320674909164)
XLA Ops:
  0.6 1.2 maximum_convert_fusion.1.refs_9_.refs_20_
  1.9 0.7 stack.18
  2.6 0.7 stack.19
  3.3 0.6 maximum_convert_fusion.refs_8_.refs_6_.refs_21_
  3.9 1.4 copy.38.refs_11_.refs_7_
  5.3 1.4 copy.39.refs_12_
  6.7 75.8 %front_kernel.1 = (f32[384,128]{1,0:T(8,128)}, f32[24,1,128]{2,1,0:T(1,128)}, f32[8,128]{1,0:T(8,128)}, f32[96,2048]{1,0:T(8,128)}, bf16[768,128]{1,0:T(8,128)(2...) custom-call(bf16[3,128,2048]{2,1,0:T(8,128)(2,1)} %refs_7_.4, ...), custom_call_target="tpu_custom_call" | custom-call | tf_op jit(solution)/shard_map/front_kernel/pallas_call | solution.py:954
  82.5 105.6 %moe_kernel.1 = (f32[96,2048]{1,0:T(8,128)}, bf16[3,32,2048]{2,1,0:T(8,128)(2,1)}, f32[1,2048]{1,0:T(1,128)}, f32[3,32,8]{2,1,0:T(8,128)}, bf16[4,4,48,2048]{3,2...) custom-call(bf16[2048,768]{1,0:T(8,128)(2,1)} %bitcast.21, ...), custom_call_target="tpu_custom_call" | custom-call | tf_op jit(solution)/shard_map/moe_kernel/pallas_call | solution.py:954
  188.1 0.0 copy-start
  188.1 0.0 copy-start.4
  188.2 142.5 %back_kernel.1 = (f32[256,768]{1,0:T(8,128)}, f32[256,768]{1,0:T(8,128)}, f32[256,768]{1,0:T(8,128)}, f32[64,1024]{1,0:T(8,128)}, f32[64,256]{1,0:T(8,128)}, /*i...) custom-call(bf16[3,32,2048]{2,1,0:T(8,128)(2,1)} %get-tuple-element., ...), custom_call_target="tpu_custom_call" | custom-call | tf_op jit(solution)/shard_map/back_kernel/pallas_call | solution.py:954
  330.7 0.0 copy-start.8
  330.7 0.0 copy-start.7
  330.7 0.0 copy-start.6
  330.7 0.0 copy-start.5
  330.7 0.0 copy-start.3
  330.7 0.0 copy-done
  330.7 2.2 add.9
  332.9 0.0 copy-start.2
  332.9 0.0 copy-done.4
  332.9 0.0 copy-start.1
  332.9 2.2 add.11
  335.1 0.0 copy-done.8
  335.1 0.6 divide_reduce_fusion
  335.8 0.5 slice_bitcast_fusion.2
  336.3 0.6 slice_bitcast_fusion
  336.9 0.0 copy-done.7
  336.9 0.7 copy.41
  337.6 0.0 copy-done.6
  337.6 0.6 fusion
  338.2 1.7 copy.47
  339.9 0.0 copy-done.5
  339.9 0.7 copy.48
  340.6 0.0 copy-done.3
  340.6 0.9 copy.49
  341.5 0.0 copy-done.2
  341.5 0.9 copy.50
  342.4 0.0 copy-done.1
  342.4 0.9 copy.51
Async XLA Ops:
  188.1 142.6 %copy-start = (f32[96,2048]{1,0:T(8,128)S(1)}, f32[96,2048]{1,0:T(8,128)}, u32[]{:S(2)}) copy-start(f32[96,2048]{1,0:T(8,128)} %get-tuple-element.43.refs_4_) | copy-start | bytes 2359300
  188.1 144.8 %copy-start.4 = (f32[96,2048]{1,0:T(8,128)S(1)}, f32[96,2048]{1,0:T(8,128)}, u32[]{:S(2)}) copy-start(f32[96,2048]{1,0:T(8,128)} %get-tuple-element.61) | copy-start | bytes 2359300
  330.7 4.5 %copy-start.8 = (f32[48,128]{1,0:T(8,128)S(1)}, f32[48,128]{1,0:T(8,128)}, u32[]{:S(2)}) copy-start(f32[48,128]{1,0:T(8,128)} %get-tuple-element.63) | copy-start | bytes 73732
  330.7 6.2 %copy-start.7 = (f32[3,32,8]{2,1,0:T(8,128)S(1)}, f32[3,32,8]{2,1,0:T(8,128)}, u32[]{:S(2)}) copy-start(f32[3,32,8]{2,1,0:T(8,128)} %get-tuple-element.96) | copy-start | bytes 9220
  330.7 6.9 %copy-start.6 = (f32[64,256]{1,0:T(8,128)S(1)}, f32[64,256]{1,0:T(8,128)}, u32[]{:S(2)}) copy-start(f32[64,256]{1,0:T(8,128)} %get-tuple-element.65) | copy-start | bytes 196612
  330.7 9.2 %copy-start.5 = (f32[64,1024]{1,0:T(8,128)S(1)}, f32[64,1024]{1,0:T(8,128)}, u32[]{:S(2)}) copy-start(f32[64,1024]{1,0:T(8,128)} %get-tuple-element.130) | copy-start | bytes 786436
  330.7 9.9 %copy-start.3 = (f32[256,768]{1,0:T(8,128)S(1)}, f32[256,768]{1,0:T(8,128)}, u32[]{:S(2)}) copy-start(f32[256,768]{1,0:T(8,128)} %get-tuple-element.68) | copy-start | bytes 2359300
  332.9 8.5 %copy-start.2 = (f32[256,768]{1,0:T(8,128)S(1)}, f32[256,768]{1,0:T(8,128)}, u32[]{:S(2)}) copy-start(f32[256,768]{1,0:T(8,128)} %get-tuple-element.69) | copy-start | bytes 2359300
  332.9 9.4 %copy-start.1 = (f32[256,768]{1,0:T(8,128)S(1)}, f32[256,768]{1,0:T(8,128)}, u32[]{:S(2)}) copy-start(f32[256,768]{1,0:T(8,128)} %get-tuple-element.70) | copy-start | bytes 2359300

commit v5 on v4

--- a/solution.py
+++ b/solution.py
@@ -55,6 +55,7 @@
         self.core, self.z_hi = lax.rem(dp, 2), dp // 2
         self.x, self.z_lo = context // 2, lax.rem(context, 2)
         self.z = self.z_hi * 2 + self.z_lo
+        self.spot = (self.core, self.z_hi, self.y)
 
     def at(self, x=None, y=None, z=None, core=None):
         x = self.x if x is None else x
@@ -112,7 +113,12 @@
     barrier = pltpu.get_barrier_semaphore()
     for device in devices:
         pl.semaphore_signal(barrier, inc=1, device_id=device, device_id_type=MESH)
-    pl.semaphore_wait(barrier, len(devices))
+    return lambda: pl.semaphore_wait(barrier, len(devices))
+
+
+def wide(ref):
+    values = ref[...].astype(jnp.float32)
+    return jnp.concatenate([values[step : step + 1] for step in range(16)], axis=1)
 
 
 def add_into(target, parts, block=32):
@@ -131,29 +137,35 @@
         lax.fori_loop(0, rows // block, body, 0)
 
 
-def ring_reduce(net, plus, minus, own, slots, target, held=None):
+def ring_reduce(net, plus, minus, own, slots, target, held=None, begun=None):
     held = own if held is None else held
-    first_plus = net.copy(own(2, 0), slots.at[0], plus)
-    first_minus = net.copy(own(2, 1), slots.at[2], minus)
-    side_plus = net.copy(own(1, 1), slots.at[1], plus)
-    side_minus = net.copy(own(3, 0), slots.at[3], minus)
-    yield
-    first_plus.wait_recv()
+    if begun is None:
+        first_plus = net.copy(own(2, 0), slots.at[0], plus)
+        first_minus = net.copy(own(2, 1), slots.at[2], minus)
+        side_plus = net.copy(own(1, 1), slots.at[1], plus)
+        side_minus = net.copy(own(3, 0), slots.at[3], minus)
+        yield
+        first_plus.wait_recv()
+        first_minus.wait_recv()
+    else:
+        load = net.load(begun, slots.at[pl.ds(0, 4)])
+        yield
+        load.wait()
     add_into(slots.at[0], [slots.at[0], held(1, 0)])
     last_plus = net.copy(slots.at[0], slots.at[4], plus)
-    first_minus.wait_recv()
     add_into(slots.at[2], [slots.at[2], held(3, 1)])
     last_minus = net.copy(slots.at[2], slots.at[5], minus)
     yield
-    side_minus.wait_recv()
+    if begun is None:
+        side_minus.wait_recv()
+        side_plus.wait_recv()
     last_plus.wait_recv()
     add_into(target(0), [held(0, 0), slots.at[3], slots.at[4]])
-    side_plus.wait_recv()
     last_minus.wait_recv()
     add_into(target(1), [held(0, 1), slots.at[1], slots.at[5]])
 
 
-def x_first(net, me, source, slots, middle, other, out, held=None):
+def x_first(net, me, source, slots, middle, other, out, held=None, begun=None):
     staged = None
     if held is not None:
         order = {(1, 0): 0, (3, 1): 1, (0, 0): 2, (0, 1): 3}
@@ -173,6 +185,7 @@
         slots,
         lambda half: middle.at[half],
         staged,
+        begun,
     )
     next(ring)
     yield
@@ -184,24 +197,6 @@
     yield
     across.wait_recv()
     add_into(out, [middle.at[me.z_lo], other])
-
-
-def z_first(net, me, source, other, middle, slots, out):
-    across = net.copy(source.at[:, 1 - me.z_lo], other, me.at(z=me.z + 1 - 2 * me.z_lo))
-    load = net.load(source.at[:, me.z_lo], middle)
-    yield
-    load.wait()
-    across.wait_recv()
-    add_into(middle, [middle, other])
-    half_rows = middle.shape[1] // 2
-    yield from ring_reduce(
-        net,
-        me.at(x=me.x_by(1)),
-        me.at(x=me.x_by(3)),
-        lambda step, half: middle.at[me.x_by(step), pl.ds(half * half_rows, half_rows)],
-        slots,
-        lambda half: out.at[pl.ds(half * half_rows, half_rows)],
-    )
 
 
 def core_pair(net, me, sending, other, middle):
@@ -285,27 +280,29 @@
     out[:40] = working[:40]
 
 
-def peers(me):
-    offsets = [(a, b) for a in (2, 3, 0, 1) for b in (1, 3, 2, 0) if a or b]
-    return [(a, b) + peer(me, a, b) for a, b in offsets]
+OFFSETS = [(a, b) for a in (2, 0, 3, 1) for b in (0, 1, 3, 2) if a or b]
 
 
 def peer(me, a, b):
     z = me.z if a < 2 else lax.rem(me.z + 2, 4)
     core = me.core if a % 2 == 0 else 1 - me.core
     y = me.y_by(b)
-    return z // 2 * 2 + core, y, me.at(z=z, core=core, y=y)
+    return (core, z // 2, y), me.at(z=z, core=core, y=y)
+
+
+def peers(me):
+    return [peer(me, a, b)[1] for a, b in OFFSETS]
 
 
 def gather_rows(table, home, store):
     def body(step, carry):
         columns = pl.ds(pl.multiple_of(step * 256, 256), 256)
-        rows = home[:, :, :, columns].reshape(768, 256)
+        rows = home[:, :, :, :, columns].reshape(768, 256)
         total = contract_first(table[...], rows)
         store(columns, total[:96])
         return carry
 
-    lax.fori_loop(0, home.shape[3] // 256, body, 0)
+    lax.fori_loop(0, home.shape[4] // 256, body, 0)
 
 
 def turned(values):
@@ -335,7 +332,7 @@
     net = Net(r.send, r.recv, r.here)
     fetch = Fetch(net)
     fetch.start("hidden", r.hidden, r.hidden_held)
-    greet(
+    greeted = greet(
         [
             me.at(x=me.x_by(1)),
             me.at(x=me.x_by(3)),
@@ -343,8 +340,11 @@
             me.at(z=me.z_by(3)),
             me.at(x=me.x_by(2)),
         ]
-        + [one[4] for one in peers(me)]
-    )
+        + peers(me)
+    )
+    gains = r.gain_rows
+    gains[...] = wide(r.attn_gain)
+    greeted()
 
     branch, whole = r.branch, r.whole
     above, below = me.at(y=me.y_by(1)), me.at(y=me.y_by(3))
@@ -354,19 +354,16 @@
     weight = r.weight
     load_out = net.load(r.w_out, weight)
     gate = x_first(
-        net, me, r.gate, r.gate_slots, r.gate_middle, r.gate_other,
-        r.gate_out, r.gate_held,
-    )
-    up = x_first(
-        net, me, r.up, r.up_slots, r.up_middle, r.up_other,
-        r.up_out, r.up_held,
-    )
-    down = z_first(
-        net, me, r.down, r.down_other, r.down_middle, r.down_slots,
-        r.down_out,
-    )
-    for task in (gate, up, down):
-        next(task)
+        net, me, r.gate, r.gate_slots, r.gate_middle, r.gate_other, r.gate_out, r.gate_held,
+        r.gate_begun,
+    )
+    up = x_first(net, me, r.up, r.up_slots, r.up_middle, r.up_other, r.up_out, r.up_held)
+    down = x_first(
+        net, me, r.down, r.down_slots, r.down_middle, r.down_other, r.down_out, r.down_held
+    )
+    next(gate)
+    next(up)
+    next(gate)
     fetch.start("pair", r.pair, r.pair_held)
     fetch.start("query", r.query, r.query_held)
     fetch.start("query_raw", r.query_raw, r.query_raw_held)
@@ -408,15 +405,17 @@
     load_query = net.load(r.w_query, weight)
 
     produced, home, table = r.produced, r.home, r.table
-    mine = pl.ds(pl.multiple_of(me.dp * 192 + me.y * 48, 16), 48)
-    home_came = [
-        net.copy(produced.at[dp, y], home.at[mine], device) for a, b, dp, y, device in peers(me)
-    ]
-    home_own = net.load(produced.at[me.dp, me.y], home.at[mine])
+    start = me.core * 384 + me.z_hi * 192 + me.y * 48
+    mine = pl.ds(pl.multiple_of(start, 16), 48)
+    home_came = []
+    for a, b in OFFSETS:
+        spot, device = peer(me, a, b)
+        home_came.append(net.copy(produced.at[spot], home.at[mine], device))
+    home_own = net.load(produced.at[me.spot], home.at[mine])
 
     query, query_raw, pair = fetch.query, fetch.query_raw, fetch.pair
     cosine, sine, mixed = fetch.cosine, fetch.sine, fetch.mixed
-    gain_query, gain_key = r.head_gains[0:1, :], r.head_gains[1:2, :]
+    gain_query, gain_key = r.query_gain[...].astype(full), r.key_gain[...].astype(full)
     bias, key_sum, value_sum = r.bias, r.key_sum, r.value_sum
     pair_grad, gain_part = r.pair_grad, r.gain_part
     gain_part[...] = jnp.zeros((8, 128), full)
@@ -469,14 +468,13 @@
 
     attend(0)
     attend(1)
-    next(gate)
-    next(up)
     attend(2)
     pairs = x_first(
         net, me, pair_grad, r.pair_slots, r.pair_middle, r.pair_other,
         r.pair_out,
     )
     next(pairs)
+    next(gate)
 
     query_low = heads_grad
 
@@ -484,7 +482,7 @@
         return hidden[:, :, columns].reshape(384, 256).astype(full)
 
     def normed(columns):
-        return (own_input(columns) * inverse[:, 0:1] * r.gains[0:1, columns]).astype(low)
+        return (own_input(columns) * inverse[:, 0:1] * gains[:, columns]).astype(low)
 
     def whole_part(columns):
         return whole[:, :, :, columns].reshape(384, 256)
@@ -518,8 +516,8 @@
         r.query_w_last, r.query_w_out,
     )
     next(pairs)
-    next(gate)
     next(up)
+    next(query_w)
 
     pair_out, key_raw, pair_low = r.pair_out, r.key_raw, r.pair_low
     next(pairs, None)
@@ -572,23 +570,22 @@
         dense_x_first, normed, pair_low, r.pair_sending, r.pair_w_other, r.pair_w_middle, r.pair_w_slots, r.pair_w_corner,
         r.pair_w_last, r.pair_w_out,
     )
-    next(query_w)
     next(smalls)
 
     def rest(*tasks):
         for task in tasks:
             next(task, None)
 
-    rest(normed_sum, out_w, pair_w, smalls, gate, up, down, query_w)
+    rest(out_w, pair_w, smalls, normed_sum, gate, up, down, query_w)
 
     next(normed_sum, None)
     for s in range(3):
         rows = pl.ds(pl.multiple_of(me.y * 32, 32), 32)
-        grad, _ = norm_back(normed_out[s], hidden[s, rows, :].astype(full), r.gains[0:1, :])
+        grad, _ = norm_back(normed_out[s], hidden[s, rows, :].astype(full), gains[...])
         normed_out[s] = grad
 
-    rest(out_w, pair_w, smalls, down, gate, up, query_w)
-    rest(pair_w, out_w, smalls, query_w)
+    rest(pair_w, smalls, out_w, up, down, query_w)
+    rest(pair_w, smalls, out_w, query_w)
 
     for made in home_came:
         made.wait_recv()
@@ -597,7 +594,7 @@
         net.load(home.at[:, pl.ds(half * 1024, 1024)], weight.at[pl.ds(half * 768, 768)])
         for half in range(2)
     ]
-    rest(pair_w, out_w, smalls, query_w, gate, up, down)
+    rest(pair_w, smalls, out_w, query_w, down)
     moe_out = r.moe_out
     for half in range(2):
         home_loads[half].wait()
@@ -642,6 +639,7 @@
         moe_out=(96, 2048),
     )
     scratch = dict(
+        gain_rows=pltpu.VMEM((1, 2048), full),
         hidden_held=pltpu.VMEM((3, 128, 2048), low),
         pair_held=pltpu.VMEM((2, 3, 1024, 128), low),
         query_held=pltpu.VMEM((384, 1024), low),
@@ -672,9 +670,10 @@
         by_x=pltpu.VMEM((4, 48, 128), full),
         by_z=pltpu.VMEM((4, 48, 128), full),
         by_y=pltpu.VMEM((4, 48, 128), full),
-        down_other=pltpu.VMEM((4, 256, 768), low),
-        down_middle=pltpu.VMEM((4, 256, 768), low),
-        down_slots=pltpu.VMEM((6, 128, 768), low),
+        down_slots=pltpu.VMEM((6, 256, 768), low),
+        down_middle=pltpu.VMEM((2, 256, 768), low),
+        down_other=pltpu.VMEM((256, 768), low),
+        down_held=pltpu.VMEM((4, 256, 768), low),
         gate_slots=pltpu.VMEM((6, 256, 768), low),
         gate_middle=pltpu.VMEM((2, 256, 768), low),
         gate_other=pltpu.VMEM((256, 768), low),
@@ -702,7 +701,7 @@
         out_w_last=None,
         send=pltpu.SemaphoreType.DMA((104,)),
         recv=pltpu.SemaphoreType.DMA((104,)),
-        here=pltpu.SemaphoreType.DMA((28,)),
+        here=pltpu.SemaphoreType.DMA((34,)),
     )
     dense = dense_slots(1024, (2, 2)) + dense_slots(256, (2, 2)) + dense_slots(1024, (4,))
     scratch = {name: one or dense.pop(0) for name, one in scratch.items()}
@@ -727,47 +726,49 @@
 
 def token_table(ids, gates, capacity, table, info):
     low, full = jnp.bfloat16, jnp.float32
-    expert = lax.broadcasted_iota(jnp.int32, (96, 128), 1)
-    routes = ids[...].reshape(96, 8)
-    values = gates[...].reshape(96, 8)
-    chosen = jnp.zeros((96, 128), full)
-    share = jnp.zeros((96, 128), full)
-    limit = jnp.zeros((1, 128), full)
-    for k in range(8):
-        named = routes[:, k : k + 1] == expert
-        chosen = chosen + jnp.where(named, 1.0, 0.0)
-        share = share + jnp.where(named, values[:, k : k + 1], 0.0)
+    expert = lax.broadcasted_iota(jnp.int32, (16, 32), 0)
+    chosen, share = [], []
+    for s in range(3):
+        chosen_here = jnp.zeros((16, 32), full)
+        share_here = jnp.zeros((16, 32), full)
+        for k in range(8):
+            named = ids[s, k : k + 1, :] == expert
+            chosen_here = chosen_here + jnp.where(named, 1.0, 0.0)
+            share_here = share_here + jnp.where(named, gates[s, k : k + 1, :], 0.0)
+        chosen.append(chosen_here)
+        share.append(share_here)
+    none = jnp.zeros((16, 32), full)
+    chosen = jnp.concatenate(chosen + [none], axis=1)
+    share = jnp.concatenate(share + [none], axis=1)
+    row = lax.broadcasted_iota(jnp.int32, (16, 128), 0)
+    limit = jnp.zeros((16, 128), full)
     for e in range(16):
-        limit = jnp.where(expert[0:1] == e, capacity[e].astype(full), limit)
-    earlier = lax.broadcasted_iota(jnp.int32, (96, 96), 1) < lax.broadcasted_iota(
-        jnp.int32, (96, 96), 0
+        limit = jnp.where(row == e, capacity[e].astype(full), limit)
+    earlier = lax.broadcasted_iota(jnp.int32, (128, 128), 0) < lax.broadcasted_iota(
+        jnp.int32, (128, 128), 1
     )
     before = jnp.dot(
-        jnp.where(earlier, 1.0, 0.0).astype(low), chosen.astype(low), preferred_element_type=full
+        chosen.astype(low), jnp.where(earlier, 1.0, 0.0).astype(low), preferred_element_type=full
     )
     slot = jnp.where((chosen > 0.0) & (before < limit), before, -1.0)
-    none = jnp.full((32, 128), -1.0, full)
-    slot = jnp.concatenate([slot, none], axis=0).T
-    share = jnp.concatenate([share, none], axis=0).T
     spot = lax.broadcasted_iota(jnp.int32, (48, 128), 0).astype(full)
-    for e in range(16):
+    for place in range(16):
+        core, z_hi, y = place // 8, place // 4 % 2, place % 4
+        e = (z_hi * 2 + core) * 4 + y
         mask = jnp.where(slot[e : e + 1, :] == spot, 1.0, 0.0)
-        table[e * 48 : e * 48 + 48, :] = mask.astype(low)
-        info[e // 4, e % 4] = jnp.concatenate(
+        table[place * 48 : place * 48 + 48, :] = mask.astype(low)
+        info[core, z_hi, y] = jnp.concatenate(
             [slot[e : e + 1, :], share[e : e + 1, :], jnp.zeros((6, 128), full)], axis=0
         )
 
 
-def dispatch(me, table, rows, sender):
-    for a, b, dp, y, device in peers(me):
-        if b == 1:
-            rest = table[pl.ds(pl.multiple_of(dp * 192, 192), 192), :]
-            columns = 512
-            for step in range(2048 // columns):
-                run = slice(step * columns, (step + 1) * columns)
-                picked = jnp.dot(rest, rows[:, run], preferred_element_type=jnp.float32)
-                sender[dp, :, :, run] = picked.astype(jnp.bfloat16).reshape(4, 48, columns)
-        yield a, b, dp, y, device
+def dispatch(table, rows, sender, core):
+    rest = table[pl.ds(pl.multiple_of(core * 384, 384), 384), :]
+    columns = 512
+    for step in range(2048 // columns):
+        run = slice(step * columns, (step + 1) * columns)
+        picked = jnp.dot(rest, rows[:, run], preferred_element_type=jnp.float32)
+        sender[core, :, :, :, run] = picked.astype(jnp.bfloat16).reshape(2, 4, 48, columns)
 
 
 def moe_kernel(names, *refs):
@@ -778,45 +779,59 @@
     fetch = Fetch(net)
     fetch.start("w_gate", r.w_gate, r.gate_weight)
     fetch.start("w_up", r.w_up, r.up_weight)
-    fetch.start("grads", r.grads, r.grads_held)
+    fetch.start("raw", r.grads, r.raw_held)
     fetch.start("w_down", r.w_down, r.down_weight)
-    greet([one[4] for one in peers(me)])
+    greeted = greet(peers(me) + [me.at(x=me.x_by(1)), me.at(x=me.x_by(3))])
     rows, sending, local, table = r.rows, r.sending, r.local, r.table
     values = r.after[...]
     inverse = lax.rsqrt(jnp.mean(values * values, axis=-1, keepdims=True) + epsilon)
-    gain = r.gains[1:2, :]
+    gain = wide(r.moe_gain)
     rows[96:, :] = jnp.zeros((32, 2048), low)
     rows[:96, :] = (values * inverse * gain).astype(low)
     came = {}
-    for a, b, dp, y, device in dispatch(me, table, rows, sending):
-        came[a, b] = net.copy(sending.at[dp, y], local.at[me.dp, me.y], device)
-    local[me.dp, me.y] = sending[me.dp, me.y]
+
+    def set_out(first, second):
+        for a, b in OFFSETS:
+            if a in (first, second):
+                spot, device = peer(me, a, b)
+                came[a, b] = net.copy(sending.at[spot], local.at[me.spot], device)
+
+    dispatch(table, rows, sending, me.core)
+    greeted()
+    set_out(0, 2)
+    local[me.spot] = sending[me.spot]
+    dispatch(table, rows, sending, 1 - me.core)
 
     act, gate_back, up_back, back, home = r.act, r.gate_back, r.up_back, r.back, r.home
-    w_gate, w_up, grads, w_down = fetch.w_gate, fetch.w_up, fetch.grads, fetch.w_down
+    w_gate, w_up, grads, w_down = fetch.w_gate, fetch.w_up, r.grads_held, fetch.w_down
+    fetch.raw
     spot = lax.broadcasted_iota(jnp.int32, (48, 128), 0).astype(full)
     back_came, dots_came = {}, {}
-    for a in (0, 1, 2, 3):
-        group = peer(me, a, 0)[0]
-        for b in range(4):
-            if a or b:
-                came[a, b].wait_recv()
+    for first in (0, 1):
+        group = me.core if first == 0 else 1 - me.core
+        for a in (first, first + 2):
+            for b in (1, 3, 2, 0):
+                if a or b:
+                    came[a, b].wait_recv()
+            if a == 0:
+                set_out(1, 3)
         masks, shares = [], []
-        for y in range(4):
-            mask = r.info_in[group, y, 0:1, :] == spot
-            masks.append(mask)
-            shares.append(
-                jnp.sum(jnp.where(mask, r.info_in[group, y, 1:2, :], 0.0), axis=1, keepdims=True)
-            )
+        for z_hi in range(2):
+            for y in range(4):
+                mask = r.info_in[group, z_hi, y, 0:1, :] == spot
+                share = jnp.where(mask, r.info_in[group, z_hi, y, 1:2, :], 0.0)
+                masks.append(mask)
+                shares.append(jnp.sum(share, axis=1, keepdims=True))
         shared = jnp.concatenate(shares, axis=0)
 
         def inner(step, carry, group=group, shared=shared):
             columns = pl.ds(pl.multiple_of(step * 256, 256), 256)
-            entered = local[group].reshape(192, 2048)
+            entered = local[group].reshape(384, 2048)
             gate_pre = jnp.dot(entered, w_gate[:, columns], preferred_element_type=full)
             up_pre = jnp.dot(entered, w_up[:, columns], preferred_element_type=full)
-            scaled = (grads[group].reshape(192, 2048).astype(full) * shared).astype(low)
-            act_back = jnp.dot(scaled, w_down[:, columns], preferred_element_type=full)
+            act_back = jnp.dot(
+                grads[group].reshape(384, 2048), w_down[:, columns], preferred_element_type=full
+            )
             sigmoid = 1.0 / (1.0 + jnp.exp(-gate_pre))
             silu = gate_pre * sigmoid
             act[group, :, columns] = (silu * up_pre).astype(low)
@@ -826,70 +841,95 @@
             up_back[group, :, columns] = (act_back * silu).astype(low)
             return carry
 
-        lax.fori_loop(0, 3, inner, 0)
-
         def outer(step, dot, group=group, shared=shared):
             columns = pl.ds(pl.multiple_of(step * 256, 256), 256)
-            made = contract_last(act[group], w_down[columns, :]).astype(low).astype(full)
-            r.produced_held[group, :, :, columns] = (
-                (made * shared).astype(low).reshape(4, 48, 256)
-            )
-            incoming = grads[group, :, :, columns].reshape(192, 256).astype(full)
-            dot = dot + jnp.sum(made * incoming, axis=1, keepdims=True)
-            grads[group, :, :, columns] = (incoming * shared).astype(low).reshape(4, 48, 256)
             row_back = contract_last(gate_back[group], w_gate[columns, :]) + contract_last(
                 up_back[group], w_up[columns, :]
             )
-            back[group, :, :, columns] = row_back.astype(low).reshape(4, 48, 256)
+            back[group, :, :, :, columns] = row_back.astype(low).reshape(2, 4, 48, 256)
             return dot
 
-        dot = lax.fori_loop(0, 8, outer, jnp.zeros((192, 1), full))
-        for y in range(4):
-            line = jnp.sum(
-                jnp.where(masks[y], dot[y * 48 : y * 48 + 48], 0.0), axis=0, keepdims=True
+        def finals(step, dot, group=group, shared=shared):
+            columns = pl.ds(pl.multiple_of(step * 256, 256), 256)
+            made = contract_last(act[group], w_down[columns, :]).astype(low).astype(full)
+            r.produced_held[group, :, :, :, columns] = (
+                (made * shared).astype(low).reshape(2, 4, 48, 256)
             )
-            r.dots[group, y] = jnp.broadcast_to(line, (8, 128))
-        for b in (2, 1, 3, 0):
-            if a or b:
-                dp, y, device = peer(me, a, b)
-                back_came[a, b] = net.copy(back.at[dp, y], home.at[me.dp, me.y], device)
-                dots_came[a, b] = net.copy(r.dots.at[dp, y], r.dots_in.at[me.dp, me.y], device)
-    home[me.dp, me.y] = back[me.dp, me.y]
-    r.dots_in[me.dp, me.y] = r.dots[me.dp, me.y]
+            incoming = r.raw_held[group, :, :, :, columns].reshape(384, 256).astype(full)
+            return dot + jnp.sum(made * incoming, axis=1, keepdims=True)
+
+        def scale(step, carry, group=group, shared=shared):
+            columns = pl.ds(pl.multiple_of(step * 256, 256), 256)
+            incoming = r.raw_held[group, :, :, :, columns].reshape(384, 256).astype(full)
+            grads[group, :, :, :, columns] = (
+                (incoming * shared).astype(low).reshape(2, 4, 48, 256)
+            )
+            return carry
+
+        lax.fori_loop(0, 8, scale, 0)
+        lax.fori_loop(0, 3, inner, 0)
+        lax.fori_loop(0, 8, outer, 0)
+        for a in (first + 2, first):
+            for b in (0, 1, 3, 2):
+                if a or b:
+                    place, device = peer(me, a, b)
+                    back_came[a, b] = net.copy(back.at[place], home.at[me.spot], device)
+        dot = lax.fori_loop(0, 8, finals, jnp.zeros((384, 1), full))
+        for place in range(8):
+            line = jnp.where(masks[place], dot[place * 48 : place * 48 + 48], 0.0)
+            line = jnp.sum(line, axis=0, keepdims=True)
+            r.dots[group, place // 4, place % 4] = jnp.broadcast_to(line, (8, 128))
+        for a in (first + 2, first):
+            for b in (0, 1, 3, 2):
+                if a or b:
+                    place, device = peer(me, a, b)
+                    dots_came[a, b] = net.copy(r.dots.at[place], r.dots_in.at[me.spot], device)
+    home[me.spot] = back[me.spot]
+    r.dots_in[me.spot] = r.dots[me.spot]
     written = [net.load(r.produced_held, r.produced)]
 
-    def weigh(step, carry):
-        columns = pl.ds(pl.multiple_of(step * 256, 256), 256)
-        entered = local[:, :, :, columns].reshape(768, 256)
-        r.gate_held[columns, :] = contract_first(entered, gate_back[...].reshape(768, 768)).astype(
-            low
-        )
-        r.up_held[columns, :] = contract_first(entered, up_back[...].reshape(768, 768)).astype(low)
-        incoming = grads[:, :, :, columns].reshape(768, 256)
-        r.down_held[columns, :] = contract_first(incoming, act[...].reshape(768, 768)).astype(low)
-        return carry
-
-    lax.fori_loop(0, 8, weigh, 0)
-    written += [
-        net.load(r.gate_held, r.full_gate),
-        net.load(r.up_held, r.full_up),
-        net.load(r.down_held, r.full_down),
+    def weigh(left, right, target):
+        def body(step, carry):
+            columns = pl.ds(pl.multiple_of(step * 256, 256), 256)
+            entered = left[:, :, :, :, columns].reshape(768, 256)
+            target[columns, :] = contract_first(entered, right[...].reshape(768, 768)).astype(low)
+            return carry
+
+        lax.fori_loop(0, 8, body, 0)
+
+    def chunk(step, half):
+        start = (me.x_by(step) * 2 + half) * 256
+        return r.gate_held.at[pl.ds(pl.multiple_of(start, 256), 256)]
+
+    weigh(local, gate_back, r.gate_held)
+    right, left = me.at(x=me.x_by(1)), me.at(x=me.x_by(3))
+    round_x = [
+        net.copy(chunk(2, 0), r.gate_slots.at[0], right),
+        net.copy(chunk(2, 1), r.gate_slots.at[2], left),
+        net.copy(chunk(1, 1), r.gate_slots.at[1], right),
+        net.copy(chunk(3, 0), r.gate_slots.at[3], left),
     ]
-
-    for a, b, *_ in peers(me):
-        dots_came[a, b].wait_recv()
-    lines = [r.dots_in[e // 4, e % 4, 0:1, :] for e in range(16)]
-    by_token = jnp.concatenate(lines + [jnp.zeros((112, 128), full)], axis=0).T[:96]
-    expert = lax.broadcasted_iota(jnp.int32, (96, 128), 1)
-    routes = r.ids[...].reshape(96, 8)
-    picked = [
-        jnp.sum(jnp.where(routes[:, k : k + 1] == expert, by_token, 0.0), axis=1, keepdims=True)
-        for k in range(8)
-    ]
-    r.gate_grad[...] = jnp.concatenate(picked, axis=1).reshape(3, 32, 8)
-
-    for a, b, *_ in peers(me):
-        back_came[a, b].wait_recv()
+    written.append(net.load(r.gate_held, r.full_gate))
+    weigh(local, up_back, r.up_held)
+    written.append(net.load(r.up_held, r.full_up))
+    weigh(grads, act, r.down_held)
+    written.append(net.load(r.down_held, r.full_down))
+
+    for offset in OFFSETS:
+        dots_came[offset].wait_recv()
+    lines = [r.dots_in[e // 4 % 2, e // 8, e % 4, 0:1, :] for e in range(16)]
+    lines = jnp.concatenate(lines, axis=0)
+    expert = lax.broadcasted_iota(jnp.int32, (16, 32), 0)
+    for s in range(3):
+        dots = lines[:, s * 32 : s * 32 + 32]
+        for k in range(8):
+            named = r.ids[s, k : k + 1, :] == expert
+            r.gate_grad[s, k : k + 1, :] = jnp.sum(
+                jnp.where(named, dots, 0.0), axis=0, keepdims=True
+            )
+
+    for offset in OFFSETS:
+        back_came[offset].wait_recv()
     after_grad = r.after_grad
 
     def keep(columns, total):
@@ -904,28 +944,32 @@
     r.branch[...] = result.astype(low).reshape(3, 32, 2048)
     for one in written:
         one.wait()
+    for one in round_x:
+        one.wait_recv()
     net.finish()
 
 
 def moe(far, near):
     low, full = jnp.bfloat16, jnp.float32
-    rows = (4, 4, 48, 2048)
+    rows = (2, 2, 4, 48, 2048)
     outs = dict(
         after_grad=jax.ShapeDtypeStruct((96, 2048), full),
         branch=jax.ShapeDtypeStruct((3, 32, 2048), low),
         gain_part=jax.ShapeDtypeStruct((1, 2048), full),
-        gate_grad=jax.ShapeDtypeStruct((3, 32, 8), full),
+        gate_grad=jax.ShapeDtypeStruct((3, 8, 32), full),
     )
     far_outs = dict(
         produced=jax.ShapeDtypeStruct(rows, low),
         full_gate=jax.ShapeDtypeStruct((2048, 768), low),
         full_up=jax.ShapeDtypeStruct((2048, 768), low),
         full_down=jax.ShapeDtypeStruct((2048, 768), low),
+        gate_slots=jax.ShapeDtypeStruct((4, 256, 768), low),
     )
     scratch = dict(
         rows=pltpu.VMEM((128, 2048), low),
         sending=pltpu.VMEM(rows, low),
         local=pltpu.VMEM(rows, low),
+        raw_held=pltpu.VMEM(rows, low),
         grads_held=pltpu.VMEM(rows, low),
         produced_held=pltpu.VMEM(rows, low),
         back=pltpu.VMEM(rows, low),
@@ -936,13 +980,13 @@
         gate_held=pltpu.VMEM((2048, 768), low),
         up_held=pltpu.VMEM((2048, 768), low),
         down_held=pltpu.VMEM((2048, 768), low),
-        act=pltpu.VMEM((4, 192, 768), low),
-        gate_back=pltpu.VMEM((4, 192, 768), low),
-        up_back=pltpu.VMEM((4, 192, 768), low),
-        dots=pltpu.VMEM((4, 4, 8, 128), full),
-        dots_in=pltpu.VMEM((4, 4, 8, 128), full),
-        send=pltpu.SemaphoreType.DMA((45,)),
-        recv=pltpu.SemaphoreType.DMA((45,)),
+        act=pltpu.VMEM((2, 384, 768), low),
+        gate_back=pltpu.VMEM((2, 384, 768), low),
+        up_back=pltpu.VMEM((2, 384, 768), low),
+        dots=pltpu.VMEM((2, 2, 4, 8, 128), full),
+        dots_in=pltpu.VMEM((2, 2, 4, 8, 128), full),
+        send=pltpu.SemaphoreType.DMA((49,)),
+        recv=pltpu.SemaphoreType.DMA((49,)),
         here=pltpu.SemaphoreType.DMA((8,)),
     )
     return call(moe_kernel, 1, far, near, outs, far_outs, scratch)
@@ -983,13 +1027,35 @@
     fetch.start("w_out", r.w_out, r.out_weight)
     beside = me.at(z=me.z + 1 - 2 * me.z_lo)
     right, left = me.at(x=me.x_by(1)), me.at(x=me.x_by(3))
-    greet([right, left, beside] + [one[4] for one in peers(me)])
+    greeted = greet([right, left, beside] + peers(me))
+    gains = r.gain_rows
+    gains[...] = wide(r.attn_gain)
+
+    token_table(r.ids, r.gates, r.capacity, r.table, r.info)
+    rows = r.rows
+    rows[96:, :] = jnp.zeros((32, 2048), low)
+    rows[:96, :] = fetch.cotangent[...].reshape(96, 2048)
+    for core in range(2):
+        dispatch(r.table, rows, r.sending, core)
+    greeted()
+    arrivals = []
+
+    def set_out(first, second):
+        for a, b in OFFSETS:
+            if a in (first, second):
+                spot, device = peer(me, a, b)
+                arrivals.append(net.copy(r.info.at[spot], r.info_in.at[me.spot], device))
+                arrivals.append(net.copy(r.sending.at[spot], r.grads.at[me.spot], device))
+
+    set_out(0, 1)
+    r.info_in[me.spot] = r.info[me.spot]
+    own_grads = net.load(r.sending.at[me.spot], r.grads.at[me.spot])
 
     hidden, normed = fetch.hidden, r.normed
     for s in range(3):
         values = hidden[s].astype(full)
         root = lax.rsqrt(jnp.mean(values * values, axis=-1, keepdims=True) + epsilon)
-        normed[s * 128 : s * 128 + 128, :] = (values * root * r.gains[0:1, :]).astype(low)
+        normed[s * 128 : s * 128 + 128, :] = (values * root * gains[...]).astype(low)
 
     def rope(values):
         cosine = jnp.concatenate([fetch.cosine[...]] * 3, axis=0)
@@ -1002,7 +1068,7 @@
     pair, key_raw = r.pair_held, r.key_raw
     made = jnp.dot(normed[...], fetch.w_pair[...], preferred_element_type=full)
     key_raw[...] = made
-    keys = rope(head_norm(made, r.head_gains[1:2, :])).astype(low)
+    keys = rope(head_norm(made, r.key_gain[...].astype(full))).astype(low)
     values = jnp.dot(normed[...], fetch.w_value[...], preferred_element_type=full).astype(low)
     own = pl.ds(pl.multiple_of(me.context * 128, 128), 128)
     pair[0, :, own, :] = keys.reshape(3, 128, 128)
@@ -1023,20 +1089,7 @@
     from_left = [pass_on(piece(me.x, own_z), right)]
     from_right = [pass_on(piece(me.x, own_z), left)]
 
-    token_table(r.ids, r.gates, r.capacity, r.table, r.info)
-    arrivals = []
-    for a, b, dp, y, device in peers(me):
-        arrivals.append(net.copy(r.info.at[dp, y], r.info_in.at[me.dp, me.y], device))
-    r.info_in[me.dp, me.y] = r.info[me.dp, me.y]
-    rows = r.rows
-    rows[96:, :] = jnp.zeros((32, 2048), low)
-    rows[:96, :] = fetch.cotangent[...].reshape(96, 2048)
-    from_z.wait_recv()
-    from_left.append(pass_on(piece(me.x, other_z), right))
-    from_right.append(pass_on(piece(me.x, other_z), left))
-    for a, b, dp, y, device in dispatch(me, r.table, rows, r.sending):
-        arrivals.append(net.copy(r.sending.at[dp, y], r.grads.at[me.dp, me.y], device))
-    own_grads = net.load(r.sending.at[me.dp, me.y], r.grads.at[me.dp, me.y])
+    set_out(2, 3)
 
     w_query, query, query_raw = fetch.w_query, r.query_held, r.query_raw_held
 
@@ -1046,12 +1099,15 @@
         query_raw[:, columns] = made
         for half in range(2):
             run = pl.ds(pl.multiple_of(step * 256 + half * 128, 128), 128)
-            one = head_norm(made[:, half * 128 : half * 128 + 128], r.head_gains[0:1, :])
+            one = head_norm(made[:, half * 128 : half * 128 + 128], r.query_gain[...].astype(full))
             query[:, run] = rope(one).astype(low)
         return carry
 
     lax.fori_loop(0, 4, project, 0)
     written = [net.load(query, r.query), net.load(query_raw, r.query_raw)]
+    from_z.wait_recv()
+    from_left.append(pass_on(piece(me.x, other_z), right))
+    from_right.append(pass_on(piece(me.x, other_z), left))
     far = [[], []]
     for spot, zs in enumerate((own_z, other_z)):
         from_left[spot].wait_recv()
@@ -1145,14 +1201,14 @@
 
 def front(far, near):
     low, full = jnp.bfloat16, jnp.float32
-    rows = (4, 4, 48, 2048)
+    rows = (2, 2, 4, 48, 2048)
     outs = dict(
         key_raw=jax.ShapeDtypeStruct((384, 128), full),
         log_sum=jax.ShapeDtypeStruct((24, 1, 128), full),
         peaks=jax.ShapeDtypeStruct((8, 128), full),
         after=jax.ShapeDtypeStruct((96, 2048), full),
         table=jax.ShapeDtypeStruct((768, 128), low),
-        info_in=jax.ShapeDtypeStruct((4, 4, 8, 128), full),
+        info_in=jax.ShapeDtypeStruct((2, 2, 4, 8, 128), full),
     )
     far_outs = dict(
         query=jax.ShapeDtypeStruct((384, 1024), low),
@@ -1162,6 +1218,7 @@
         grads=jax.ShapeDtypeStruct(rows, low),
     )
     scratch = dict(
+        gain_rows=pltpu.VMEM((1, 2048), full),
         hidden_held=pltpu.VMEM((3, 128, 2048), low),
         key_weight=pltpu.VMEM((2048, 128), low),
         value_weight=pltpu.VMEM((2048, 128), low),
@@ -1172,7 +1229,7 @@
         out_weight=pltpu.VMEM((2048, 1024), low),
         normed=pltpu.VMEM((384, 2048), low),
         pair_held=pltpu.VMEM((2, 3, 1024, 128), low),
-        info=pltpu.VMEM((4, 4, 8, 128), full),
+        info=pltpu.VMEM((2, 2, 4, 8, 128), full),
         rows=pltpu.VMEM((128, 2048), low),
         sending=pltpu.VMEM(rows, low),
         query_held=pltpu.VMEM((384, 1024), low),
@@ -1188,6 +1245,58 @@
         here=pltpu.SemaphoreType.DMA((16,)),
     )
     return call(front_kernel, 2, far, near, outs, far_outs, scratch)
+
+
+def finish_kernel(names, *refs):
+    r = types.SimpleNamespace(**dict(zip(names, refs, strict=True)))
+    r.layer_out[...] = r.after[...] + r.moe_out[...]
+    r.input_grad[...] = r.after_grad[...] + r.normed_out[...].reshape(96, 2048)
+    r.gate_w[...] = r.gate_part[...]
+    r.up_w[...] = r.up_part[...]
+    r.down_w[...] = r.down_part[...]
+    r.query_w[...] = r.query_part[...]
+    r.out_w[...] = r.out_part[...]
+    r.gate_grad[...] = r.gate_grad_part[...]
+    r.key_w[...] = r.pair_w[:, :128]
+    r.value_w[...] = r.pair_w[:, 128:]
+    r.attn_gain[...] = r.small[:16]
+    r.moe_gain[...] = r.small[16:32]
+    r.query_gain[...] = r.small[32:33]
+    r.key_gain[...] = r.small[33:34]
+    diagonal = lax.broadcasted_iota(jnp.int32, (8, 128), 0) == lax.broadcasted_iota(
+        jnp.int32, (8, 128), 1
+    )
+    peaks = jnp.sum(jnp.where(diagonal, r.small[40:], 0.0), axis=0, keepdims=True)
+    r.clip[...] = (clip_limit / jnp.maximum(peaks, clip_limit))[:, :8]
+
+
+def finish(near):
+    outs = dict(
+        layer_out=(96, 2048),
+        input_grad=(96, 2048),
+        gate_w=(256, 768),
+        up_w=(256, 768),
+        down_w=(256, 768),
+        query_w=(64, 1024),
+        out_w=(64, 1024),
+        gate_grad=(3, 8, 32),
+        key_w=(64, 128),
+        value_w=(64, 128),
+        attn_gain=(16, 128),
+        moe_gain=(16, 128),
+        query_gain=(1, 128),
+        key_gain=(1, 128),
+        clip=(1, 8),
+    )
+    results = pl.pallas_call(
+        functools.partial(finish_kernel, list(near) + list(outs)),
+        out_shape=[jax.ShapeDtypeStruct(size, jnp.float32) for size in outs.values()],
+        in_specs=[VMEM] * len(near),
+        out_specs=[VMEM] * len(outs),
+        compiler_params=pltpu.CompilerParams(vmem_limit_bytes=62 << 20),
+        name="finish",
+    )(*near.values())
+    return types.SimpleNamespace(**dict(zip(outs, results, strict=True)))
 
 
 def shards(
@@ -1209,9 +1318,9 @@
     w_down,
     cotangent,
 ):
-    full = jnp.float32
-    gains = jnp.stack([attn_gain, moe_gain]).astype(full)
-    head_gains = jnp.stack([query_gain, key_gain]).astype(full)
+    attn_wide, moe_wide = attn_gain.reshape(16, 128), moe_gain.reshape(16, 128)
+    query_row, key_row = query_gain[None], key_gain[None]
+    ids, gates = expert_ids.swapaxes(1, 2), gate_values.swapaxes(1, 2)
     cosine, sine = rotary()
     first = front(
         dict(
@@ -1225,11 +1334,12 @@
             w_out=w_out,
         ),
         dict(
-            gains=gains,
-            head_gains=head_gains,
+            attn_gain=attn_wide,
+            query_gain=query_row,
+            key_gain=key_row,
             segments=segments,
-            ids=expert_ids,
-            gates=gate_values,
+            ids=ids,
+            gates=gates,
             capacity=capacity,
         ),
     )
@@ -1238,8 +1348,8 @@
         dict(
             after=first.after,
             cotangent=cotangent,
-            gains=gains,
-            ids=expert_ids,
+            moe_gain=moe_wide,
+            ids=ids,
             table=first.table,
             info_in=first.info_in,
         ),
@@ -1253,6 +1363,7 @@
             up=second.full_up.reshape(4, 2, 256, 768),
             down=second.full_down.reshape(4, 2, 256, 768),
             produced=second.produced,
+            gate_begun=second.gate_slots,
             hidden=hidden_in,
             mixed=first.mixed,
             query=first.query,
@@ -1268,28 +1379,38 @@
             key_raw=first.key_raw,
             log_sum=first.log_sum,
             segments=segments,
-            head_gains=head_gains,
-            gains=gains,
+            attn_gain=attn_wide,
+            query_gain=query_row,
+            key_gain=key_row,
             moe_gain_part=second.gain_part,
             peaks=first.peaks,
         ),
     )
-    own_shape = cotangent.shape
-    layer_out = first.after.reshape(own_shape) + done.moe_out.reshape(own_shape)
-    input_grad = second.after_grad.reshape(own_shape) + done.normed_out
-    gate_grad = second.gate_grad
-    w_key_grad, w_value_grad = done.pair_w_out[:, :128], done.pair_w_out[:, 128:]
-    w_query_grad, w_out_grad = done.query_w_out, done.out_w_out
-    w_gate_grad, w_up_grad, w_down_grad = (
-        done.gate_out[None],
-        done.up_out[None],
-        done.down_out[None],
-    )
-    small = done.small_out
-    attn_gain_grad = small[:16].reshape(2048)
-    moe_gain_grad = small[16:32].reshape(2048)
-    query_gain_grad, key_gain_grad = small[32], small[33]
-    head_clip_scale = clip_limit / jnp.maximum(small[40:, 0], clip_limit)
+    last = finish(
+        dict(
+            after=first.after,
+            moe_out=done.moe_out,
+            after_grad=second.after_grad,
+            normed_out=done.normed_out,
+            small=done.small_out,
+            pair_w=done.pair_w_out,
+            gate_part=done.gate_out,
+            up_part=done.up_out,
+            down_part=done.down_out,
+            query_part=done.query_w_out,
+            out_part=done.out_w_out,
+            gate_grad_part=second.gate_grad,
+        )
+    )
+    layer_out = last.layer_out.reshape(cotangent.shape)
+    input_grad = last.input_grad.reshape(cotangent.shape)
+    gate_grad = last.gate_grad.swapaxes(1, 2)
+    w_key_grad, w_value_grad = last.key_w, last.value_w
+    w_query_grad, w_out_grad = last.query_w, last.out_w
+    w_gate_grad, w_up_grad, w_down_grad = last.gate_w[None], last.up_w[None], last.down_w[None]
+    attn_gain_grad, moe_gain_grad = last.attn_gain.reshape(2048), last.moe_gain.reshape(2048)
+    query_gain_grad, key_gain_grad = last.query_gain.reshape(128), last.key_gain.reshape(128)
+    head_clip_scale = last.clip.reshape(8)
     return (
         layer_out,
         input_grad,

time: 344 us -> 296 us (0.86)
  Pallas kernels: 324 us -> 294 us
  local copies, waits for them, and re-layouts: 11.7 us -> 0 us
  other arithmetic: 6.9 us -> 0 us
    pallas_call x3, Pallas kernels: 324 us -> 289 us  [call(): pl.pallas_call(functools.partial(kernel, names), out_shape=list(shapes.va...]
    unnamed x26 -> x0, local copies, waits for them, and re-layouts: 8.54 us -> none
    pallas_call x0 -> x1, Pallas kernels: none -> 4.93 us  [finish(): pl.pallas_call(functools.partial(finish_kernel, list(near) + list(outs)),...]
    add x2 -> x0, other arithmetic: 4.4 us -> none  [the longest x1 2.21 us: shards(): input_grad = second.after_grad.reshape(own_shape) + done.normed_out]
where the time goes in v5:
time: 296 us; the launch traced here: 295 us
  Pallas kernels  294 us (99%)
    pallas_call x3, Pallas kernels, call(): pl.pallas_call(functools.partial(kernel, names), out_shape=list(shapes.va...  289 us

profile of v5, /device:TPU:0, one launch (start us, length us, event | category | flops | bytes accessed | tf_op | source)
XLA Modules:
  0.0 294.5 jit_solution(11281310973024499222)
XLA Ops:
  0.6 66.3 %front_kernel.1 = (f32[384,128]{1,0:T(8,128)}, f32[24,1,128]{2,1,0:T(1,128)}, f32[8,128]{1,0:T(8,128)}, f32[96,2048]{1,0:T(8,128)}, bf16[768,128]{1,0:T(8,128)(2...) custom-call(bf16[3,128,2048]{2,1,0:T(8,128)(2,1)} %refs_8_.1, ...), custom_call_target="tpu_custom_call" | custom-call | tf_op jit(solution)/shard_map/front_kernel/pallas_call | solution.py:998
  67.0 92.2 %moe_kernel.1 = (f32[96,2048]{1,0:T(8,128)}, bf16[3,32,2048]{2,1,0:T(8,128)(2,1)}, f32[1,2048]{1,0:T(1,128)}, f32[3,8,32]{2,1,0:T(8,128)}, bf16[2,2,4,48,2048]{4...) custom-call(bf16[2048,768]{1,0:T(8,128)(2,1)} %bitcast.26, ...), custom_call_target="tpu_custom_call" | custom-call | tf_op jit(solution)/shard_map/moe_kernel/pallas_call | solution.py:998
  159.2 130.3 %back_kernel.1 = (f32[256,768]{1,0:T(8,128)}, f32[256,768]{1,0:T(8,128)}, f32[256,768]{1,0:T(8,128)}, f32[64,1024]{1,0:T(8,128)}, f32[64,256]{1,0:T(8,128)}, /*i...) custom-call(bf16[3,32,2048]{2,1,0:T(8,128)(2,1)} %get-tuple-element., ...), custom_call_target="tpu_custom_call" | custom-call | tf_op jit(solution)/shard_map/back_kernel/pallas_call | solution.py:998
  289.4 4.9 %finish.1 = (f32[96,2048]{1,0:T(8,128)}, f32[96,2048]{1,0:T(8,128)}, f32[256,768]{1,0:T(8,128)}, f32[256,768]{1,0:T(8,128)}, f32[256,768]{1,0:T(8,128)}, /*index...) custom-call(f32[96,2048]{1,0:T(8,128)} %get-tuple-element.59.refs_4_, ...), custom_call_target="tpu_custom_call" | custom-call | tf_op jit(solution)/shard_map/finish/pallas_call | solution.py:1291

commit v6 on v5

--- a/solution.py
+++ b/solution.py
@@ -139,24 +139,30 @@
 
 def ring_reduce(net, plus, minus, own, slots, target, held=None, begun=None):
     held = own if held is None else held
-    if begun is None:
+    done = 0 if begun is None else begun.shape[0]
+    if done == 4:
+        loads = [net.load(begun, slots.at[pl.ds(0, 4)])]
+    elif done == 2:
+        loads = [net.load(begun.at[step], slots.at[step * 2]) for step in range(2)]
+    else:
         first_plus = net.copy(own(2, 0), slots.at[0], plus)
         first_minus = net.copy(own(2, 1), slots.at[2], minus)
+    if done != 4:
         side_plus = net.copy(own(1, 1), slots.at[1], plus)
         side_minus = net.copy(own(3, 0), slots.at[3], minus)
-        yield
+    yield
+    if done:
+        for load in loads:
+            load.wait()
+    else:
         first_plus.wait_recv()
         first_minus.wait_recv()
-    else:
-        load = net.load(begun, slots.at[pl.ds(0, 4)])
-        yield
-        load.wait()
     add_into(slots.at[0], [slots.at[0], held(1, 0)])
     last_plus = net.copy(slots.at[0], slots.at[4], plus)
     add_into(slots.at[2], [slots.at[2], held(3, 1)])
     last_minus = net.copy(slots.at[2], slots.at[5], minus)
     yield
-    if begun is None:
+    if done != 4:
         side_minus.wait_recv()
         side_plus.wait_recv()
     last_plus.wait_recv()
@@ -357,13 +363,29 @@
         net, me, r.gate, r.gate_slots, r.gate_middle, r.gate_other, r.gate_out, r.gate_held,
         r.gate_begun,
     )
-    up = x_first(net, me, r.up, r.up_slots, r.up_middle, r.up_other, r.up_out, r.up_held)
+    up = x_first(
+        net, me, r.up, r.up_slots, r.up_middle, r.up_other, r.up_out, r.up_held, r.up_begun
+    )
     down = x_first(
         net, me, r.down, r.down_slots, r.down_middle, r.down_other, r.down_out, r.down_held
     )
     next(gate)
+    next(gate)
     next(up)
-    next(gate)
+    produced, home, table = r.produced, r.home, r.table
+    start = me.core * 384 + me.z_hi * 192 + me.y * 48
+    mine = pl.ds(pl.multiple_of(start, 16), 48)
+    home_came = []
+
+    def bring_home(offsets):
+        for a, b in offsets:
+            spot, device = peer(me, a, b)
+            home_came.append(net.copy(produced.at[spot], home.at[mine], device))
+
+    straight = [(2, 0), (3, 0)]
+    bring_home(straight)
+    home_own = net.load(produced.at[me.spot], home.at[mine])
+    next(up)
     fetch.start("pair", r.pair, r.pair_held)
     fetch.start("query", r.query, r.query_held)
     fetch.start("query_raw", r.query_raw, r.query_raw_held)
@@ -379,6 +401,10 @@
         values = hidden[s].astype(full)
         root = lax.rsqrt(jnp.mean(values * values, axis=-1, keepdims=True) + epsilon)
         inverse[rows, :] = jnp.broadcast_to(root, (128, 128))
+        for step in range(8):
+            run = slice(step * 256, step * 256 + 256)
+            tile = hidden[s, :, run].astype(full) * root * gains[:, run]
+            r.normed[run, rows] = tile.T.astype(low)
 
     first, second = pl.ds(0, 1024), pl.ds(1024, 1024)
     to_above.wait_recv()
@@ -389,8 +415,11 @@
     far_below = net.copy(passed, passed, below)
     own_branch.wait()
     load_out.wait()
+    next(gate)
     far_above.wait_recv()
     far_below.wait_recv()
+
+    bring_home([offset for offset in OFFSETS if offset not in straight])
 
     heads_grad = r.heads_grad
 
@@ -404,17 +433,45 @@
     lax.fori_loop(0, 4, heads_step, 0)
     load_query = net.load(r.w_query, weight)
 
-    produced, home, table = r.produced, r.home, r.table
-    start = me.core * 384 + me.z_hi * 192 + me.y * 48
-    mine = pl.ds(pl.multiple_of(start, 16), 48)
-    home_came = []
-    for a, b in OFFSETS:
-        spot, device = peer(me, a, b)
-        home_came.append(net.copy(produced.at[spot], home.at[mine], device))
-    home_own = net.load(produced.at[me.spot], home.at[mine])
+    query_low = heads_grad
+
+    def own_input(columns):
+        return hidden[:, :, columns].reshape(384, 256).astype(full)
+
+    def normed(columns, right):
+        return jnp.dot(r.normed[columns, :], right, preferred_element_type=full)
+
+    def whole_part(columns):
+        return whole[:, :, :, columns].reshape(384, 256)
+
+    def branch_weight(columns, right):
+        return contract_first(whole_part(columns), right)
+
+    def weigh(core, left, right, target):
+        def body(step, carry):
+            z_hi, part = step // 2, lax.rem(step, 2)
+            columns = pl.ds(pl.multiple_of((z_hi * 2 + core) * 512 + part * 256, 256), 256)
+            made = left(columns, right[...]).astype(low)
+            target[z_hi, pl.ds(part * 2, 2)] = made.reshape(2, 2, 64, right.shape[1])
+            return carry
+
+        lax.fori_loop(0, 4, body, 0)
+
+    def dense(order, left, right, sending, other, middle, *more):
+        weigh(1 - me.core, left, right, sending)
+        task = order(net, me, sending, other, middle, *more)
+        next(task)
+        weigh(me.core, left, right, middle)
+        return task
+
+    out_w = dense(
+        dense_z_first, branch_weight, fetch.mixed, r.sending, r.out_w_other, r.out_w_middle,
+        r.out_w_slots, r.out_w_corner, r.out_w_last, r.out_w_out,
+    )
+    next(down)
 
     query, query_raw, pair = fetch.query, fetch.query_raw, fetch.pair
-    cosine, sine, mixed = fetch.cosine, fetch.sine, fetch.mixed
+    cosine, sine = fetch.cosine, fetch.sine
     gain_query, gain_key = r.query_gain[...].astype(full), r.key_gain[...].astype(full)
     bias, key_sum, value_sum = r.bias, r.key_sum, r.value_sum
     pair_grad, gain_part = r.pair_grad, r.gain_part
@@ -463,81 +520,63 @@
             return carry
 
         lax.fori_loop(0, 4, two_heads, 0)
-        pair_grad[:, :, 0, s] = (key_sum[...] * score_scale).astype(low).reshape(4, 2, 128, 128)
-        pair_grad[:, :, 1, s] = value_sum[...].astype(low).reshape(4, 2, 128, 128)
-
-    attend(0)
-    attend(1)
-    attend(2)
-    pairs = x_first(
-        net, me, pair_grad, r.pair_slots, r.pair_middle, r.pair_other,
-        r.pair_out,
-    )
-    next(pairs)
-    next(gate)
-
-    query_low = heads_grad
-
-    def own_input(columns):
-        return hidden[:, :, columns].reshape(384, 256).astype(full)
-
-    def normed(columns):
-        return (own_input(columns) * inverse[:, 0:1] * gains[:, columns]).astype(low)
-
-    def whole_part(columns):
-        return whole[:, :, :, columns].reshape(384, 256)
-
-    def weigh(core, left, right, target):
-        def body(step, carry):
-            z_hi, part = step // 2, lax.rem(step, 2)
-            columns = pl.ds(pl.multiple_of((z_hi * 2 + core) * 512 + part * 256, 256), 256)
-            made = contract_first(left(columns), right[...]).astype(low)
-            target[z_hi, pl.ds(part * 2, 2)] = made.reshape(2, 2, 64, right.shape[1])
-            return carry
-
-        lax.fori_loop(0, 4, body, 0)
-
-    def dense(order, left, right, sending, other, middle, *more):
-        weigh(1 - me.core, left, right, sending)
-        task = order(net, me, sending, other, middle, *more)
-        next(task)
-        weigh(me.core, left, right, middle)
-        return task
-
-    out_w = dense(
-        dense_z_first, whole_part, mixed, r.sending, r.out_w_other, r.out_w_middle, r.out_w_slots, r.out_w_corner,
-        r.out_w_last, r.out_w_out,
-    )
-    next(pairs)
-    next(down)
+        pair_grad[s, :, :, 0] = (key_sum[...] * score_scale).astype(low).reshape(4, 2, 128, 128)
+        pair_grad[s, :, :, 1] = value_sum[...].astype(low).reshape(4, 2, 128, 128)
+        return x_first(
+            net, me, pair_grad.at[s], r.pair_slots.at[s], r.pair_middle.at[s], r.pair_other.at[s],
+            r.pair_out.at[s],
+        )
+
+    pairs = [attend(0)]
+    next(pairs[0])
     next(out_w)
+    pairs.append(attend(1))
+    next(pairs[1])
+    next(pairs[0])
+    next(up)
+    pairs.append(attend(2))
+    next(pairs[2])
+    next(pairs[1])
+    next(pairs[0])
+
     query_w = dense(
-        dense_x_first, normed, query_low, r.sending, r.query_w_other, r.query_w_middle, r.query_w_slots, r.query_w_corner,
-        r.query_w_last, r.query_w_out,
-    )
-    next(pairs)
-    next(up)
+        dense_x_first, normed, query_low, r.sending, r.query_w_other, r.query_w_middle,
+        r.query_w_slots, r.query_w_corner, r.query_w_last, r.query_w_out,
+    )
+    next(pairs[2])
+    next(pairs[1])
     next(query_w)
-
-    pair_out, key_raw, pair_low = r.pair_out, r.key_raw, r.pair_low
-    next(pairs, None)
-    for s in range(3):
-        rows = slice(s * 128, s * 128 + 128)
-        grad, part = norm_back(rope_back(pair_out[0, s]), key_raw[rows, :], gain_key)
-        gain_part[1:2, :] += part
-        pair_low[rows, :128] = grad.astype(low)
-        pair_low[rows, 128:] = pair_out[1, s].astype(low)
+    next(pairs[2])
 
     load_query.wait()
     net.sent(far_above)
     net.sent(far_below)
+
+    def query_step(step, carry):
+        columns = pl.ds(pl.multiple_of(step * 256, 256), 256)
+        made = contract_last(query_low[...], weight[columns, :])
+        whole[:, :, :, columns] = made.astype(low).reshape(3, 4, 32, 256)
+        return carry
+
+    lax.fori_loop(0, 8, query_step, 0)
+    next(down)
+
+    pair_out, key_raw, pair_low = r.pair_out, r.key_raw, r.pair_low
+    for s in range(3):
+        next(pairs[s], None)
+        rows = slice(s * 128, s * 128 + 128)
+        grad, part = norm_back(rope_back(pair_out[s, 0]), key_raw[rows, :], gain_key)
+        gain_part[1:2, :] += part
+        pair_low[rows, :128] = grad.astype(low)
+        pair_low[rows, 128:] = pair_out[s, 1].astype(low)
+
     w_key, w_value = fetch.w_key, fetch.w_value
     small = r.small
     normed_part = r.normed_part
 
     def normed_step(step, carry):
         columns = pl.ds(pl.multiple_of(step * 256, 256), 256)
-        made = contract_last(query_low[...], weight[columns, :])
+        made = whole_part(columns).astype(full)
         made = made + contract_last(pair_low[:, :128], w_key[columns, :])
         made = made + contract_last(pair_low[:, 128:], w_value[columns, :])
         normal = own_input(columns) * inverse[:, 0:1]
@@ -565,27 +604,11 @@
     smalls = all_small(
         net, me, small, r.by_core, r.by_x, r.by_z, r.by_y, r.small_out
     )
-    next(smalls)
     pair_w = dense(
-        dense_x_first, normed, pair_low, r.pair_sending, r.pair_w_other, r.pair_w_middle, r.pair_w_slots, r.pair_w_corner,
-        r.pair_w_last, r.pair_w_out,
-    )
-    next(smalls)
-
-    def rest(*tasks):
-        for task in tasks:
-            next(task, None)
-
-    rest(out_w, pair_w, smalls, normed_sum, gate, up, down, query_w)
-
-    next(normed_sum, None)
-    for s in range(3):
-        rows = pl.ds(pl.multiple_of(me.y * 32, 32), 32)
-        grad, _ = norm_back(normed_out[s], hidden[s, rows, :].astype(full), gains[...])
-        normed_out[s] = grad
-
-    rest(pair_w, smalls, out_w, up, down, query_w)
-    rest(pair_w, smalls, out_w, query_w)
+        dense_x_first, normed, pair_low, r.pair_sending, r.pair_w_other, r.pair_w_middle,
+        r.pair_w_slots, r.pair_w_corner, r.pair_w_last, r.pair_w_out,
+    )
+    next(out_w)
 
     for made in home_came:
         made.wait_recv()
@@ -594,7 +617,8 @@
         net.load(home.at[:, pl.ds(half * 1024, 1024)], weight.at[pl.ds(half * 768, 768)])
         for half in range(2)
     ]
-    rest(pair_w, smalls, out_w, query_w, down)
+    next(pair_w)
+    next(smalls)
     moe_out = r.moe_out
     for half in range(2):
         home_loads[half].wait()
@@ -606,6 +630,21 @@
             return carry
 
         lax.fori_loop(0, 4, gather, 0)
+
+    def rest(*tasks):
+        for task in tasks:
+            next(task, None)
+
+    rest(normed_sum, query_w, out_w, down, smalls)
+
+    next(normed_sum, None)
+    for s in range(3):
+        rows = pl.ds(pl.multiple_of(me.y * 32, 32), 32)
+        grad, _ = norm_back(normed_out[s], hidden[s, rows, :].astype(full), gains[...])
+        normed_out[s] = grad
+
+    rest(pair_w, out_w, query_w, down, smalls, gate, up)
+    rest(pair_w, out_w, query_w, smalls)
     tasks = [pair_w, out_w, smalls, query_w, gate, up, down]
     while tasks:
         for task in list(tasks):
@@ -652,15 +691,16 @@
         whole=pltpu.VMEM((3, 4, 32, 2048), low),
         weight=pltpu.VMEM((2048, 1024), low),
         inverse=pltpu.VMEM((384, 128), full),
+        normed=pltpu.VMEM((2048, 384), low),
         heads_grad=pltpu.VMEM((384, 1024), low),
         bias=pltpu.VMEM((128, 1024), full),
         key_sum=pltpu.VMEM((1024, 128), full),
         value_sum=pltpu.VMEM((1024, 128), full),
-        pair_grad=pltpu.VMEM((4, 2, 2, 3, 128, 128), low),
-        pair_slots=pltpu.VMEM((6, 2, 3, 128, 128), low),
-        pair_middle=pltpu.VMEM((2, 2, 3, 128, 128), low),
-        pair_other=pltpu.VMEM((2, 3, 128, 128), low),
-        pair_out=pltpu.VMEM((2, 3, 128, 128), full),
+        pair_grad=pltpu.VMEM((3, 4, 2, 2, 128, 128), low),
+        pair_slots=pltpu.VMEM((3, 6, 2, 128, 128), low),
+        pair_middle=pltpu.VMEM((3, 2, 2, 128, 128), low),
+        pair_other=pltpu.VMEM((3, 2, 128, 128), low),
+        pair_out=pltpu.VMEM((3, 2, 128, 128), full),
         pair_low=pltpu.VMEM((384, 256), low),
         gain_part=pltpu.VMEM((8, 128), full),
         normed_part=pltpu.VMEM((1, 2048), full),
@@ -699,8 +739,8 @@
         out_w_slots=None,
         out_w_corner=None,
         out_w_last=None,
-        send=pltpu.SemaphoreType.DMA((104,)),
-        recv=pltpu.SemaphoreType.DMA((104,)),
+        send=pltpu.SemaphoreType.DMA((116,)),
+        recv=pltpu.SemaphoreType.DMA((116,)),
         here=pltpu.SemaphoreType.DMA((34,)),
     )
     dense = dense_slots(1024, (2, 2)) + dense_slots(256, (2, 2)) + dense_slots(1024, (4,))
@@ -806,7 +846,26 @@
     w_gate, w_up, grads, w_down = fetch.w_gate, fetch.w_up, r.grads_held, fetch.w_down
     fetch.raw
     spot = lax.broadcasted_iota(jnp.int32, (48, 128), 0).astype(full)
-    back_came, dots_came = {}, {}
+    back_came, dots_came, round_x, written = {}, {}, [], []
+    right, left = me.at(x=me.x_by(1)), me.at(x=me.x_by(3))
+
+    def weigh(first, group, entered, given, target):
+        def body(step, carry):
+            columns = pl.ds(pl.multiple_of(step * 256, 256), 256)
+            made = contract_first(
+                entered[group, :, :, :, columns].reshape(384, 256), given[group]
+            )
+            if first == 1:
+                made = made + target[columns, :].astype(full)
+            target[columns, :] = made.astype(low)
+            return carry
+
+        lax.fori_loop(0, 8, body, 0)
+
+    def chunk(target, step, half):
+        start = (me.x_by(step) * 2 + half) * 256
+        return target.at[pl.ds(pl.multiple_of(start, 256), 256)]
+
     for first in (0, 1):
         group = me.core if first == 0 else 1 - me.core
         for a in (first, first + 2):
@@ -874,6 +933,21 @@
                 if a or b:
                     place, device = peer(me, a, b)
                     back_came[a, b] = net.copy(back.at[place], home.at[me.spot], device)
+        if first == 1:
+            weigh(first, group, local, gate_back, r.gate_held)
+            round_x += [
+                net.copy(chunk(r.gate_held, 2, 0), r.gate_slots.at[0], right),
+                net.copy(chunk(r.gate_held, 2, 1), r.gate_slots.at[2], left),
+                net.copy(chunk(r.gate_held, 1, 1), r.gate_slots.at[1], right),
+                net.copy(chunk(r.gate_held, 3, 0), r.gate_slots.at[3], left),
+            ]
+            written.append(net.load(r.gate_held, r.full_gate))
+            weigh(first, group, local, up_back, r.up_held)
+            round_x += [
+                net.copy(chunk(r.up_held, 2, 0), r.up_slots.at[0], right),
+                net.copy(chunk(r.up_held, 2, 1), r.up_slots.at[1], left),
+            ]
+            written.append(net.load(r.up_held, r.full_up))
         dot = lax.fori_loop(0, 8, finals, jnp.zeros((384, 1), full))
         for place in range(8):
             line = jnp.where(masks[place], dot[place * 48 : place * 48 + 48], 0.0)
@@ -884,36 +958,14 @@
                 if a or b:
                     place, device = peer(me, a, b)
                     dots_came[a, b] = net.copy(r.dots.at[place], r.dots_in.at[me.spot], device)
+        if first == 0:
+            weigh(first, group, local, gate_back, r.gate_held)
+            weigh(first, group, local, up_back, r.up_held)
+        weigh(first, group, grads, act, r.down_held)
+    written.append(net.load(r.produced_held, r.produced))
+    written.append(net.load(r.down_held, r.full_down))
     home[me.spot] = back[me.spot]
     r.dots_in[me.spot] = r.dots[me.spot]
-    written = [net.load(r.produced_held, r.produced)]
-
-    def weigh(left, right, target):
-        def body(step, carry):
-            columns = pl.ds(pl.multiple_of(step * 256, 256), 256)
-            entered = left[:, :, :, :, columns].reshape(768, 256)
-            target[columns, :] = contract_first(entered, right[...].reshape(768, 768)).astype(low)
-            return carry
-
-        lax.fori_loop(0, 8, body, 0)
-
-    def chunk(step, half):
-        start = (me.x_by(step) * 2 + half) * 256
-        return r.gate_held.at[pl.ds(pl.multiple_of(start, 256), 256)]
-
-    weigh(local, gate_back, r.gate_held)
-    right, left = me.at(x=me.x_by(1)), me.at(x=me.x_by(3))
-    round_x = [
-        net.copy(chunk(2, 0), r.gate_slots.at[0], right),
-        net.copy(chunk(2, 1), r.gate_slots.at[2], left),
-        net.copy(chunk(1, 1), r.gate_slots.at[1], right),
-        net.copy(chunk(3, 0), r.gate_slots.at[3], left),
-    ]
-    written.append(net.load(r.gate_held, r.full_gate))
-    weigh(local, up_back, r.up_held)
-    written.append(net.load(r.up_held, r.full_up))
-    weigh(grads, act, r.down_held)
-    written.append(net.load(r.down_held, r.full_down))
 
     for offset in OFFSETS:
         dots_came[offset].wait_recv()
@@ -964,6 +1016,7 @@
         full_up=jax.ShapeDtypeStruct((2048, 768), low),
         full_down=jax.ShapeDtypeStruct((2048, 768), low),
         gate_slots=jax.ShapeDtypeStruct((4, 256, 768), low),
+        up_slots=jax.ShapeDtypeStruct((2, 256, 768), low),
     )
     scratch = dict(
         rows=pltpu.VMEM((128, 2048), low),
@@ -985,8 +1038,8 @@
         up_back=pltpu.VMEM((2, 384, 768), low),
         dots=pltpu.VMEM((2, 2, 4, 8, 128), full),
         dots_in=pltpu.VMEM((2, 2, 4, 8, 128), full),
-        send=pltpu.SemaphoreType.DMA((49,)),
-        recv=pltpu.SemaphoreType.DMA((49,)),
+        send=pltpu.SemaphoreType.DMA((51,)),
+        recv=pltpu.SemaphoreType.DMA((51,)),
         here=pltpu.SemaphoreType.DMA((8,)),
     )
     return call(moe_kernel, 1, far, near, outs, far_outs, scratch)
@@ -1003,7 +1056,7 @@
         out_specs=[VMEM] * len(outs) + [ANY] * len(far_outs),
         scratch_shapes=list(scratch.values()),
         compiler_params=pltpu.CompilerParams(
-            collective_id=number, has_side_effects=True, vmem_limit_bytes=62 << 20
+            collective_id=number, has_side_effects=True, vmem_limit_bytes=63 << 20
         ),
         name=kernel.__name__,
     )(*far.values(), *near.values())
@@ -1364,6 +1417,7 @@
             down=second.full_down.reshape(4, 2, 256, 768),
             produced=second.produced,
             gate_begun=second.gate_slots,
+            up_begun=second.up_slots,
             hidden=hidden_in,
             mixed=first.mixed,
             query=first.query,

time: 296 us -> 284 us (0.959)
  Pallas kernels: 294 us -> 283 us
    pallas_call x3, Pallas kernels: 289 us -> 278 us  [call(): pl.pallas_call(functools.partial(kernel, names), out_shape=list(shapes.va...]
where the time goes in v6:
time: 284 us
  Pallas kernels  283 us (100%)
    pallas_call x3, Pallas kernels, call(): pl.pallas_call(functools.partial(kernel, names), out_shape=list(shapes.va...  278 us

profile of v6, /device:TPU:0, one launch (start us, length us, event | category | flops | bytes accessed | tf_op | source)
XLA Modules:
  0.0 283.7 jit_solution(5944201983302026217)
XLA Ops:
  0.6 66.3 %front_kernel.1 = (f32[384,128]{1,0:T(8,128)}, f32[24,1,128]{2,1,0:T(1,128)}, f32[8,128]{1,0:T(8,128)}, f32[96,2048]{1,0:T(8,128)}, bf16[768,128]{1,0:T(8,128)(2...) custom-call(bf16[3,128,2048]{2,1,0:T(8,128)(2,1)} %refs_9_.1, ...), custom_call_target="tpu_custom_call" | custom-call | tf_op jit(solution)/shard_map/front_kernel/pallas_call | solution.py:1051
  67.0 94.9 %moe_kernel.1 = (f32[96,2048]{1,0:T(8,128)}, bf16[3,32,2048]{2,1,0:T(8,128)(2,1)}, f32[1,2048]{1,0:T(1,128)}, f32[3,8,32]{2,1,0:T(8,128)}, bf16[2,2,4,48,2048]{4...) custom-call(bf16[2048,768]{1,0:T(8,128)(2,1)} %bitcast.26, ...), custom_call_target="tpu_custom_call" | custom-call | tf_op jit(solution)/shard_map/moe_kernel/pallas_call | solution.py:1051
  161.9 116.7 %back_kernel.1 = (f32[256,768]{1,0:T(8,128)}, f32[256,768]{1,0:T(8,128)}, f32[256,768]{1,0:T(8,128)}, f32[64,1024]{1,0:T(8,128)}, f32[64,256]{1,0:T(8,128)}, /*i...) custom-call(bf16[3,32,2048]{2,1,0:T(8,128)(2,1)} %get-tuple-element., ...), custom_call_target="tpu_custom_call" | custom-call | tf_op jit(solution)/shard_map/back_kernel/pallas_call | solution.py:1051
  278.6 4.9 %finish.1 = (f32[96,2048]{1,0:T(8,128)}, f32[96,2048]{1,0:T(8,128)}, f32[256,768]{1,0:T(8,128)}, f32[256,768]{1,0:T(8,128)}, f32[256,768]{1,0:T(8,128)}, /*index...) custom-call(f32[96,2048]{1,0:T(8,128)} %get-tuple-element.60.refs_4_, ...), custom_call_target="tpu_custom_call" | custom-call | tf_op jit(solution)/shard_map/finish/pallas_call | solution.py:1344

commit v7 on v6

--- a/solution.py
+++ b/solution.py
@@ -379,12 +379,12 @@
 
     def bring_home(offsets):
         for a, b in offsets:
-            spot, device = peer(me, a, b)
-            home_came.append(net.copy(produced.at[spot], home.at[mine], device))
+            device = peer(me, a, b)[1]
+            home_came.append(net.copy(produced.at[SLOTS[a, b]], home.at[mine], device))
 
     straight = [(2, 0), (3, 0)]
     bring_home(straight)
-    home_own = net.load(produced.at[me.spot], home.at[mine])
+    home_own = net.load(produced.at[0, 0], home.at[mine])
     next(up)
     fetch.start("pair", r.pair, r.pair_held)
     fetch.start("query", r.query, r.query_held)
@@ -802,13 +802,43 @@
         )
 
 
-def dispatch(table, rows, sender, core):
-    rest = table[pl.ds(pl.multiple_of(core * 384, 384), 384), :]
-    columns = 512
-    for step in range(2048 // columns):
-        run = slice(step * columns, (step + 1) * columns)
-        picked = jnp.dot(rest, rows[:, run], preferred_element_type=jnp.float32)
-        sender[core, :, :, :, run] = picked.astype(jnp.bfloat16).reshape(2, 4, 48, columns)
+PHASES = (
+    [(0, 0), (0, 1), (0, 3), (2, 0), (1, 0), (1, 1), (1, 3), (3, 0)],
+    [(0, 2), (2, 1), (2, 3), (2, 2), (1, 2), (3, 1), (3, 3), (3, 2)],
+)
+SLOTS = {offset: (phase, spot) for phase in (0, 1) for spot, offset in enumerate(PHASES[phase])}
+
+
+def spread(net, me, everyone, source, came):
+    above, below = me.at(y=me.y_by(1)), me.at(y=me.y_by(3))
+    sibling = me.at(core=1 - me.core)
+    a, z_hi = (2, 1 - me.z_hi) if source is None else (0, me.z_hi)
+
+    def block(b):
+        return everyone.at[me.core, z_hi, me.y_by(b)]
+
+    def half(b, part):
+        return block(b).at[:, pl.ds(part * 16, 16)]
+
+    def forward(view, device):
+        return net.copy(view, view, device)
+
+    source = block(0) if source is None else source
+    up = net.copy(source, block(0), above)
+    down = net.copy(source, block(0), below)
+    came[a + 1, 0] = net.copy(source, block(0), sibling)
+    yield
+    up.wait_recv()
+    far_up = forward(half(3, 0), above)
+    came[a + 1, 3] = forward(block(3), sibling)
+    down.wait_recv()
+    far_down = forward(half(1, 1), below)
+    came[a + 1, 1] = forward(block(1), sibling)
+    yield
+    far_up.wait_recv()
+    far_down.wait_recv()
+    came[a + 1, 2] = forward(block(2), sibling)
+    yield
 
 
 def moe_kernel(names, *refs):
@@ -819,45 +849,53 @@
     fetch = Fetch(net)
     fetch.start("w_gate", r.w_gate, r.gate_weight)
     fetch.start("w_up", r.w_up, r.up_weight)
-    fetch.start("raw", r.grads, r.raw_held)
+    fetch.start("cots", r.cots, r.cots_held)
     fetch.start("w_down", r.w_down, r.down_weight)
     greeted = greet(peers(me) + [me.at(x=me.x_by(1)), me.at(x=me.x_by(3))])
-    rows, sending, local, table = r.rows, r.sending, r.local, r.table
+    everyone, local, table = r.everyone, r.local, r.table
     values = r.after[...]
     inverse = lax.rsqrt(jnp.mean(values * values, axis=-1, keepdims=True) + epsilon)
     gain = wide(r.moe_gain)
-    rows[96:, :] = jnp.zeros((32, 2048), low)
-    rows[:96, :] = (values * inverse * gain).astype(low)
+    everyone[me.spot] = (values * inverse * gain).astype(low).reshape(3, 32, 2048)
+
+    greeted()
     came = {}
-
-    def set_out(first, second):
-        for a, b in OFFSETS:
-            if a in (first, second):
-                spot, device = peer(me, a, b)
-                came[a, b] = net.copy(sending.at[spot], local.at[me.spot], device)
-
-    dispatch(table, rows, sending, me.core)
-    greeted()
-    set_out(0, 2)
-    local[me.spot] = sending[me.spot]
-    dispatch(table, rows, sending, 1 - me.core)
+    own_rows = everyone.at[me.spot]
+    here_rows = spread(net, me, everyone, own_rows, came)
+    next(here_rows)
+    from_across = net.copy(own_rows, own_rows, me.at(z=me.z_by(2)))
 
     act, gate_back, up_back, back, home = r.act, r.gate_back, r.up_back, r.back, r.home
-    w_gate, w_up, grads, w_down = fetch.w_gate, fetch.w_up, r.grads_held, fetch.w_down
-    fetch.raw
-    spot = lax.broadcasted_iota(jnp.int32, (48, 128), 0).astype(full)
+    grads = r.grads_held
+    iota = lax.broadcasted_iota(jnp.int32, (48, 128), 0).astype(full)
+
+    def slots_of(offset):
+        core, z_hi, y = peer(me, *offset)[0]
+        mask = r.info_in[core, z_hi, y, 0:1, :] == iota
+        share = jnp.where(mask, r.info_in[core, z_hi, y, 1:2, :], 0.0)
+        return mask, jnp.sum(share, axis=1, keepdims=True)
+
+    def select(source, offset):
+        mask, share = slots_of(offset)
+        named = jnp.where(mask, 1.0, 0.0).astype(low)[:, :96]
+        rows = source[peer(me, *offset)[0]].reshape(96, 2048)
+        return jnp.dot(named, rows, preferred_element_type=full), share
+
+    cots = fetch.cots
+    for offset, slot in SLOTS.items():
+        picked, share = select(cots, offset)
+        r.raw_held[slot] = picked.astype(low)
+        grads[slot] = (picked * share).astype(low)
+
+    w_gate, w_up, w_down = fetch.w_gate, fetch.w_up, fetch.w_down
     back_came, dots_came, round_x, written = {}, {}, [], []
     right, left = me.at(x=me.x_by(1)), me.at(x=me.x_by(3))
 
-    def weigh(first, group, entered, given, target):
+    def weigh(entered, given, target):
         def body(step, carry):
             columns = pl.ds(pl.multiple_of(step * 256, 256), 256)
-            made = contract_first(
-                entered[group, :, :, :, columns].reshape(384, 256), given[group]
-            )
-            if first == 1:
-                made = made + target[columns, :].astype(full)
-            target[columns, :] = made.astype(low)
+            left = entered[:, :, :, columns].reshape(768, 256)
+            target[columns, :] = contract_first(left, given[...].reshape(768, 768)).astype(low)
             return carry
 
         lax.fori_loop(0, 8, body, 0)
@@ -867,20 +905,20 @@
         return target.at[pl.ds(pl.multiple_of(start, 256), 256)]
 
     for first in (0, 1):
-        group = me.core if first == 0 else 1 - me.core
-        for a in (first, first + 2):
-            for b in (1, 3, 2, 0):
-                if a or b:
-                    came[a, b].wait_recv()
-            if a == 0:
-                set_out(1, 3)
+        group = first
+        if first == 0:
+            next(here_rows)
+            from_across.wait_recv()
+            other_rows = spread(net, me, everyone, None, came)
+            next(other_rows)
         masks, shares = [], []
-        for z_hi in range(2):
-            for y in range(4):
-                mask = r.info_in[group, z_hi, y, 0:1, :] == spot
-                share = jnp.where(mask, r.info_in[group, z_hi, y, 1:2, :], 0.0)
-                masks.append(mask)
-                shares.append(jnp.sum(share, axis=1, keepdims=True))
+        for offset in PHASES[first]:
+            if offset in came:
+                came[offset].wait_recv()
+            picked, share = select(everyone, offset)
+            local[SLOTS[offset]] = picked.astype(low)
+            masks.append(slots_of(offset)[0])
+            shares.append(share)
         shared = jnp.concatenate(shares, axis=0)
 
         def inner(step, carry, group=group, shared=shared):
@@ -905,36 +943,28 @@
             row_back = contract_last(gate_back[group], w_gate[columns, :]) + contract_last(
                 up_back[group], w_up[columns, :]
             )
-            back[group, :, :, :, columns] = row_back.astype(low).reshape(2, 4, 48, 256)
+            back[group, :, :, columns] = row_back.astype(low).reshape(8, 48, 256)
             return dot
 
         def finals(step, dot, group=group, shared=shared):
             columns = pl.ds(pl.multiple_of(step * 256, 256), 256)
             made = contract_last(act[group], w_down[columns, :]).astype(low).astype(full)
-            r.produced_held[group, :, :, :, columns] = (
-                (made * shared).astype(low).reshape(2, 4, 48, 256)
-            )
-            incoming = r.raw_held[group, :, :, :, columns].reshape(384, 256).astype(full)
+            r.produced_held[group, :, :, columns] = (made * shared).astype(low).reshape(8, 48, 256)
+            incoming = r.raw_held[group, :, :, columns].reshape(384, 256).astype(full)
             return dot + jnp.sum(made * incoming, axis=1, keepdims=True)
 
-        def scale(step, carry, group=group, shared=shared):
-            columns = pl.ds(pl.multiple_of(step * 256, 256), 256)
-            incoming = r.raw_held[group, :, :, :, columns].reshape(384, 256).astype(full)
-            grads[group, :, :, :, columns] = (
-                (incoming * shared).astype(low).reshape(2, 4, 48, 256)
-            )
-            return carry
-
-        lax.fori_loop(0, 8, scale, 0)
         lax.fori_loop(0, 3, inner, 0)
+        if first == 0:
+            next(here_rows)
         lax.fori_loop(0, 8, outer, 0)
-        for a in (first + 2, first):
-            for b in (0, 1, 3, 2):
-                if a or b:
-                    place, device = peer(me, a, b)
-                    back_came[a, b] = net.copy(back.at[place], home.at[me.spot], device)
+        if first == 0:
+            next(other_rows)
+        sources = [offset for offset in OFFSETS if offset in PHASES[first]]
+        for offset in sources:
+            device = peer(me, *offset)[1]
+            back_came[offset] = net.copy(back.at[SLOTS[offset]], home.at[me.spot], device)
         if first == 1:
-            weigh(first, group, local, gate_back, r.gate_held)
+            weigh(local, gate_back, r.gate_held)
             round_x += [
                 net.copy(chunk(r.gate_held, 2, 0), r.gate_slots.at[0], right),
                 net.copy(chunk(r.gate_held, 2, 1), r.gate_slots.at[2], left),
@@ -942,7 +972,7 @@
                 net.copy(chunk(r.gate_held, 3, 0), r.gate_slots.at[3], left),
             ]
             written.append(net.load(r.gate_held, r.full_gate))
-            weigh(first, group, local, up_back, r.up_held)
+            weigh(local, up_back, r.up_held)
             round_x += [
                 net.copy(chunk(r.up_held, 2, 0), r.up_slots.at[0], right),
                 net.copy(chunk(r.up_held, 2, 1), r.up_slots.at[1], left),
@@ -952,20 +982,17 @@
         for place in range(8):
             line = jnp.where(masks[place], dot[place * 48 : place * 48 + 48], 0.0)
             line = jnp.sum(line, axis=0, keepdims=True)
-            r.dots[group, place // 4, place % 4] = jnp.broadcast_to(line, (8, 128))
-        for a in (first + 2, first):
-            for b in (0, 1, 3, 2):
-                if a or b:
-                    place, device = peer(me, a, b)
-                    dots_came[a, b] = net.copy(r.dots.at[place], r.dots_in.at[me.spot], device)
+            r.dots[group, place] = jnp.broadcast_to(line, (8, 128))
+        for offset in sources:
+            device = peer(me, *offset)[1]
+            dots_came[offset] = net.copy(r.dots.at[SLOTS[offset]], r.dots_in.at[me.spot], device)
         if first == 0:
-            weigh(first, group, local, gate_back, r.gate_held)
-            weigh(first, group, local, up_back, r.up_held)
-        weigh(first, group, grads, act, r.down_held)
+            next(other_rows)
+    weigh(grads, act, r.down_held)
     written.append(net.load(r.produced_held, r.produced))
     written.append(net.load(r.down_held, r.full_down))
-    home[me.spot] = back[me.spot]
-    r.dots_in[me.spot] = r.dots[me.spot]
+    home[me.spot] = back[0, 0]
+    r.dots_in[me.spot] = r.dots[0, 0]
 
     for offset in OFFSETS:
         dots_came[offset].wait_recv()
@@ -1003,7 +1030,7 @@
 
 def moe(far, near):
     low, full = jnp.bfloat16, jnp.float32
-    rows = (2, 2, 4, 48, 2048)
+    rows, home = (2, 8, 48, 2048), (2, 2, 4, 48, 2048)
     outs = dict(
         after_grad=jax.ShapeDtypeStruct((96, 2048), full),
         branch=jax.ShapeDtypeStruct((3, 32, 2048), low),
@@ -1019,14 +1046,14 @@
         up_slots=jax.ShapeDtypeStruct((2, 256, 768), low),
     )
     scratch = dict(
-        rows=pltpu.VMEM((128, 2048), low),
-        sending=pltpu.VMEM(rows, low),
+        everyone=pltpu.VMEM((2, 2, 4, 3, 32, 2048), low),
         local=pltpu.VMEM(rows, low),
+        cots_held=pltpu.VMEM((2, 2, 4, 3, 32, 2048), low),
         raw_held=pltpu.VMEM(rows, low),
         grads_held=pltpu.VMEM(rows, low),
         produced_held=pltpu.VMEM(rows, low),
         back=pltpu.VMEM(rows, low),
-        home=pltpu.VMEM(rows, low),
+        home=pltpu.VMEM(home, low),
         gate_weight=pltpu.VMEM((2048, 768), low),
         up_weight=pltpu.VMEM((2048, 768), low),
         down_weight=pltpu.VMEM((2048, 768), low),
@@ -1036,10 +1063,10 @@
         act=pltpu.VMEM((2, 384, 768), low),
         gate_back=pltpu.VMEM((2, 384, 768), low),
         up_back=pltpu.VMEM((2, 384, 768), low),
-        dots=pltpu.VMEM((2, 2, 4, 8, 128), full),
+        dots=pltpu.VMEM((2, 8, 8, 128), full),
         dots_in=pltpu.VMEM((2, 2, 4, 8, 128), full),
-        send=pltpu.SemaphoreType.DMA((51,)),
-        recv=pltpu.SemaphoreType.DMA((51,)),
+        send=pltpu.SemaphoreType.DMA((54,)),
+        recv=pltpu.SemaphoreType.DMA((54,)),
         here=pltpu.SemaphoreType.DMA((8,)),
     )
     return call(moe_kernel, 1, far, near, outs, far_outs, scratch)
@@ -1076,7 +1103,6 @@
     fetch.start("cosine", r.cosine.at[me.context], r.cosine_held)
     fetch.start("sine", r.sine.at[me.context], r.sine_held)
     fetch.start("w_query", r.w_query, r.query_weight)
-    fetch.start("cotangent", r.cotangent, r.cotangent_held)
     fetch.start("w_out", r.w_out, r.out_weight)
     beside = me.at(z=me.z + 1 - 2 * me.z_lo)
     right, left = me.at(x=me.x_by(1)), me.at(x=me.x_by(3))
@@ -1084,25 +1110,13 @@
     gains = r.gain_rows
     gains[...] = wide(r.attn_gain)
 
-    token_table(r.ids, r.gates, r.capacity, r.table, r.info)
-    rows = r.rows
-    rows[96:, :] = jnp.zeros((32, 2048), low)
-    rows[:96, :] = fetch.cotangent[...].reshape(96, 2048)
-    for core in range(2):
-        dispatch(r.table, rows, r.sending, core)
+    above, below = me.at(y=me.y_by(1)), me.at(y=me.y_by(3))
+    across, came, told = me.at(z=me.z_by(2)), {}, []
     greeted()
-    arrivals = []
-
-    def set_out(first, second):
-        for a, b in OFFSETS:
-            if a in (first, second):
-                spot, device = peer(me, a, b)
-                arrivals.append(net.copy(r.info.at[spot], r.info_in.at[me.spot], device))
-                arrivals.append(net.copy(r.sending.at[spot], r.grads.at[me.spot], device))
-
-    set_out(0, 1)
-    r.info_in[me.spot] = r.info[me.spot]
-    own_grads = net.load(r.sending.at[me.spot], r.grads.at[me.spot])
+    own_cot = net.load(r.cotangent, r.cots.at[me.spot])
+    here_cot = spread(net, me, r.cots, r.cotangent, came)
+    next(here_cot)
+    from_across = net.copy(r.cotangent, r.cots.at[me.spot], across)
 
     hidden, normed = fetch.hidden, r.normed
     for s in range(3):
@@ -1130,19 +1144,42 @@
     def block(x, z_lo):
         return pl.ds(pl.multiple_of((x * 2 + z_lo) * 128, 128), 128)
 
-    def piece(x, z_lo, half=None):
+    def piece(s, x, z_lo, half=None):
         rows = block(x, z_lo)
-        return pair.at[:, :, rows, :] if half is None else pair.at[half, :, rows, :]
+        return pair.at[:, s, rows, :] if half is None else pair.at[half, s, rows, :]
 
     def pass_on(view, device):
         return net.copy(view, view, device)
 
     own_z, other_z = me.z_lo, 1 - me.z_lo
-    from_z = pass_on(piece(me.x, own_z), beside)
-    from_left = [pass_on(piece(me.x, own_z), right)]
-    from_right = [pass_on(piece(me.x, own_z), left)]
-
-    set_out(2, 3)
+
+    def bring_pair(s):
+        from_z = pass_on(piece(s, me.x, own_z), beside)
+        came = [(pass_on(piece(s, me.x, own_z), right), pass_on(piece(s, me.x, own_z), left))]
+        yield
+        from_z.wait_recv()
+        came.append((pass_on(piece(s, me.x, other_z), right), pass_on(piece(s, me.x, other_z), left)))
+        yield
+        far = []
+        for zs, (from_left, from_right) in zip((own_z, other_z), came, strict=True):
+            from_left.wait_recv()
+            far.append(pass_on(piece(s, me.x_by(3), zs, 0), right))
+            from_right.wait_recv()
+            far.append(pass_on(piece(s, me.x_by(1), zs, 1), left))
+            yield
+        for one in far:
+            one.wait_recv()
+        yield
+
+    brought = [bring_pair(s) for s in range(3)]
+    for s in range(3):
+        next(brought[s])
+
+    token_table(r.ids, r.gates, r.capacity, r.table, r.info)
+    r.info_in[me.spot] = r.info[me.spot]
+    for a, b in OFFSETS:
+        spot, device = peer(me, a, b)
+        told.append(net.copy(r.info.at[spot], r.info_in.at[me.spot], device))
 
     w_query, query, query_raw = fetch.w_query, r.query_held, r.query_raw_held
 
@@ -1158,26 +1195,26 @@
 
     lax.fori_loop(0, 4, project, 0)
     written = [net.load(query, r.query), net.load(query_raw, r.query_raw)]
-    from_z.wait_recv()
-    from_left.append(pass_on(piece(me.x, other_z), right))
-    from_right.append(pass_on(piece(me.x, other_z), left))
-    far = [[], []]
-    for spot, zs in enumerate((own_z, other_z)):
-        from_left[spot].wait_recv()
-        far[0].append(pass_on(piece(me.x_by(3), zs, 0), right))
-        from_right[spot].wait_recv()
-        far[1].append(pass_on(piece(me.x_by(1), zs, 1), left))
-    for one in far[0] + far[1]:
-        one.wait_recv()
-    written.append(net.load(pair, r.pair))
+    for s in range(3):
+        next(brought[s])
+    next(here_cot)
+    from_across.wait_recv()
+    other_cot = spread(net, me, r.cots, None, came)
+    next(other_cot)
+    next(brought[0])
+    next(brought[1])
+    next(brought[0])
+    next(brought[2])
+    next(brought[1])
 
     bias, peaks, mixed = r.bias, r.peak_rows, r.mixed_held
     peaks[...] = jnp.full((8, 1, 128), -jnp.inf, full)
-    for s in range(3):
+
+    def attend(s):
         here = pl.ds(s * 128, 128)
         bias[...] = mask_bias(me, r.segments, s)
 
-        def two_heads(step, carry, s=s, here=here):
+        def two_heads(step, carry):
             columns = pl.ds(pl.multiple_of(step * 256, 256), 256)
             both = query[here, columns]
             q = jnp.concatenate([both[:, :128], both[:, 128:]], axis=0)
@@ -1200,36 +1237,59 @@
             return carry
 
         lax.fori_loop(0, 4, two_heads, 0)
+    shares, after = r.shares, r.after_sum
+
+    def branch(s):
+        w_out = fetch.w_out
+
+        def body(step, carry):
+            columns = pl.ds(pl.multiple_of(step * 256, 256), 256)
+            made = contract_last(mixed[pl.ds(s * 128, 128), :], w_out[columns, :])
+            shares[s, :, :, columns] = made.astype(low).reshape(4, 32, 256)
+            return carry
+
+        lax.fori_loop(0, 8, body, 0)
+        return ring_reduce(
+            net,
+            above,
+            below,
+            lambda step, half: shares.at[s, me.y_by(step), :, pl.ds(half * 1024, 1024)],
+            r.branch_slots.at[s],
+            lambda half: after.at[s, :, pl.ds(half * 1024, 1024)],
+        )
+
+    next(brought[0])
+    attend(0)
+    next(brought[2])
+    first = branch(0)
+    next(first)
+    next(brought[1])
+    attend(1)
+    next(other_cot)
+    second = branch(1)
+    next(second)
+    next(first)
+    next(brought[2])
+    attend(2)
+    third = branch(2)
+    next(third)
+    next(second)
+    next(here_cot)
+    written.append(net.load(pair, r.pair))
+    written.append(net.load(mixed, r.mixed))
     for head in range(8):
         r.peaks[head : head + 1, :] = peaks[head]
-    written.append(net.load(mixed, r.mixed))
-
-    w_out, shares = fetch.w_out, r.shares
-
-    def branch_step(step, carry):
-        columns = pl.ds(pl.multiple_of(step * 256, 256), 256)
-        made = contract_last(mixed[...], w_out[columns, :])
-        shares[:, :, :, columns] = made.astype(low).reshape(3, 4, 32, 256)
-        return carry
-
-    lax.fori_loop(0, 8, branch_step, 0)
-    after = r.after_sum
-    ring = ring_reduce(
-        net,
-        me.at(y=me.y_by(1)),
-        me.at(y=me.y_by(3)),
-        lambda step, half: shares.at[:, me.y_by(step), :, pl.ds(half * 1024, 1024)],
-        r.branch_slots,
-        lambda half: after.at[:, :, pl.ds(half * 1024, 1024)],
-    )
-    for _ in ring:
-        pass
+    next(first, None)
+    next(third)
+    next(other_cot)
+    next(second, None)
+    next(third, None)
     own_rows = pl.ds(pl.multiple_of(me.y * 32, 32), 32)
     for s in range(3):
         r.after[s * 32 : s * 32 + 32, :] = after[s] + hidden[s, own_rows, :].astype(full)
-    for one in arrivals:
+    for one in list(came.values()) + told:
         one.wait_recv()
-    own_grads.wait()
+    own_cot.wait()
     for one in written:
         one.wait()
     net.finish()
@@ -1254,7 +1314,6 @@
 
 def front(far, near):
     low, full = jnp.bfloat16, jnp.float32
-    rows = (2, 2, 4, 48, 2048)
     outs = dict(
         key_raw=jax.ShapeDtypeStruct((384, 128), full),
         log_sum=jax.ShapeDtypeStruct((24, 1, 128), full),
@@ -1268,7 +1327,7 @@
         query_raw=jax.ShapeDtypeStruct((384, 1024), full),
         pair=jax.ShapeDtypeStruct((2, 3, 1024, 128), low),
         mixed=jax.ShapeDtypeStruct((384, 1024), low),
-        grads=jax.ShapeDtypeStruct(rows, low),
+        cots=jax.ShapeDtypeStruct((2, 2, 4, 3, 32, 2048), low),
     )
     scratch = dict(
         gain_rows=pltpu.VMEM((1, 2048), full),
@@ -1278,23 +1337,20 @@
         cosine_held=pltpu.VMEM((128, 128), full),
         sine_held=pltpu.VMEM((128, 128), full),
         query_weight=pltpu.VMEM((2048, 1024), low),
-        cotangent_held=pltpu.VMEM((3, 32, 2048), low),
         out_weight=pltpu.VMEM((2048, 1024), low),
         normed=pltpu.VMEM((384, 2048), low),
         pair_held=pltpu.VMEM((2, 3, 1024, 128), low),
         info=pltpu.VMEM((2, 2, 4, 8, 128), full),
-        rows=pltpu.VMEM((128, 2048), low),
-        sending=pltpu.VMEM(rows, low),
         query_held=pltpu.VMEM((384, 1024), low),
         query_raw_held=pltpu.VMEM((384, 1024), full),
         bias=pltpu.VMEM((128, 1024), full),
         peak_rows=pltpu.VMEM((8, 1, 128), full),
         mixed_held=pltpu.VMEM((384, 1024), low),
         shares=pltpu.VMEM((3, 4, 32, 2048), low),
-        branch_slots=pltpu.VMEM((6, 3, 32, 1024), low),
+        branch_slots=pltpu.VMEM((3, 6, 32, 1024), low),
         after_sum=pltpu.VMEM((3, 32, 2048), full),
-        send=pltpu.SemaphoreType.DMA((46,)),
-        recv=pltpu.SemaphoreType.DMA((46,)),
+        send=pltpu.SemaphoreType.DMA((84,)),
+        recv=pltpu.SemaphoreType.DMA((84,)),
         here=pltpu.SemaphoreType.DMA((16,)),
     )
     return call(front_kernel, 2, far, near, outs, far_outs, scratch)
@@ -1397,7 +1453,7 @@
         ),
     )
     second = moe(
-        dict(w_gate=w_gate[0], w_up=w_up[0], w_down=w_down[0], grads=first.grads),
+        dict(w_gate=w_gate[0], w_up=w_up[0], w_down=w_down[0], cots=first.cots),
         dict(
             after=first.after,
             cotangent=cotangent,

time: 284 us -> 271 us (0.954)
  Pallas kernels: 283 us -> 270 us
    pallas_call x3, Pallas kernels: 278 us -> 265 us  [call(): pl.pallas_call(functools.partial(kernel, names), out_shape=list(shapes.va...]
where the time goes in v7:
time: 271 us
  Pallas kernels  270 us (100%)
    pallas_call x3, Pallas kernels, call(): pl.pallas_call(functools.partial(kernel, names), out_shape=list(shapes.va...  265 us

profile of v7, /device:TPU:0, one launch (start us, length us, event | category | flops | bytes accessed | tf_op | source)
XLA Modules:
  0.0 271.0 jit_solution(6536187373142500977)
XLA Ops:
  0.6 60.3 %front_kernel.1 = (f32[384,128]{1,0:T(8,128)}, f32[24,1,128]{2,1,0:T(1,128)}, f32[8,128]{1,0:T(8,128)}, f32[96,2048]{1,0:T(8,128)}, bf16[768,128]{1,0:T(8,128)(2...) custom-call(bf16[3,128,2048]{2,1,0:T(8,128)(2,1)} %refs_9_.1, ...), custom_call_target="tpu_custom_call" | custom-call | tf_op jit(solution)/shard_map/front_kernel/pallas_call | solution.py:1078
  61.0 89.8 %moe_kernel.1 = (f32[96,2048]{1,0:T(8,128)}, bf16[3,32,2048]{2,1,0:T(8,128)(2,1)}, f32[1,2048]{1,0:T(1,128)}, f32[3,8,32]{2,1,0:T(8,128)}, bf16[2,8,48,2048]{3,2...) custom-call(bf16[2048,768]{1,0:T(8,128)(2,1)} %bitcast.23, ...), custom_call_target="tpu_custom_call" | custom-call | tf_op jit(solution)/shard_map/moe_kernel/pallas_call | solution.py:1078
  150.7 115.1 %back_kernel.1 = (f32[256,768]{1,0:T(8,128)}, f32[256,768]{1,0:T(8,128)}, f32[256,768]{1,0:T(8,128)}, f32[64,1024]{1,0:T(8,128)}, f32[64,256]{1,0:T(8,128)}, /*i...) custom-call(bf16[3,32,2048]{2,1,0:T(8,128)(2,1)} %get-tuple-element., ...), custom_call_target="tpu_custom_call" | custom-call | tf_op jit(solution)/shard_map/back_kernel/pallas_call | solution.py:1078
  265.8 4.9 %finish.1 = (f32[96,2048]{1,0:T(8,128)}, f32[96,2048]{1,0:T(8,128)}, f32[256,768]{1,0:T(8,128)}, f32[256,768]{1,0:T(8,128)}, f32[256,768]{1,0:T(8,128)}, /*index...) custom-call(f32[96,2048]{1,0:T(8,128)} %get-tuple-element.60.refs_4_, ...), custom_call_target="tpu_custom_call" | custom-call | tf_op jit(solution)/shard_map/finish/pallas_call | solution.py:1400

commit v8 on v7

--- a/solution.py
+++ b/solution.py
@@ -804,7 +804,7 @@
 
 PHASES = (
     [(0, 0), (0, 1), (0, 3), (2, 0), (1, 0), (1, 1), (1, 3), (3, 0)],
-    [(0, 2), (2, 1), (2, 3), (2, 2), (1, 2), (3, 1), (3, 3), (3, 2)],
+    [(0, 2), (1, 2), (2, 1), (2, 3), (3, 1), (3, 3), (2, 2), (3, 2)],
 )
 SLOTS = {offset: (phase, spot) for phase in (0, 1) for spot, offset in enumerate(PHASES[phase])}
 
@@ -904,90 +904,99 @@
         start = (me.x_by(step) * 2 + half) * 256
         return target.at[pl.ds(pl.multiple_of(start, 256), 256)]
 
-    for first in (0, 1):
-        group = first
-        if first == 0:
-            next(here_rows)
-            from_across.wait_recv()
-            other_rows = spread(net, me, everyone, None, came)
-            next(other_rows)
-        masks, shares = [], []
-        for offset in PHASES[first]:
+    def send_back(offsets):
+        for offset in offsets:
+            device = peer(me, *offset)[1]
+            back_came[offset] = net.copy(back.at[SLOTS[offset]], home.at[me.spot], device)
+
+    def through(group, low_slot, high_slot, between):
+        run = slice(low_slot * 48, high_slot * 48)
+        slots, rows = slice(low_slot, high_slot), (high_slot - low_slot) * 48
+        for offset in PHASES[group][slots]:
             if offset in came:
                 came[offset].wait_recv()
-            picked, share = select(everyone, offset)
-            local[SLOTS[offset]] = picked.astype(low)
-            masks.append(slots_of(offset)[0])
-            shares.append(share)
-        shared = jnp.concatenate(shares, axis=0)
-
-        def inner(step, carry, group=group, shared=shared):
+            local[SLOTS[offset]] = select(everyone, offset)[0].astype(low)
+
+        def inner(step, carry):
             columns = pl.ds(pl.multiple_of(step * 256, 256), 256)
-            entered = local[group].reshape(384, 2048)
+            entered = local[group, slots].reshape(rows, 2048)
             gate_pre = jnp.dot(entered, w_gate[:, columns], preferred_element_type=full)
             up_pre = jnp.dot(entered, w_up[:, columns], preferred_element_type=full)
             act_back = jnp.dot(
-                grads[group].reshape(384, 2048), w_down[:, columns], preferred_element_type=full
+                grads[group, slots].reshape(rows, 2048),
+                w_down[:, columns],
+                preferred_element_type=full,
             )
             sigmoid = 1.0 / (1.0 + jnp.exp(-gate_pre))
             silu = gate_pre * sigmoid
-            act[group, :, columns] = (silu * up_pre).astype(low)
-            gate_back[group, :, columns] = (
+            act[group, run, columns] = (silu * up_pre).astype(low)
+            gate_back[group, run, columns] = (
                 act_back * up_pre * sigmoid * (1.0 + gate_pre * (1.0 - sigmoid))
             ).astype(low)
-            up_back[group, :, columns] = (act_back * silu).astype(low)
+            up_back[group, run, columns] = (act_back * silu).astype(low)
             return carry
 
-        def outer(step, dot, group=group, shared=shared):
+        def outer(step, carry):
             columns = pl.ds(pl.multiple_of(step * 256, 256), 256)
-            row_back = contract_last(gate_back[group], w_gate[columns, :]) + contract_last(
-                up_back[group], w_up[columns, :]
+            row_back = contract_last(gate_back[group, run, :], w_gate[columns, :]) + contract_last(
+                up_back[group, run, :], w_up[columns, :]
             )
-            back[group, :, :, columns] = row_back.astype(low).reshape(8, 48, 256)
-            return dot
-
-        def finals(step, dot, group=group, shared=shared):
+            back[group, slots, :, columns] = row_back.astype(low).reshape(rows // 48, 48, 256)
+            return carry
+
+        lax.fori_loop(0, 3, inner, 0)
+        between()
+        lax.fori_loop(0, 8, outer, 0)
+
+    def results(group):
+        given = [slots_of(offset) for offset in PHASES[group]]
+        shared = jnp.concatenate([share for _, share in given], axis=0)
+
+        def finals(step, dot):
             columns = pl.ds(pl.multiple_of(step * 256, 256), 256)
             made = contract_last(act[group], w_down[columns, :]).astype(low).astype(full)
             r.produced_held[group, :, :, columns] = (made * shared).astype(low).reshape(8, 48, 256)
             incoming = r.raw_held[group, :, :, columns].reshape(384, 256).astype(full)
             return dot + jnp.sum(made * incoming, axis=1, keepdims=True)
 
-        lax.fori_loop(0, 3, inner, 0)
-        if first == 0:
-            next(here_rows)
-        lax.fori_loop(0, 8, outer, 0)
-        if first == 0:
-            next(other_rows)
-        sources = [offset for offset in OFFSETS if offset in PHASES[first]]
-        for offset in sources:
-            device = peer(me, *offset)[1]
-            back_came[offset] = net.copy(back.at[SLOTS[offset]], home.at[me.spot], device)
-        if first == 1:
-            weigh(local, gate_back, r.gate_held)
-            round_x += [
-                net.copy(chunk(r.gate_held, 2, 0), r.gate_slots.at[0], right),
-                net.copy(chunk(r.gate_held, 2, 1), r.gate_slots.at[2], left),
-                net.copy(chunk(r.gate_held, 1, 1), r.gate_slots.at[1], right),
-                net.copy(chunk(r.gate_held, 3, 0), r.gate_slots.at[3], left),
-            ]
-            written.append(net.load(r.gate_held, r.full_gate))
-            weigh(local, up_back, r.up_held)
-            round_x += [
-                net.copy(chunk(r.up_held, 2, 0), r.up_slots.at[0], right),
-                net.copy(chunk(r.up_held, 2, 1), r.up_slots.at[1], left),
-            ]
-            written.append(net.load(r.up_held, r.full_up))
         dot = lax.fori_loop(0, 8, finals, jnp.zeros((384, 1), full))
-        for place in range(8):
-            line = jnp.where(masks[place], dot[place * 48 : place * 48 + 48], 0.0)
+        for spot, offset in enumerate(PHASES[group]):
+            line = jnp.where(given[spot][0], dot[spot * 48 : spot * 48 + 48], 0.0)
             line = jnp.sum(line, axis=0, keepdims=True)
-            r.dots[group, place] = jnp.broadcast_to(line, (8, 128))
-        for offset in sources:
-            device = peer(me, *offset)[1]
-            dots_came[offset] = net.copy(r.dots.at[SLOTS[offset]], r.dots_in.at[me.spot], device)
-        if first == 0:
-            next(other_rows)
+            r.dots[group, spot] = jnp.broadcast_to(line, (8, 128))
+            if offset != (0, 0):
+                device = peer(me, *offset)[1]
+                dots_came[offset] = net.copy(
+                    r.dots.at[group, spot], r.dots_in.at[me.spot], device
+                )
+
+    next(here_rows)
+    from_across.wait_recv()
+    other_rows = spread(net, me, everyone, None, came)
+    next(other_rows)
+    through(0, 0, 8, lambda: next(here_rows))
+    next(other_rows)
+    send_back([offset for offset in PHASES[0] if offset != (0, 0)])
+    through(1, 0, 6, lambda: next(other_rows))
+    send_back(PHASES[1][:6])
+    through(1, 6, 8, lambda: None)
+    send_back(PHASES[1][6:])
+    weigh(local, gate_back, r.gate_held)
+    round_x += [
+        net.copy(chunk(r.gate_held, 2, 0), r.gate_slots.at[0], right),
+        net.copy(chunk(r.gate_held, 2, 1), r.gate_slots.at[2], left),
+        net.copy(chunk(r.gate_held, 1, 1), r.gate_slots.at[1], right),
+        net.copy(chunk(r.gate_held, 3, 0), r.gate_slots.at[3], left),
+    ]
+    written.append(net.load(r.gate_held, r.full_gate))
+    weigh(local, up_back, r.up_held)
+    round_x += [
+        net.copy(chunk(r.up_held, 2, 0), r.up_slots.at[0], right),
+        net.copy(chunk(r.up_held, 2, 1), r.up_slots.at[1], left),
+    ]
+    written.append(net.load(r.up_held, r.full_up))
+    results(0)
+    results(1)
     weigh(grads, act, r.down_held)
     written.append(net.load(r.produced_held, r.produced))
     written.append(net.load(r.down_held, r.full_down))

time: 271 us -> 263 us (0.970)
  Pallas kernels: 270 us -> 262 us
    pallas_call x3, Pallas kernels: 265 us -> 257 us  [call(): pl.pallas_call(functools.partial(kernel, names), out_shape=list(shapes.va...]
where the time goes in v8:
time: 263 us
  Pallas kernels  262 us (100%)
    pallas_call x3, Pallas kernels, call(): pl.pallas_call(functools.partial(kernel, names), out_shape=list(shapes.va...  257 us

profile of v8, /device:TPU:0, one launch (start us, length us, event | category | flops | bytes accessed | tf_op | source)
XLA Modules:
  0.0 262.8 jit_solution(17627309600147914067)
XLA Ops:
  0.6 60.3 %front_kernel.1 = (f32[384,128]{1,0:T(8,128)}, f32[24,1,128]{2,1,0:T(1,128)}, f32[8,128]{1,0:T(8,128)}, f32[96,2048]{1,0:T(8,128)}, bf16[768,128]{1,0:T(8,128)(2...) custom-call(bf16[3,128,2048]{2,1,0:T(8,128)(2,1)} %refs_9_.1, ...), custom_call_target="tpu_custom_call" | custom-call | tf_op jit(solution)/shard_map/front_kernel/pallas_call | solution.py:1087
  61.0 81.1 %moe_kernel.1 = (f32[96,2048]{1,0:T(8,128)}, bf16[3,32,2048]{2,1,0:T(8,128)(2,1)}, f32[1,2048]{1,0:T(1,128)}, f32[3,8,32]{2,1,0:T(8,128)}, bf16[2,8,48,2048]{3,2...) custom-call(bf16[2048,768]{1,0:T(8,128)(2,1)} %bitcast.23, ...), custom_call_target="tpu_custom_call" | custom-call | tf_op jit(solution)/shard_map/moe_kernel/pallas_call | solution.py:1087
  142.1 115.6 %back_kernel.1 = (f32[256,768]{1,0:T(8,128)}, f32[256,768]{1,0:T(8,128)}, f32[256,768]{1,0:T(8,128)}, f32[64,1024]{1,0:T(8,128)}, f32[64,256]{1,0:T(8,128)}, /*i...) custom-call(bf16[3,32,2048]{2,1,0:T(8,128)(2,1)} %get-tuple-element., ...), custom_call_target="tpu_custom_call" | custom-call | tf_op jit(solution)/shard_map/back_kernel/pallas_call | solution.py:1087
  257.7 4.9 %finish.1 = (f32[96,2048]{1,0:T(8,128)}, f32[96,2048]{1,0:T(8,128)}, f32[256,768]{1,0:T(8,128)}, f32[256,768]{1,0:T(8,128)}, f32[256,768]{1,0:T(8,128)}, /*index...) custom-call(f32[96,2048]{1,0:T(8,128)} %get-tuple-element.60.refs_4_, ...), custom_call_target="tpu_custom_call" | custom-call | tf_op jit(solution)/shard_map/finish/pallas_call | solution.py:1409

commit v9 on v8

--- a/solution.py
+++ b/solution.py
@@ -809,10 +809,11 @@
 SLOTS = {offset: (phase, spot) for phase in (0, 1) for spot, offset in enumerate(PHASES[phase])}
 
 
-def spread(net, me, everyone, source, came):
+def spread(net, me, everyone, source, came, crossed):
     above, below = me.at(y=me.y_by(1)), me.at(y=me.y_by(3))
-    sibling = me.at(core=1 - me.core)
-    a, z_hi = (2, 1 - me.z_hi) if source is None else (0, me.z_hi)
+    sibling, across = me.at(core=1 - me.core), me.at(z=me.z_by(2))
+    own = source is not None
+    a, z_hi = (0, me.z_hi) if own else (2, 1 - me.z_hi)
 
     def block(b):
         return everyone.at[me.core, z_hi, me.y_by(b)]
@@ -820,24 +821,39 @@
     def half(b, part):
         return block(b).at[:, pl.ds(part * 16, 16)]
 
+    def quarter(b, part):
+        return block(b).at[:, pl.ds(0, 16), pl.ds(part * 1024, 1024)]
+
     def forward(view, device):
         return net.copy(view, view, device)
 
-    source = block(0) if source is None else source
-    up = net.copy(source, block(0), above)
-    down = net.copy(source, block(0), below)
-    came[a + 1, 0] = net.copy(source, block(0), sibling)
+    def pass_on(b):
+        if own:
+            crossed[b] = forward(half(b, 1), across)
+        else:
+            crossed[b].wait_recv()
+        came[a + 1, b] = forward(block(b), sibling)
+
+    piece = half if own else quarter
+    if own:
+        up = net.copy(source, block(0), above)
+        down = net.copy(source, block(0), below)
+        came[a + 1, 0] = net.copy(source, block(0), sibling)
+    else:
+        up = forward(half(0, 0), above)
+        down = forward(half(0, 0), below)
+        came[a + 1, 0] = forward(block(0), sibling)
     yield
     up.wait_recv()
-    far_up = forward(half(3, 0), above)
-    came[a + 1, 3] = forward(block(3), sibling)
+    far_up = forward(piece(3, 0), above)
     down.wait_recv()
-    far_down = forward(half(1, 1), below)
-    came[a + 1, 1] = forward(block(1), sibling)
+    far_down = forward(piece(1, 1), below)
+    pass_on(3)
+    pass_on(1)
     yield
     far_up.wait_recv()
     far_down.wait_recv()
-    came[a + 1, 2] = forward(block(2), sibling)
+    pass_on(2)
     yield
 
 
@@ -859,9 +875,9 @@
     everyone[me.spot] = (values * inverse * gain).astype(low).reshape(3, 32, 2048)
 
     greeted()
-    came = {}
+    came, crossed = {}, {}
     own_rows = everyone.at[me.spot]
-    here_rows = spread(net, me, everyone, own_rows, came)
+    here_rows = spread(net, me, everyone, own_rows, came, crossed)
     next(here_rows)
     from_across = net.copy(own_rows, own_rows, me.at(z=me.z_by(2)))
 
@@ -972,7 +988,7 @@
 
     next(here_rows)
     from_across.wait_recv()
-    other_rows = spread(net, me, everyone, None, came)
+    other_rows = spread(net, me, everyone, None, came, crossed)
     next(other_rows)
     through(0, 0, 8, lambda: next(here_rows))
     next(other_rows)
@@ -1074,8 +1090,8 @@
         up_back=pltpu.VMEM((2, 384, 768), low),
         dots=pltpu.VMEM((2, 8, 8, 128), full),
         dots_in=pltpu.VMEM((2, 2, 4, 8, 128), full),
-        send=pltpu.SemaphoreType.DMA((54,)),
-        recv=pltpu.SemaphoreType.DMA((54,)),
+        send=pltpu.SemaphoreType.DMA((58,)),
+        recv=pltpu.SemaphoreType.DMA((58,)),
         here=pltpu.SemaphoreType.DMA((8,)),
     )
     return call(moe_kernel, 1, far, near, outs, far_outs, scratch)
@@ -1120,10 +1136,10 @@
     gains[...] = wide(r.attn_gain)
 
     above, below = me.at(y=me.y_by(1)), me.at(y=me.y_by(3))
-    across, came, told = me.at(z=me.z_by(2)), {}, []
+    across, came, crossed, told = me.at(z=me.z_by(2)), {}, {}, []
     greeted()
     own_cot = net.load(r.cotangent, r.cots.at[me.spot])
-    here_cot = spread(net, me, r.cots, r.cotangent, came)
+    here_cot = spread(net, me, r.cots, r.cotangent, came, crossed)
     next(here_cot)
     from_across = net.copy(r.cotangent, r.cots.at[me.spot], across)
 
@@ -1184,12 +1200,6 @@
     for s in range(3):
         next(brought[s])
 
-    token_table(r.ids, r.gates, r.capacity, r.table, r.info)
-    r.info_in[me.spot] = r.info[me.spot]
-    for a, b in OFFSETS:
-        spot, device = peer(me, a, b)
-        told.append(net.copy(r.info.at[spot], r.info_in.at[me.spot], device))
-
     w_query, query, query_raw = fetch.w_query, r.query_held, r.query_raw_held
 
     def project(step, carry):
@@ -1202,14 +1212,15 @@
             query[:, run] = rope(one).astype(low)
         return carry
 
-    lax.fori_loop(0, 4, project, 0)
-    written = [net.load(query, r.query), net.load(query_raw, r.query_raw)]
+    lax.fori_loop(0, 2, project, 0)
     for s in range(3):
         next(brought[s])
     next(here_cot)
     from_across.wait_recv()
-    other_cot = spread(net, me, r.cots, None, came)
+    other_cot = spread(net, me, r.cots, None, came, crossed)
     next(other_cot)
+    lax.fori_loop(2, 4, project, 0)
+    written = [net.load(query, r.query), net.load(query_raw, r.query_raw)]
     next(brought[0])
     next(brought[1])
     next(brought[0])
@@ -1274,6 +1285,7 @@
     next(first)
     next(brought[1])
     attend(1)
+    next(here_cot)
     next(other_cot)
     second = branch(1)
     next(second)
@@ -1282,8 +1294,14 @@
     attend(2)
     third = branch(2)
     next(third)
+
+    token_table(r.ids, r.gates, r.capacity, r.table, r.info)
+    r.info_in[me.spot] = r.info[me.spot]
+    for a, b in OFFSETS:
+        spot, device = peer(me, a, b)
+        told.append(net.copy(r.info.at[spot], r.info_in.at[me.spot], device))
+
     next(second)
-    next(here_cot)
     written.append(net.load(pair, r.pair))
     written.append(net.load(mixed, r.mixed))
     for head in range(8):

time: 263 us -> 261 us (level)
  no operation moved by 1% of the time
where the time goes in v9:
time: 261 us
  Pallas kernels  260 us (100%)
    pallas_call x3, Pallas kernels, call(): pl.pallas_call(functools.partial(kernel, names), out_shape=list(shapes.va...  255 us

profile of v9, /device:TPU:0, one launch (start us, length us, event | category | flops | bytes accessed | tf_op | source)
XLA Modules:
  0.0 260.8 jit_solution(5601505088442063296)
XLA Ops:
  0.6 59.8 %front_kernel.1 = (f32[384,128]{1,0:T(8,128)}, f32[24,1,128]{2,1,0:T(1,128)}, f32[8,128]{1,0:T(8,128)}, f32[96,2048]{1,0:T(8,128)}, bf16[768,128]{1,0:T(8,128)(2...) custom-call(bf16[3,128,2048]{2,1,0:T(8,128)(2,1)} %refs_9_.1, ...), custom_call_target="tpu_custom_call" | custom-call | tf_op jit(solution)/shard_map/front_kernel/pallas_call | solution.py:1103
  60.5 80.2 %moe_kernel.1 = (f32[96,2048]{1,0:T(8,128)}, bf16[3,32,2048]{2,1,0:T(8,128)(2,1)}, f32[1,2048]{1,0:T(1,128)}, f32[3,8,32]{2,1,0:T(8,128)}, bf16[2,8,48,2048]{3,2...) custom-call(bf16[2048,768]{1,0:T(8,128)(2,1)} %bitcast.23, ...), custom_call_target="tpu_custom_call" | custom-call | tf_op jit(solution)/shard_map/moe_kernel/pallas_call | solution.py:1103
  140.7 114.9 %back_kernel.1 = (f32[256,768]{1,0:T(8,128)}, f32[256,768]{1,0:T(8,128)}, f32[256,768]{1,0:T(8,128)}, f32[64,1024]{1,0:T(8,128)}, f32[64,256]{1,0:T(8,128)}, /*i...) custom-call(bf16[3,32,2048]{2,1,0:T(8,128)(2,1)} %get-tuple-element., ...), custom_call_target="tpu_custom_call" | custom-call | tf_op jit(solution)/shard_map/back_kernel/pallas_call | solution.py:1103
  255.7 4.9 %finish.1 = (f32[96,2048]{1,0:T(8,128)}, f32[96,2048]{1,0:T(8,128)}, f32[256,768]{1,0:T(8,128)}, f32[256,768]{1,0:T(8,128)}, f32[256,768]{1,0:T(8,128)}, /*index...) custom-call(f32[96,2048]{1,0:T(8,128)} %get-tuple-element.60.refs_4_, ...), custom_call_target="tpu_custom_call" | custom-call | tf_op jit(solution)/shard_map/finish/pallas_call | solution.py:1427

commit v10 on v9

--- a/solution.py
+++ b/solution.py
@@ -420,6 +420,7 @@
     far_below.wait_recv()
 
     bring_home([offset for offset in OFFSETS if offset not in straight])
+    next(down)
 
     heads_grad = r.heads_grad
 
@@ -468,7 +469,6 @@
         dense_z_first, branch_weight, fetch.mixed, r.sending, r.out_w_other, r.out_w_middle,
         r.out_w_slots, r.out_w_corner, r.out_w_last, r.out_w_out,
     )
-    next(down)
 
     query, query_raw, pair = fetch.query, fetch.query_raw, fetch.pair
     cosine, sine = fetch.cosine, fetch.sine
@@ -619,6 +619,11 @@
     ]
     next(pair_w)
     next(smalls)
+    def rest(*tasks):
+        for task in tasks:
+            next(task, None)
+
+    rest(query_w, normed_sum, pair_w, smalls, out_w, down, query_w, pair_w, smalls)
     moe_out = r.moe_out
     for half in range(2):
         home_loads[half].wait()
@@ -631,20 +636,13 @@
 
         lax.fori_loop(0, 4, gather, 0)
 
-    def rest(*tasks):
-        for task in tasks:
-            next(task, None)
-
-    rest(normed_sum, query_w, out_w, down, smalls)
-
     next(normed_sum, None)
     for s in range(3):
         rows = pl.ds(pl.multiple_of(me.y * 32, 32), 32)
         grad, _ = norm_back(normed_out[s], hidden[s, rows, :].astype(full), gains[...])
         normed_out[s] = grad
 
-    rest(pair_w, out_w, query_w, down, smalls, gate, up)
-    rest(pair_w, out_w, query_w, smalls)
+    rest(out_w, query_w, pair_w, smalls, gate, up, down, out_w, query_w, pair_w)
     tasks = [pair_w, out_w, smalls, query_w, gate, up, down]
     while tasks:
         for task in list(tasks):

time: 261 us -> 262 us (level)
  no operation moved by 1% of the time
where the time goes in v10:
time: 262 us
  Pallas kernels  261 us (100%)
    pallas_call x3, Pallas kernels, call(): pl.pallas_call(functools.partial(kernel, names), out_shape=list(shapes.va...  256 us

profile of v10, /device:TPU:0, one launch (start us, length us, event | category | flops | bytes accessed | tf_op | source)
XLA Modules:
  0.0 262.2 jit_solution(5713193898060657437)
XLA Ops:
  0.6 59.8 %front_kernel.1 = (f32[384,128]{1,0:T(8,128)}, f32[24,1,128]{2,1,0:T(1,128)}, f32[8,128]{1,0:T(8,128)}, f32[96,2048]{1,0:T(8,128)}, bf16[768,128]{1,0:T(8,128)(2...) custom-call(bf16[3,128,2048]{2,1,0:T(8,128)(2,1)} %refs_9_.1, ...), custom_call_target="tpu_custom_call" | custom-call | tf_op jit(solution)/shard_map/front_kernel/pallas_call | solution.py:1101
  60.5 80.2 %moe_kernel.1 = (f32[96,2048]{1,0:T(8,128)}, bf16[3,32,2048]{2,1,0:T(8,128)(2,1)}, f32[1,2048]{1,0:T(1,128)}, f32[3,8,32]{2,1,0:T(8,128)}, bf16[2,8,48,2048]{3,2...) custom-call(bf16[2048,768]{1,0:T(8,128)(2,1)} %bitcast.23, ...), custom_call_target="tpu_custom_call" | custom-call | tf_op jit(solution)/shard_map/moe_kernel/pallas_call | solution.py:1101
  140.7 116.4 %back_kernel.1 = (f32[256,768]{1,0:T(8,128)}, f32[256,768]{1,0:T(8,128)}, f32[256,768]{1,0:T(8,128)}, f32[64,1024]{1,0:T(8,128)}, f32[64,256]{1,0:T(8,128)}, /*i...) custom-call(bf16[3,32,2048]{2,1,0:T(8,128)(2,1)} %get-tuple-element., ...), custom_call_target="tpu_custom_call" | custom-call | tf_op jit(solution)/shard_map/back_kernel/pallas_call | solution.py:1101
  257.1 4.9 %finish.1 = (f32[96,2048]{1,0:T(8,128)}, f32[96,2048]{1,0:T(8,128)}, f32[256,768]{1,0:T(8,128)}, f32[256,768]{1,0:T(8,128)}, f32[256,768]{1,0:T(8,128)}, /*index...) custom-call(f32[96,2048]{1,0:T(8,128)} %get-tuple-element.60.refs_4_, ...), custom_call_target="tpu_custom_call" | custom-call | tf_op jit(solution)/shard_map/finish/pallas_call | solution.py:1425
